TPU v7x, 128 devices: a whole 4x4x4 slice. The times are simulated.
128 devices in a mesh: dp: 16 (over y, z_lo, core), seq: 8 (over x, z_hi).
Axes of the slice: x: 4, y: 4, z: 4 (z_hi: 2, z_lo: 2; z = z_hi * 2 + z_lo), core: 2. Of those that a mesh axis runs over, the one named last changes fastest.
Arguments:
- hidden_states: bfloat16 [16384, 5120], P(('dp', 'seq')), may hold values from -24 to 24
- value_weight: bfloat16 [5120, 1024], P('dp'), may hold values from -0.078125 to 0.078125
- query_states: bfloat16 [16384, 8192], P(('dp', 'seq')), may hold values from -140 to 140
- key_states: bfloat16 [16384, 1024], P(('dp', 'seq')), may hold values from -4.5 to 4.5
- cotangent: bfloat16 [16384, 8192], P(('dp', 'seq')), may hold values from -6 to 6
- lengths: int32 [16, 8], P('dp'), may hold values from 1 to 512, 1024 in all within a row
Outputs:
- attention_out: bfloat16 [16384, 8192], P(('dp', 'seq'))
- query_grad: bfloat16 [16384, 8192], P(('dp', 'seq'))
- key_grad: bfloat16 [16384, 1024], P(('dp', 'seq'))
- input_grad: bfloat16 [16384, 5120], P(('dp', 'seq'))
- value_weight_grad: float32 [5120, 1024], P('dp')
Inputs may be any that keep to these rules, and one draw needn't show every extreme that they name: Row g lists the 8 response lengths of group g's pack; they sum to 1024 and the longest is 512.
All inputs are finite; a program needn't handle non-finite values.
Results may differ from a plain program's by a relative error of at most 0.04.
Values may be sent and summed in bfloat16 or wider, within the bound.
No kernel may reach another device: no remote copies, remote signals or barrier semaphores. Data moves between devices by JAX's collectives and lax.ppermute only.
A program may use at most 256 MiB of HBM per device.

v0:
```python
import jax
import jax.numpy as jnp
from jax import lax
from jax.sharding import PartitionSpec as P

HEADS = 64
KV_HEADS = 8
HEAD_DIM = 128


def softmax_rows(query_rows, key_rows, allowed):
    scores = jnp.einsum(
        "qcgd,kcd->qcgk", query_rows, key_rows, preferred_element_type=jnp.float32
    ) * HEAD_DIM ** (-0.5)
    scores = jnp.where(allowed[:, None, None, :], scores, -jnp.inf)
    highest = jnp.max(scores, axis=-1, keepdims=True)
    expo = jnp.exp(scores - highest)
    return expo / jnp.sum(expo, axis=-1, keepdims=True)


def body(hidden_states, value_weight, query_states, key_states, cotangent, lengths):
    tok_rows = hidden_states.shape[0]
    score_scale = HEAD_DIM ** (-0.5)
    full_weight = lax.all_gather(value_weight, "dp", axis=0, tiled=True)
    values = jnp.dot(hidden_states, full_weight, preferred_element_type=jnp.float32).astype(
        jnp.bfloat16
    )
    head_q, head_k, head_v, head_cot = (
        lax.all_to_all(
            query_states.reshape(tok_rows, HEADS, HEAD_DIM),
            "seq",
            split_axis=1,
            concat_axis=0,
            tiled=True,
        ),
        lax.all_to_all(
            key_states.reshape(tok_rows, KV_HEADS, HEAD_DIM),
            "seq",
            split_axis=1,
            concat_axis=0,
            tiled=True,
        ),
        lax.all_to_all(
            values.reshape(tok_rows, KV_HEADS, HEAD_DIM),
            "seq",
            split_axis=1,
            concat_axis=0,
            tiled=True,
        ),
        lax.all_to_all(
            cotangent.reshape(tok_rows, HEADS, HEAD_DIM),
            "seq",
            split_axis=1,
            concat_axis=0,
            tiled=True,
        ),
    )
    packed = head_q.shape[0]
    local_heads = head_q.shape[1]
    local_kv = head_k.shape[1]
    group = local_heads // local_kv
    head_q = head_q.reshape(packed, local_kv, group, HEAD_DIM)
    head_cot = head_cot.reshape(packed, local_kv, group, HEAD_DIM)
    positions = jnp.arange(packed, dtype=jnp.int32)
    doc_ends = jnp.cumsum(lengths[0])
    doc_ids = jnp.sum((positions[:, None] >= doc_ends[None, :-1]).astype(jnp.int32), axis=1)
    row_block = min(512, packed)
    key_total = jnp.zeros((packed, local_kv, HEAD_DIM), jnp.float32)
    value_total = jnp.zeros((packed, local_kv, HEAD_DIM), jnp.float32)
    attended_parts = []
    query_parts = []
    for block_index in range(packed // row_block):
        begin_row = block_index * row_block
        end_row = begin_row + row_block
        query_rows = head_q[begin_row:end_row]
        cot_rows = head_cot[begin_row:end_row]
        allowed = (doc_ids[begin_row:end_row, None] == doc_ids[None, :packed]) & (
            positions[None, :packed] <= positions[begin_row:end_row, None]
        )
        probabilities = softmax_rows(query_rows, head_k, allowed)
        rounded = probabilities.astype(jnp.bfloat16)
        attended = jnp.einsum(
            "qcgk,kcd->qcgd", rounded, head_v, preferred_element_type=jnp.float32
        ).astype(jnp.bfloat16)
        through_values = jnp.einsum(
            "qcgd,kcd->qcgk", cot_rows, head_v, preferred_element_type=jnp.float32
        )
        row_delta = jnp.sum(
            cot_rows.astype(jnp.float32) * attended.astype(jnp.float32), axis=-1, keepdims=True
        )
        score_grad = (probabilities * (through_values - row_delta)).astype(jnp.bfloat16)
        query_grad = (
            jnp.einsum("qcgk,kcd->qcgd", score_grad, head_k, preferred_element_type=jnp.float32)
            * score_scale
        ).astype(jnp.bfloat16)
        key_part = jnp.einsum(
            "qcgk,qcgd->kcd", score_grad, query_rows, preferred_element_type=jnp.float32
        )
        value_part = jnp.einsum(
            "qcgk,qcgd->kcd", rounded, cot_rows, preferred_element_type=jnp.float32
        )
        key_total = key_total + key_part
        value_total = value_total + value_part
        attended_parts.append(attended)
        query_parts.append(query_grad)
    attended_all = jnp.concatenate(attended_parts, axis=0).reshape(packed, local_heads, HEAD_DIM)
    query_all = jnp.concatenate(query_parts, axis=0).reshape(packed, local_heads, HEAD_DIM)
    key_grads = (key_total * score_scale).astype(jnp.bfloat16)
    value_grads = value_total.astype(jnp.bfloat16)
    token_out, token_query, token_key, token_value = (
        lax.all_to_all(attended_all, "seq", split_axis=0, concat_axis=1, tiled=True),
        lax.all_to_all(query_all, "seq", split_axis=0, concat_axis=1, tiled=True),
        lax.all_to_all(key_grads, "seq", split_axis=0, concat_axis=1, tiled=True),
        lax.all_to_all(value_grads, "seq", split_axis=0, concat_axis=1, tiled=True),
    )
    attention_out = token_out.reshape(tok_rows, HEADS * HEAD_DIM)
    query_out = token_query.reshape(tok_rows, HEADS * HEAD_DIM)
    key_out = token_key.reshape(tok_rows, KV_HEADS * HEAD_DIM)
    value_rows_grad = token_value.reshape(tok_rows, KV_HEADS * HEAD_DIM)
    input_grad = lax.dot_general(
        value_rows_grad, full_weight, (((1,), (1,)), ((), ())), preferred_element_type=jnp.float32
    ).astype(jnp.bfloat16)
    shard_rows = lax.psum_scatter(
        lax.dot_general(
            hidden_states,
            value_rows_grad,
            (((0,), (0,)), ((), ())),
            preferred_element_type=jnp.float32,
        ),
        "dp",
        scatter_dimension=0,
        tiled=True,
    )
    weight_grad = lax.psum(shard_rows, "seq")
    return (attention_out, query_out, key_out, input_grad, weight_grad)


def solution(mesh):
    placed = (
        P(("dp", "seq"), None),
        P("dp", None),
        P(("dp", "seq"), None),
        P(("dp", "seq"), None),
        P(("dp", "seq"), None),
        P("dp", None),
    )
    return jax.shard_map(
        body,
        mesh=mesh,
        in_specs=placed,
        out_specs=(
            P(("dp", "seq"), None),
            P(("dp", "seq"), None),
            P(("dp", "seq"), None),
            P(("dp", "seq"), None),
            P("dp", None),
        ),
        check_vma=False,
    )
```

profile of v0, /device:TPU:0, one launch (start us, length us, event | category | flops | bytes accessed | tf_op | source)
XLA Modules:
  0.0 571.3 jit_solution(3897778916011336083)
XLA Ops:
  7.9 3.2 copy.132
  11.1 2.9 copy.133
  14.1 7.8 %all-to-all-start.2 = ((bf16[128,64,128]{2,0,1:T(8,128)(2,1)}), bf16[128,64,128]{2,0,1:T(8,128)(2,1)S(1)}, u32[]{:S(2)}, u32[]{:S(2)}) async-start(bf16[128,64,128]{2,0,1:T(8,128)(2,1)} %copy.133), calls=%async_computation.2 | async-start | bytes 4194304 | tf_op jit(solution)/shard_map/all_to_all | solution.py:29
  21.9 4.1 copy.141
  26.0 4.1 copy.142
  30.1 24.6 %all-to-all-done.2 = bf16[128,64,128]{2,0,1:T(8,128)(2,1)S(1)} async-done(((bf16[128,64,128]{2,0,1:T(8,128)(2,1)}), bf16[128,64,128]{2,0,1:T(8,128)(2,1)S(1)}, u32[]{:S(2)}, u32[]{:S(2)}) %all-to-all-start.2) | async-done | bytes 2097184 | tf_op jit(solution)/shard_map/all_to_all | solution.py:29
  54.7 4.3 all-to-all-start.4
  61.9 2.9 copy.184
  68.0 23.5 %all-to-all-done.4 = bf16[128,64,128]{2,0,1:T(8,128)(2,1)} async-done(((bf16[128,64,128]{2,0,1:T(8,128)(2,1)}), bf16[128,64,128]{2,0,1:T(8,128)(2,1)}, u32[]{:S(2)}, u32[]{:S(2)}) %all-to-all-start.4) | async-done | bytes 2097184 | tf_op jit(solution)/shard_map/all_to_all | solution.py:50
  91.5 3.4 all-to-all-start.1
  95.0 3.0 copy.183
  98.1 2.8 slice_convert_fusion.1
  103.6 4.7 fusion.7
  108.4 7.8 %fusion.6 = (f32[512,8]{0,1:T(8,128)S(1)}, f32[1024,512,8]{1,0,2:T(8,128)}) fusion(pred[512,1024]{0,1:T(8,128)(4,1)S(1)} %get-tuple-element.41, bf16[1024,128,1]{1,0,2:T(8,128)(2,1)S(1)} %bitcast.297, bf16[512,8,128]{2,0,1:T(8,128)(2,1)S(1)} %bitcast.292), kind=kOutput, calls=%fused_computation.14 | convolution fusion | flops 1086320640 | bytes 18628608 | tf_op jit(solution)/shard_map/qcgd,kcd->qcgk/dot_general | solution.py:12
  116.1 13.1 %fusion.3 = (f32[512,8]{0,1:T(8,128)S(1)}, f32[512,8]{0,1:T(8,128)S(1)}) fusion(f32[1024,512,8]{1,0,2:T(8,128)} %get-tuple-element.48, f32[512,8]{0,1:T(8,128)S(1)} %get-tuple-element.47, pred[512,1024]{0,1:T(8,128)(4,1)S(1)} %get-tuple-element.41, f32[512,8]{0,1:T(8,128)S(1)} %get-tuple-element.45, f32[1024,512,8]{1,0,2:T(8,128)S(1)} %get-tuple-element.46, ...), kind=kLoop, calls=%fused_computation.11 | loop fusion | flops 33546240 | bytes 34668544 | tf_op jit(solution)/shard_map/reduce_sum | solution.py:18
  129.3 8.0 %fusion.50 = f32[1024,128]{1,0:T(8,128)S(1)} fusion(bf16[512,8,128]{2,0,1:T(8,128)(2,1)S(1)} %bitcast.307, f32[512,8]{0,1:T(8,128)S(1)} %get-tuple-element.53, f32[512,8]{0,1:T(8,128)S(1)} %get-tuple-element.47, f32[1024,512,8]{1,0,2:T(8,128)} %get-tuple-element.48, pred[512,1024]{0,1:T(8,128)(4,1)S(1)} %get-tuple-element.41), kind=kOutput, calls=%fused_computation.56 | convolution fusion | flops 1094713344 | bytes 18907136 | tf_op jit(solution)/shard_map/qcgk,qcgd->kcd/dot_general | solution.py:99
  137.4 5.1 fusion.81
  143.8 15.3 %all_to_all.120 = bf16[8,2,8192]{2,1,0:T(2,128)(2,1)S(1)} all-to-all(bf16[8,2,8192]{2,1,0:T(2,128)(2,1)S(1)} %reshape.327), channel_id=1, replica_groups=mesh['dp'=16,'seq'=8] {'seq'}, dimensions={0} | all-to-all | bytes 524288 | tf_op jit(solution)/shard_map/all_to_all | solution.py:114
  159.6 8.5 %convolution_bitcast_fusion = f32[5120,1024]{0,1:T(8,128)} fusion(bf16[128,1024]{0,1:T(8,128)(2,1)S(1)} %bitcast.294, bf16[128,5120]{1,0:T(8,128)(2,1)S(1)} %copy-done), kind=kOutput, calls=%fused_computation.16 | convolution fusion | flops 1342177280 | bytes 22544384 | tf_op jit(solution)/shard_map/dot_general | solution.py:124
  168.2 21.3 %copy.167 = f32[5120,1024]{1,0:T(8,128)} copy(f32[5120,1024]{0,1:T(8,128)} %convolution_bitcast_fusion) | data formatting | bytes 41943040
  189.6 5.5 fusion.77
  195.8 3.8 all-to-all-start
  199.7 4.0 copy.146
  203.7 3.1 reshape.313
  206.8 4.0 copy.150
  210.8 3.1 reshape.314
  213.9 4.4 all-to-all-done
  218.3 10.9 %multiply_reduce_fusion.1 = (f32[512,8]{0,1:T(8,128)S(1)}, bf16[512,1,8,128]{0,3,2,1:T(8,128)(2,1)}) fusion(f32[512,1,8,128]{0,3,2,1:T(8,128)} %reshape.313, bf16[1024,128,1]{1,0,2:T(8,128)(2,1)S(1)} %bitcast.309, f32[512,8]{0,1:T(8,128)S(1)} %get-tuple-element.53, f32[512,8]{0,1:T(8,128)S(1)} %get-tuple-element.47, f32[1024,512,8]{1,0,2:T(8,128)} %get-tuple-element.48, ...), kind=kOutput, calls=%fused_computation.45 | convolution fusion | flops 1096806400 | bytes 20758528 | tf_op jit(solution)/shard_map/qcgk,kcd->qcgd/dot_general | solution.py:82
  229.1 11.9 %fusion.1 = bf16[512,1,8,1024]{0,3,2,1:T(8,128)(2,1)} fusion(bf16[1024,128,1]{1,0,2:T(8,128)(2,1)S(1)} %bitcast.310, bf16[512,8,128]{2,0,1:T(8,128)(2,1)} %bitcast.306, f32[512,8]{0,1:T(8,128)S(1)} %get-tuple-element.51, f32[512,8]{0,1:T(8,128)S(1)} %get-tuple-element.53, f32[512,8]{0,1:T(8,128)S(1)} %get-tuple-element.47, ...), kind=kOutput, calls=%fused_computation.6 | convolution fusion | flops 1103101952 | bytes 27049984 | tf_op jit(solution)/shard_map/qcgd,kcd->qcgk/dot_general | solution.py:85
  241.0 6.0 %fusion.56 = f32[1024,128]{1,0:T(8,128)S(1)} fusion(bf16[512,8,128]{2,0,1:T(8,128)(2,1)S(1)} %bitcast.293, bf16[512,1,8,1024]{0,3,2,1:T(8,128)(2,1)} %fusion.1), kind=kOutput, calls=%fused_computation.58 | convolution fusion | flops 1073741824 | bytes 9961472 | tf_op jit(solution)/shard_map/qcgk,qcgd->kcd/dot_general | solution.py:96
  247.0 5.8 %multiply_reduce_fusion = (f32[512,8]{0,1:T(8,128)S(1)}, bf16[512,1,8,128]{0,3,2,1:T(8,128)(2,1)}) fusion(f32[512,1,8,128]{0,3,2,1:T(8,128)S(1)} %copy-done.11, bf16[1024,128,1]{1,0,2:T(8,128)(2,1)S(1)} %bitcast.311, f32[512,8]{0,1:T(8,128)S(1)} %get-tuple-element.54, f32[512,8]{0,1:T(8,128)S(1)} %get-tuple-element.45, f32[1024,512,8]{1,0,2:T(8,128)S(1)} %bitcast.282, ...), kind=kOutput, calls=%fused_computation.43 | convolution fusion | flops 1096806400 | bytes 20758528 | tf_op jit(solution)/shard_map/qcgk,kcd->qcgd/dot_general | solution.py:82
  252.8 9.8 %fusion = bf16[512,1,8,1024]{0,3,2,1:T(8,128)(2,1)} fusion(bf16[1024,128,1]{1,0,2:T(8,128)(2,1)S(1)} %bitcast.312, bf16[512,8,128]{2,0,1:T(8,128)(2,1)} %bitcast.304, f32[512,8]{0,1:T(8,128)S(1)} %get-tuple-element.49, f32[512,8]{0,1:T(8,128)S(1)} %get-tuple-element.54, f32[512,8]{0,1:T(8,128)S(1)} %get-tuple-element.45, f32[1024,512,8]{1,0,2:T(8,128)S(1)} %bitcast.282, ...), kind=kOutput, calls=%fused_computation.3 | convolution fusion | flops 1103101952 | bytes 27049984 | tf_op jit(solution)/shard_map/qcgd,kcd->qcgk/dot_general | solution.py:85
  262.6 5.9 %fusion.78 = bf16[1024,1,128]{2,0,1:T(8,128)(2,1)S(1)} fusion(f32[1024,128]{1,0:T(8,128)S(1)} %fusion.56, bf16[512,8,128]{2,0,1:T(8,128)(2,1)S(1)} %bitcast.291, bf16[512,1,8,1024]{0,3,2,1:T(8,128)(2,1)} %fusion), kind=kOutput, calls=%fused_computation.67 | convolution fusion | flops 1074135040 | bytes 10223616 | tf_op jit(solution)/shard_map/qcgk,qcgd->kcd/dot_general | solution.py:96
  270.1 4.3 all-to-all-start.6
  274.4 6.0 %fusion.44 = bf16[512,1,8,128]{3,0,2,1:T(8,128)(2,1)S(1)} fusion(bf16[1024,128,1]{1,0,2:T(8,128)(2,1)S(1)} %bitcast.298, bf16[512,1,8,1024]{0,3,2,1:T(8,128)(2,1)} %fusion.1), kind=kOutput, calls=%fused_computation.54 | convolution fusion | flops 1074790400 | bytes 9699328 | tf_op jit(solution)/shard_map/qcgk,kcd->qcgd/dot_general | solution.py:93
  283.0 2.7 copy.152
  285.7 7.4 %all-to-all-start.5 = ((bf16[1024,8,128]{2,1,0:T(8,128)(2,1)}), bf16[1024,8,128]{2,1,0:T(8,128)(2,1)S(1)}, u32[]{:S(2)}, u32[]{:S(2)}) async-start(bf16[1024,8,128]{2,1,0:T(8,128)(2,1)} %copy.152), calls=%async_computation.5 | async-start | bytes 4194304 | tf_op jit(solution)/shard_map/all_to_all | solution.py:112
  293.2 3.2 maximum_bitcast_fusion
  296.4 4.1 copy.139
  300.5 23.9 %all-to-all-done.5 = bf16[1024,8,128]{2,1,0:T(8,128)(2,1)S(1)} async-done(((bf16[1024,8,128]{2,1,0:T(8,128)(2,1)}), bf16[1024,8,128]{2,1,0:T(8,128)(2,1)S(1)}, u32[]{:S(2)}, u32[]{:S(2)}) %all-to-all-start.5) | async-done | bytes 2097184 | tf_op jit(solution)/shard_map/all_to_all | solution.py:112
  324.5 6.6 %all-to-all-start.3 = ((bf16[1024,8,128]{2,1,0:T(8,128)(2,1)}), bf16[1024,8,128]{2,1,0:T(8,128)(2,1)}, u32[]{:S(2)}, u32[]{:S(2)}) async-start(bf16[1024,8,128]{2,1,0:T(8,128)(2,1)} %copy.139), calls=%async_computation.3 | async-start | bytes 4194304 | tf_op jit(solution)/shard_map/all_to_all | solution.py:111
  331.1 123.3 %reduce-scatter.4.cloned.1.call-done = f32[320,1024]{1,0:T(8,128)} async-done(((f32[5120,1024]{1,0:T(8,128)}), f32[320,1024]{1,0:T(8,128)}) %reduce-scatter.4.cloned.1.call-update) | async-done | bytes 1310736
  454.4 3.0 copy.168
  457.4 8.6 %convolution_convert_fusion = bf16[128,5120]{1,0:T(8,128)(2,1)} fusion(bf16[128,1024]{0,1:T(8,128)(2,1)S(1)} %bitcast.295, bf16[5120,1024]{1,0:T(8,128)(2,1)} %all-gather.2.cloned.1.call-done), kind=kOutput, calls=%fused_computation.35 | convolution fusion | flops 1342832640 | bytes 12058624 | tf_op jit(solution)/shard_map/dot_general | solution.py:120
  468.0 3.1 copy.181
  473.3 3.1 copy.182
  476.4 85.2 %all-reduce.2.cloned.1.call-done = f32[320,1024]{0,1:T(8,128)} async-done(((f32[320,1024]{0,1:T(8,128)}), f32[320,1024]{0,1:T(8,128)}) %all-reduce.2.cloned.1.call-update) | async-done | bytes 1310736 | tf_op jit(solution)/shard_map/psum | solution.py:134
  561.7 2.9 copy.159
  (83 shorter events, 20.6 us)
Async XLA Ops:
  7.2 152.5 %copy-start = (bf16[128,5120]{1,0:T(8,128)(2,1)S(1)}, bf16[128,5120]{1,0:T(8,128)(2,1)}, u32[]{:S(2)}) copy-start(bf16[128,5120]{1,0:T(8,128)(2,1)} %param.6) | copy-start | bytes 3932164
  7.2 182.4 %all-gather.2.cloned.1.call-start = ((), (), s32[]{:S(2)}) async-start(), calls=%async_computation.9 | async-start | bytes 11141120 | tf_op jit(solution)/shard_map/all_gather | solution.py:24
  14.1 45.0 %copy-start.14 = (s32[1,8]{1,0:T(1,128)S(1)}, s32[1,8]{1,0:T(1,128)}, u32[]{:S(2)}) copy-start(s32[1,8]{1,0:T(1,128)} %param.11) | copy-start | bytes 100
  14.1 40.6 %all-to-all-start.2 = ((bf16[128,64,128]{2,0,1:T(8,128)(2,1)}), bf16[128,64,128]{2,0,1:T(8,128)(2,1)S(1)}, u32[]{:S(2)}, u32[]{:S(2)}) async-start(bf16[128,64,128]{2,0,1:T(8,128)(2,1)} %copy.133), calls=%async_computation.2 | async-start | bytes 4194304 | tf_op jit(solution)/shard_map/all_to_all | solution.py:29
  54.7 6.4 %copy-start.3 = (bf16[128,64,128]{2,0,1:T(8,128)(2,1)}, bf16[128,64,128]{2,0,1:T(8,128)(2,1)S(1)}, u32[]{:S(2)}) copy-start(bf16[128,64,128]{2,0,1:T(8,128)(2,1)S(1)} %all-to-all-done.2) | copy-start | bytes 6291460
  54.7 36.9 %all-to-all-start.4 = ((bf16[128,64,128]{2,0,1:T(8,128)(2,1)}), bf16[128,64,128]{2,0,1:T(8,128)(2,1)}, u32[]{:S(2)}, u32[]{:S(2)}) async-start(bf16[128,64,128]{2,0,1:T(8,128)(2,1)} %copy.142), calls=%async_computation.4 | async-start | bytes 4194304 | tf_op jit(solution)/shard_map/all_to_all | solution.py:50
  91.5 12.1 %all-to-all-start.1 = ((bf16[128,8,128]{2,0,1:T(8,128)(2,1)}), bf16[128,8,128]{2,0,1:T(8,128)(2,1)S(1)}, u32[]{:S(2)}, u32[]{:S(2)}) async-start(bf16[128,8,128]{2,0,1:T(8,128)(2,1)} %copy_bitcast_fusion.4), calls=%async_computation.1 | async-start | bytes 524288 | tf_op jit(solution)/shard_map/all_to_all | solution.py:36
  95.0 359.4 %reduce-scatter.4.cloned.1.call-start = ((), (), s32[]{:S(2)}) async-start(), calls=%async_computation.11 | async-start | bytes 22282240
  103.6 4.7 copy-start.9
  103.6 4.7 copy-start.5
  108.3 29.0 %copy-start.2 = (f32[1024,512,8]{1,0,2:T(8,128)}, f32[1024,512,8]{1,0,2:T(8,128)S(1)}, u32[]{:S(2)}) copy-start(f32[1024,512,8]{1,0,2:T(8,128)S(1)} %get-tuple-element.46) | copy-start | bytes 50331652
  116.1 13.2 %copy-start.13 = (bf16[4,128,8,128]{3,1,0,2:T(8,128)(2,1)S(1)}, bf16[4,128,8,128]{3,1,0,2:T(8,128)(2,1)}, u32[]{:S(2)}) copy-start(bf16[4,128,8,128]{3,1,0,2:T(8,128)(2,1)} %copy.144) | copy-start | bytes 3145732
  129.3 8.1 %copy-start.12 = (bf16[4,128,8,128]{3,1,0,2:T(8,128)(2,1)S(1)}, bf16[4,128,8,128]{3,1,0,2:T(8,128)(2,1)}, u32[]{:S(2)}) copy-start(bf16[4,128,8,128]{3,1,0,2:T(8,128)(2,1)} %copy.148) | copy-start | bytes 3145732
  159.6 8.6 %copy-start.7 = (bf16[128,8,1,128]{0,3,1,2:T(8,128)(2,1)}, bf16[128,8,1,128]{0,3,1,2:T(8,128)(2,1)S(1)}, u32[]{:S(2)}) copy-start(bf16[128,8,1,128]{0,3,1,2:T(8,128)(2,1)S(1)} %copy.157) | copy-start | bytes 786436
  195.8 22.4 %all-to-all-start = ((bf16[128,8,128]{2,0,1:T(8,128)(2,1)}), bf16[128,8,128]{2,0,1:T(8,128)(2,1)S(1)}, u32[]{:S(2)}, u32[]{:S(2)}) async-start(bf16[128,8,128]{2,0,1:T(8,128)(2,1)} %bitcast.280), calls=%async_computation | async-start | bytes 524288 | tf_op jit(solution)/shard_map/all_to_all | solution.py:43
  218.2 28.7 %slice-start = ((s8[16777216]{0:T(1024)(128)(4,1)}), s8[4194304]{0:T(1024)(128)(4,1)S(1)}, s32[]{:S(2)}) async-start(s8[16777216]{0:T(1024)(128)(4,1)} %bitcast.281), calls=%async_computation.12 | async-start | bytes 8388608
  218.3 28.7 %slice-start.1 = ((s8[16777216]{0:T(1024)(128)(4,1)}), s8[4194304]{0:T(1024)(128)(4,1)S(1)}, s32[]{:S(2)}) async-start(s8[16777216]{0:T(1024)(128)(4,1)} %bitcast.281), calls=%async_computation.13 | async-start | bytes 8388608
  229.1 11.9 %copy-start.6 = (bf16[4,128,8,128]{3,1,0,2:T(8,128)(2,1)S(1)}, bf16[4,128,8,128]{3,1,0,2:T(8,128)(2,1)}, u32[]{:S(2)}) copy-start(bf16[4,128,8,128]{3,1,0,2:T(8,128)(2,1)} %copy.135) | copy-start | bytes 3145732
  229.1 17.9 %slice-start.2 = ((s8[16777216]{0:T(1024)(128)(4,1)}), s8[4194304]{0:T(1024)(128)(4,1)S(1)}, s32[]{:S(2)}) async-start(s8[16777216]{0:T(1024)(128)(4,1)} %bitcast.281), calls=%async_computation.14 | async-start | bytes 8388608
  229.1 17.9 %slice-start.3 = ((s8[16777216]{0:T(1024)(128)(4,1)}), s8[4194304]{0:T(1024)(128)(4,1)S(1)}, s32[]{:S(2)}) async-start(s8[16777216]{0:T(1024)(128)(4,1)} %bitcast.281), calls=%async_computation.15 | async-start | bytes 8388608
  241.0 6.0 %copy-start.11 = (f32[512,1,8,128]{0,3,2,1:T(8,128)S(1)}, f32[512,1,8,128]{0,3,2,1:T(8,128)}, u32[]{:S(2)}) copy-start(f32[512,1,8,128]{0,3,2,1:T(8,128)} %reshape.314) | copy-start | bytes 6291460
  252.8 9.8 %copy-start.4 = (bf16[4,128,8,128]{3,1,0,2:T(8,128)(2,1)S(1)}, bf16[4,128,8,128]{3,1,0,2:T(8,128)(2,1)}, u32[]{:S(2)}) copy-start(bf16[4,128,8,128]{3,1,0,2:T(8,128)(2,1)} %copy.137) | copy-start | bytes 3145732
  262.6 11.7 %copy-start.10 = (bf16[128,8,128]{2,0,1:T(8,128)(2,1)S(1)}, bf16[128,8,128]{2,0,1:T(8,128)(2,1)}, u32[]{:S(2)}) copy-start(bf16[128,8,128]{2,0,1:T(8,128)(2,1)} %copy-done.9) | copy-start | bytes 786436
  270.1 15.7 %all-to-all-start.6 = ((bf16[8,2,8192]{2,1,0:T(2,128)(2,1)}), bf16[8,2,8192]{2,1,0:T(2,128)(2,1)S(1)}, u32[]{:S(2)}, u32[]{:S(2)}) async-start(bf16[8,2,8192]{2,1,0:T(2,128)(2,1)} %reshape.325), calls=%async_computation.6 | async-start | bytes 524288 | tf_op jit(solution)/shard_map/all_to_all | solution.py:113
  274.4 6.1 %copy-start.15 = (bf16[512,1,8,1024]{0,3,2,1:T(8,128)(2,1)S(1)}, bf16[512,1,8,1024]{0,3,2,1:T(8,128)(2,1)}, u32[]{:S(2)}) copy-start(bf16[512,1,8,1024]{0,3,2,1:T(8,128)(2,1)} %fusion) | copy-start | bytes 25165828
  285.7 38.8 %all-to-all-start.5 = ((bf16[1024,8,128]{2,1,0:T(8,128)(2,1)}), bf16[1024,8,128]{2,1,0:T(8,128)(2,1)S(1)}, u32[]{:S(2)}, u32[]{:S(2)}) async-start(bf16[1024,8,128]{2,1,0:T(8,128)(2,1)} %copy.152), calls=%async_computation.5 | async-start | bytes 4194304 | tf_op jit(solution)/shard_map/all_to_all | solution.py:112
  293.2 164.2 %copy-start.8 = (bf16[128,8,1,128]{0,3,1,2:T(8,128)(2,1)S(1)}, bf16[128,8,1,128]{0,3,1,2:T(8,128)(2,1)}, u32[]{:S(2)}) copy-start(bf16[128,8,1,128]{0,3,1,2:T(8,128)(2,1)} %copy-done.7) | copy-start | bytes 786436
  324.5 146.6 %all-to-all-start.3 = ((bf16[1024,8,128]{2,1,0:T(8,128)(2,1)}), bf16[1024,8,128]{2,1,0:T(8,128)(2,1)}, u32[]{:S(2)}, u32[]{:S(2)}) async-start(bf16[1024,8,128]{2,1,0:T(8,128)(2,1)} %copy.139), calls=%async_computation.3 | async-start | bytes 4194304 | tf_op jit(solution)/shard_map/all_to_all | solution.py:111
  331.1 230.6 %all-reduce.2.cloned.1.call-start = ((), (), s32[]{:S(2)}) async-start(), calls=%async_computation.10 | async-start | bytes 3145728 | tf_op jit(solution)/shard_map/psum | solution.py:134
  467.4 97.2 %copy-start.1 = (bf16[128,5120]{1,0:T(8,128)(2,1)S(1)}, bf16[128,5120]{1,0:T(8,128)(2,1)}, u32[]{:S(2)}) copy-start(bf16[128,5120]{1,0:T(8,128)(2,1)} %param.6) | copy-start | bytes 3932164
Sparse Core Ops, SparseCore 0:
  9.7 112.2 all-gather.1
  189.7 264.7 reduce-scatter.3
  457.5 104.0 all-reduce.1
where the time goes:
time: 579 us; the launch traced here: 571 us
  waiting for transfers between devices  286 us (49%)
  matrix products  107 us (18%)
  local copies, waits for them, and re-layouts  89.2 us (15%)
  starting transfers between devices  37.8 us (7%)
  other arithmetic  22 us (4%)
  blocking collectives  15.3 us (3%)
  between operations  14.4 us (2%)
    unnamed x4, waiting for transfers between devices  124 us
    psum x1, waiting for transfers between devices, body(): weight_grad = lax.psum(shard_rows, 'seq')  85.2 us
    unnamed x54, local copies, waits for them, and re-layouts  43.1 us
    all_to_all x1, waiting for transfers between devices, body(): lax.all_to_all(query_states.reshape(tok_rows, HEADS, HEAD_DIM), 'seq', sp...  24.6 us
    all_to_all x1, waiting for transfers between devices, body(): lax.all_to_all(query_all, 'seq', split_axis=0, concat_axis=1, tiled=True)  23.9 us
    all_to_all x1, waiting for transfers between devices, body(): lax.all_to_all(cotangent.reshape(tok_rows, HEADS, HEAD_DIM), 'seq', split...  23.5 us
    dot_general x2, matrix products, body(): jnp.einsum('qcgd,kcd->qcgk', cot_rows, head_v, preferred_element_type=jnp...  21.7 us
    dot_general x2, matrix products, body(): jnp.einsum('qcgk,kcd->qcgd', rounded, head_v, preferred_element_type=jnp....  16.6 us
  transfers between devices with their start and end apart: 10, of which 6 were waited for; matrix products, arithmetic and copies ran while one was open for 38% of the time, Pallas kernels for 0%

commit v1 on v0

v1 whole, which is shorter than its diff:
```python
import functools
import math

import jax
import jax.numpy as jnp
from jax import lax
from jax.experimental import pallas as pl
from jax.experimental.pallas import tpu as pltpu
from jax.sharding import PartitionSpec as P

HD = 128
KV = 8
G = 8
CH = 5
SC = HD**-0.5
L2 = SC * math.log2(math.e)
bf = jnp.bfloat16
f32 = jnp.float32
VL = 56 * 1024 * 1024

def probs_kernel(meta, q, do, k0,k1,k2,k3,k4, e_out, qt_out, dot_out, li_out, v0,v1,v2,v3,v4, bias):
    rows=q.shape[0]
    @pl.when(pl.program_id(0)==0)
    def _():
        s=meta[KV]
        r=lax.broadcasted_iota(jnp.int32,(1,rows),1)
        pos=r+s*rows
        start=jnp.zeros((1,rows),jnp.int32)
        total=meta[0]
        for d in range(1,8):
            start=jnp.where(pos>=total,total,start)
            total=total+meta[d]
        low=start-(s-(CH-1))*rows
        j=lax.broadcasted_iota(jnp.int32,(CH*rows,rows),0)
        ok=(j>=low)&(j<=r+(CH-1)*rows)
        bias[...]=jnp.where(ok,0.0,-1e30)
    for h in range(G):
        qt_out[0,:,h*rows:(h+1)*rows]=q[:,h*HD:(h+1)*HD].T
    ks=(k0,k1,k2,k3,k4)
    W=2
    n=W*rows
    for p in range(G//W):
        cols=slice(p*n,(p+1)*n)
        qt=qt_out[0,:,cols]
        ts=[]
        for c in range(CH):
            b=bias[c*rows:(c+1)*rows,:]
            b=jnp.concatenate([b]*W,axis=1)
            ts.append(jnp.dot(ks[c][...],qt,preferred_element_type=f32)*L2+b)
        m=functools.reduce(jnp.maximum,[jnp.max(t,axis=0,keepdims=True) for t in ts])
        l=jnp.zeros((1,n),f32)
        for c in range(CH):
            e=jnp.exp2(ts[c]-m)
            l=l+jnp.sum(e,axis=0,keepdims=True)
            e_out[0,c*rows:(c+1)*rows,cols]=e.astype(bf)
        li=1.0/l
        li_out[0,:,cols]=jnp.broadcast_to(li,(8,n))
        dt=jnp.concatenate([do[:,h*HD:(h+1)*HD].T for h in range(p*W,(p+1)*W)],axis=1)
        dot_out[0,:,cols]=(dt.astype(f32)*li).astype(bf)
    dall=dot_out[0]
    for c,v in enumerate((v0,v1,v2,v3,v4)):
        v[...]=lax.dot_general(e_out[0,c*rows:(c+1)*rows,:],dall,(((1,),(1,)),((),())),preferred_element_type=f32).astype(v.dtype)

def probs_call(meta,q,do,ks):
    rows=q.shape[0]
    wide=G*rows
    bs=lambda: pl.BlockSpec((rows,HD),lambda j:(0,j))
    bw=lambda: pl.BlockSpec((rows,G*HD),lambda j:(0,j))
    b3=lambda a,b: pl.BlockSpec((1,a,b),lambda j:(j,0,0))
    S=jax.ShapeDtypeStruct
    return pl.pallas_call(probs_kernel,grid=(KV,),
        in_specs=[pl.BlockSpec(memory_space=pltpu.SMEM),bw(),bw()]+[bs() for _ in range(CH)],
        out_specs=[b3(CH*rows,wide),b3(HD,wide),b3(HD,wide),b3(8,wide)]+[bs() for _ in range(CH)],
        out_shape=[S((KV,CH*rows,wide),bf),S((KV,HD,wide),bf),S((KV,HD,wide),bf),S((KV,8,wide),f32)]+[S((rows,KV*HD),bf)]*(CH-1)+[S((rows,KV*HD),f32)],
        scratch_shapes=[pltpu.VMEM((CH*rows,rows),f32)],
        compiler_params=pltpu.CompilerParams(vmem_limit_bytes=VL),
        cost_estimate=pl.CostEstimate(flops=2*2*KV*CH*rows*wide*HD,bytes_accessed=KV*CH*rows*wide*2+8*rows*8192,transcendentals=KV*CH*rows*wide),
        )(meta,q,do,*ks)

def grads_kernel(e,qt,dott,li,k0,k1,k2,k3,k4,v0,v1,v2,v3,v4,out,dq,g0,g1,g2,g3,g4,ds):
    rows=out.shape[0]
    ks=(k0,k1,k2,k3,k4); vs=(v0,v1,v2,v3,v4)
    W=2; n=W*rows
    kt=jnp.concatenate([k[...].T for k in ks],axis=1)
    vt=jnp.concatenate([v[...].T for v in vs],axis=1)
    for p in range(G//W):
        cols=slice(p*n,(p+1)*n)
        o=jnp.dot(vt,e[0,:,cols],preferred_element_type=f32)*li[0,0:1,cols]
        ob=o.astype(bf)
        dt=dott[0,:,cols]
        delta=jnp.sum(dt.astype(f32)*o,axis=0,keepdims=True)
        for c in range(CH):
            dp=jnp.dot(vs[c][...],dt,preferred_element_type=f32)
            ds[c*rows:(c+1)*rows,cols]=(e[0,c*rows:(c+1)*rows,cols].astype(f32)*(dp-delta)).astype(bf)
        dqt=(jnp.dot(kt,ds[:,cols],preferred_element_type=f32)*SC).astype(bf)
        for w in range(W):
            h=p*W+w
            out[:,h*HD:(h+1)*HD]=ob[:,w*rows:(w+1)*rows].T
            dq[:,h*HD:(h+1)*HD]=dqt[:,w*rows:(w+1)*rows].T
    qall=qt[0]
    for c,g in enumerate((g0,g1,g2,g3,g4)):
        g[...]=(lax.dot_general(ds[c*rows:(c+1)*rows,:],qall,(((1,),(1,)),((),())),preferred_element_type=f32)*SC).astype(g.dtype)

def grads_call(e,qt,dott,li,ks,vs):
    rows=ks[0].shape[0]; wide=G*rows
    bs=lambda: pl.BlockSpec((rows,HD),lambda j:(0,j))
    bw=lambda: pl.BlockSpec((rows,G*HD),lambda j:(0,j))
    b3=lambda a,b: pl.BlockSpec((1,a,b),lambda j:(j,0,0))
    S=jax.ShapeDtypeStruct
    return pl.pallas_call(grads_kernel,grid=(KV,),
        in_specs=[b3(CH*rows,wide),b3(HD,wide),b3(HD,wide),b3(8,wide)]+[bs() for _ in range(2*CH)],
        out_specs=[bw(),bw()]+[bs() for _ in range(CH)],
        out_shape=[S((rows,KV*G*HD),bf)]*2+[S((rows,KV*HD),bf)]*(CH-1)+[S((rows,KV*HD),f32)],
        scratch_shapes=[pltpu.VMEM((CH*rows,wide),bf)],
        compiler_params=pltpu.CompilerParams(vmem_limit_bytes=VL),
        cost_estimate=pl.CostEstimate(flops=2*4*KV*CH*rows*wide*HD,bytes_accessed=KV*CH*rows*wide*2+8*rows*8192,transcendentals=0),
        )(e,qt,dott,li,*ks,*vs)


def forward(x, k):
    return lax.ppermute(x, "seq", [(i, i + k) for i in range(8 - k)])


def backward(x, k):
    return lax.ppermute(x, "seq", [(i + k, i) for i in range(8 - k)])


def along_y(x, k):
    return lax.ppermute(x, "dp", [(i, (i + 4 * k) % 16) for i in range(16)])


def flip_dp(x, m):
    return lax.ppermute(x, "dp", [(i, i ^ m) for i in range(16)])


def flip_seq(x, m):
    return lax.ppermute(x, "seq", [(i, i ^ m) for i in range(8)])


def flip_both(x, a, b):
    return lax.ppermute(x, ("dp", "seq"), [(i * 8 + j, (i ^ a) * 8 + (j ^ b)) for i in range(16) for j in range(8)])


def pick(x, i):
    return lax.dynamic_index_in_dim(x, i, 0, keepdims=False)


def place(parts, ids):
    out = jnp.zeros((len(parts),) + parts[0].shape, parts[0].dtype)
    for part, i in zip(parts, ids):
        out = lax.dynamic_update_index_in_dim(out, part, i, 0)
    return out


def body(hidden, weight, query, key, cot, lengths):
    rows = hidden.shape[0]
    dp = lax.axis_index("dp")
    seq = lax.axis_index("seq")
    y, u = dp // 4, dp % 4
    zl, core = u // 2, u % 2
    x, zh = seq // 2, seq % 2
    depth = hidden.shape[1] // 4
    meta = jnp.concatenate([lengths[0], seq.astype(jnp.int32)[None]])
    with jax.named_scope("keys_forward"):
        ks = [forward(key, CH - 1 - c) for c in range(CH - 1)] + [key]
    with jax.named_scope("hidden_columns"):
        blocks = [lax.dynamic_slice_in_dim(hidden, ((y + k) % 4) * depth, depth, axis=1) for k in range(4)]
        hid = jnp.concatenate([blocks[0]] + [along_y(blocks[k], k) for k in (1, 2, 3)], axis=0)
    with jax.named_scope("weight_rows"):
        w1 = flip_dp(weight, 1)
        w2 = flip_dp(weight, 2)
        w3 = flip_dp(w2, 1)
        wu = place([weight, w1, w2, w3], [u, u ^ 1, u ^ 2, u ^ 3]).reshape(depth, -1)
    with jax.named_scope("values"):
        part = jnp.dot(hid, wu, preferred_element_type=f32)
        back = [along_y(part[k * rows : (k + 1) * rows].astype(bf), 4 - k) for k in (1, 2, 3)]
        values = (part[:rows] + sum(b.astype(f32) for b in back)).astype(bf)
        vs = [forward(values, CH - 1 - c) for c in range(CH - 1)] + [values]
    with jax.named_scope("probs"):
        e, qt, dott, li, *dv = probs_call(meta, query, cot, ks)
    with jax.named_scope("value_grad"):
        vgrad = (dv[-1] + sum(backward(dv[c], CH - 1 - c).astype(f32) for c in range(CH - 1))).astype(bf)
        vy = jnp.concatenate([vgrad] + [along_y(vgrad, k) for k in (1, 2, 3)], axis=0)
    with jax.named_scope("weight_grad"):
        g = lax.dot_general(hid, vy, (((0,), (0,)), ((), ())), preferred_element_type=f32)
        g = g.reshape(2, 2, weight.shape[0], -1)
        mine = lax.dynamic_index_in_dim(g, core, 1, keepdims=False)
        other = lax.dynamic_index_in_dim(g, 1 - core, 1, keepdims=False)
        g = mine + flip_dp(other.astype(bf), 1).astype(f32)
        g = g.reshape(2, 2, weight.shape[0] // 2, -1)

        def piece(a, b):
            return pick(pick(g, zl ^ a), zh ^ b)

        g = (
            piece(0, 0)
            + flip_both(piece(1, 0).astype(bf), 2, 0).astype(f32)
            + flip_both(piece(0, 1).astype(bf), 0, 1).astype(f32)
            + flip_both(piece(1, 1).astype(bf), 2, 1).astype(f32)
        )
        g = g.reshape(4, weight.shape[0] // 8, -1)
        g = pick(g, x) + sum(flip_seq(pick(g, x ^ k).astype(bf), 2 * k).astype(f32) for k in (1, 2, 3))
        g = g.astype(bf)
        g = place([g] + [flip_seq(g, 2 * k) for k in (1, 2, 3)], [x, x ^ 1, x ^ 2, x ^ 3])
        wgrad = place([g, flip_seq(g, 1)], [zh, 1 - zh]).reshape(weight.shape).astype(f32)
    with jax.named_scope("input_grad"):
        ig = lax.dot_general(vy, wu, (((1,), (1,)), ((), ())), preferred_element_type=f32).astype(bf)
        igs = [ig[:rows]] + [along_y(ig[k * rows : (k + 1) * rows], 4 - k) for k in (1, 2, 3)]
        input_grad = jnp.zeros(hidden.shape, bf)
        for k in range(4):
            input_grad = lax.dynamic_update_slice_in_dim(input_grad, igs[k], ((y + k) % 4) * depth, axis=1)
    with jax.named_scope("grads"):
        out, dq, *dk = grads_call(e, qt, dott, li, ks, vs)
    with jax.named_scope("key_grad"):
        kgrad = (dk[-1] + sum(backward(dk[c], CH - 1 - c).astype(f32) for c in range(CH - 1))).astype(bf)
    return out, dq, kgrad, input_grad, wgrad


def solution(mesh):
    tok = P(("dp", "seq"), None)
    own = P("dp", None)
    return jax.shard_map(
        body,
        mesh=mesh,
        in_specs=(tok, own, tok, tok, tok, own),
        out_specs=(tok, tok, tok, tok, own),
        check_vma=False,
    )
```

time: 579 us -> 240 us (0.41)
  the two profiles are of different devices: /device:TPU:0 before, /device:TPU:26 now
where the time goes in v1:
time: 240 us; the launch traced here: 239 us
  waiting for transfers between devices  117 us (49%)
  starting transfers between devices  67.3 us (28%)
  Pallas kernels  32.6 us (14%)
  other arithmetic  6.93 us (3%)
  local copies, waits for them, and re-layouts  6.88 us (3%)
  matrix products  6.8 us (3%)
    ppermute x12, waiting for transfers between devices, along_y(): return lax.ppermute(x, 'dp', [(i, (i + 4 * k) % 16) for i in range(16)])  38.3 us
    ppermute x7, waiting for transfers between devices, flip_seq(): return lax.ppermute(x, 'seq', [(i, i ^ m) for i in range(8)])  35.4 us
    ppermute x8, starting transfers between devices, forward(): return lax.ppermute(x, 'seq', [(i, i + k) for i in range(8 - k)])  25.6 us
    ppermute x8, waiting for transfers between devices, forward(): return lax.ppermute(x, 'seq', [(i, i + k) for i in range(8 - k)])  18.5 us
    pallas_call x1, Pallas kernels, grads_call(): pl.pallas_call(grads_kernel, grid=(KV,), in_specs=[b3(CH * rows, wide), b...  16.8 us
    pallas_call x1, Pallas kernels, probs_call(): pl.pallas_call(probs_kernel, grid=(KV,), in_specs=[pl.BlockSpec(memory_sp...  15.8 us
    ppermute x8, waiting for transfers between devices, backward(): return lax.ppermute(x, 'seq', [(i + k, i) for i in range(8 - k)])  14.1 us
    ppermute x8, starting transfers between devices, backward(): return lax.ppermute(x, 'seq', [(i + k, i) for i in range(8 - k)])  14 us
  transfers between devices with their start and end apart: 42, of which 20 were waited for; matrix products, arithmetic and copies ran while one was open for 7% of the time, Pallas kernels for 14%

profile of v1, /device:TPU:26, one launch (start us, length us, event | category | flops | bytes accessed | tf_op | source)
XLA Modules:
  0.0 239.1 jit_solution(8717075944988537839)
XLA Ops:
  0.6 4.0 %collective-permute-start = (bf16[128,1024]{1,0:T(8,128)(2,1)}, bf16[128,1024]{1,0:T(8,128)(2,1)S(1)}, u32[]{:S(2)}, u32[]{:S(2)}) collective-permute-start(bf16[128,1024]{1,0:T(8,128)(2,1)} %k4.3), channel_id=1, source_target_pairs={{0,4},{1,5},{2,6},{3,7},{8,12},{9,13},{10,14},{11,15},{16,20},{17,... | collective-permute-start | bytes 786440 | tf_op jit(solution)/shard_map/keys_forward/ppermute | solution.py:121
  4.7 4.0 %collective-permute-start.1 = (bf16[128,1024]{1,0:T(8,128)(2,1)}, bf16[128,1024]{1,0:T(8,128)(2,1)S(1)}, u32[]{:S(2)}, u32[]{:S(2)}) collective-permute-start(bf16[128,1024]{1,0:T(8,128)(2,1)} %k4.3), channel_id=1, source_target_pairs={{0,3},{1,4},{2,5},{3,6},{4,7},{8,11},{9,12},{10,13},{11,14},{12,15... | collective-permute-start | bytes 786440 | tf_op jit(solution)/shard_map/keys_forward/ppermute | solution.py:121
  8.7 3.1 %collective-permute-start.2 = (bf16[128,1024]{1,0:T(8,128)(2,1)}, bf16[128,1024]{1,0:T(8,128)(2,1)S(1)}, u32[]{:S(2)}, u32[]{:S(2)}) collective-permute-start(bf16[128,1024]{1,0:T(8,128)(2,1)} %k4.3), channel_id=1, source_target_pairs={{0,2},{1,3},{2,4},{3,5},{4,6},{5,7},{8,10},{9,11},{10,12},{11,13},... | collective-permute-start | bytes 786440 | tf_op jit(solution)/shard_map/keys_forward/ppermute | solution.py:121
  11.8 2.6 %collective-permute-start.3 = (bf16[128,1024]{1,0:T(8,128)(2,1)}, bf16[128,1024]{1,0:T(8,128)(2,1)S(1)}, u32[]{:S(2)}, u32[]{:S(2)}) collective-permute-start(bf16[128,1024]{1,0:T(8,128)(2,1)} %k4.3), channel_id=1, source_target_pairs={{0,1},{1,2},{2,3},{3,4},{4,5},{5,6},{6,7},{8,9},{9,10},{10,11},{11... | collective-permute-start | bytes 786440 | tf_op jit(solution)/shard_map/keys_forward/ppermute | solution.py:121
  17.2 6.4 %collective-permute-done.2.k2 = bf16[128,1024]{1,0:T(8,128)(2,1)S(1)} collective-permute-done((bf16[128,1024]{1,0:T(8,128)(2,1)}, bf16[128,1024]{1,0:T(8,128)(2,1)S(1)}, u32[]{:S(2)}, u32[]{:S(2)}) %collective-permute-start.2) | collective-permute-done | bytes 262176 | tf_op jit(solution)/shard_map/keys_forward/ppermute | solution.py:121
  23.6 9.1 %collective-permute-done.3.k3 = bf16[128,1024]{1,0:T(8,128)(2,1)S(1)} collective-permute-done((bf16[128,1024]{1,0:T(8,128)(2,1)}, bf16[128,1024]{1,0:T(8,128)(2,1)S(1)}, u32[]{:S(2)}, u32[]{:S(2)}) %collective-permute-start.3) | collective-permute-done | bytes 262176 | tf_op jit(solution)/shard_map/keys_forward/ppermute | solution.py:121
  33.4 15.8 %probs.1 = (bf16[8,640,1024]{2,1,0:T(8,128)(2,1)}, bf16[8,128,1024]{2,1,0:T(8,128)(2,1)}, bf16[8,128,1024]{2,1,0:T(8,128)(2,1)}, f32[8,8,1024]{2,1,0:T(8,128)}, ...) custom-call(s32[9]{0:T(128)} %pad_add_fusion.meta, ...), custom_call_target="tpu_custom_call" | custom-call | flops 2684354560 | bytes 18874368 | tf_op jit(solution)/shard_map/probs/pallas_call | solution.py:71
  49.2 1.3 collective-permute-start.21
  51.8 2.1 collective-permute-start.23
  54.9 7.2 %collective-permute-done.21 = bf16[128,1024]{1,0:T(8,128)(2,1)S(1)} collective-permute-done((bf16[128,1024]{1,0:T(8,128)(2,1)}, bf16[128,1024]{1,0:T(8,128)(2,1)S(1)}, u32[]{:S(2)}, u32[]{:S(2)}) %collective-permute-start.21) | collective-permute-done | bytes 262176 | tf_op jit(solution)/shard_map/value_grad/ppermute | solution.py:125
  62.1 1.9 collective-permute-start.24
  64.0 1.6 collective-permute-done.22
  65.9 5.3 %collective-permute-done.23 = bf16[128,1024]{1,0:T(8,128)(2,1)S(1)} collective-permute-done((bf16[128,1024]{1,0:T(8,128)(2,1)}, bf16[128,1024]{1,0:T(8,128)(2,1)S(1)}, u32[]{:S(2)}, u32[]{:S(2)}) %collective-permute-start.23) | collective-permute-done | bytes 262176 | tf_op jit(solution)/shard_map/value_grad/ppermute | solution.py:125
  73.8 1.5 add_convert_fusion
  75.3 1.3 collective-permute-done.4
  76.6 2.0 collective-permute-start.25
  78.6 5.8 %collective-permute-done.5 = bf16[128,1280]{1,0:T(8,128)(2,1)} collective-permute-done((bf16[128,1280]{1,0:T(8,128)(2,1)}, bf16[128,1280]{1,0:T(8,128)(2,1)}, u32[]{:S(2)}, u32[]{:S(2)}) %collective-permute-start.5) | collective-permute-done | bytes 327712 | tf_op jit(solution)/shard_map/hidden_columns/ppermute | solution.py:129
  85.6 1.6 collective-permute-start.27
  89.6 1.8 collective-permute-done.6
  91.3 5.6 %collective-permute-done.26 = bf16[128,1024]{1,0:T(8,128)(2,1)S(1)} collective-permute-done((bf16[128,1024]{1,0:T(8,128)(2,1)S(1)}, bf16[128,1024]{1,0:T(8,128)(2,1)S(1)}, u32[]{:S(2)}, u32[]{:S(2)}) %collective-permute-start.26) | collective-permute-done | bytes 262176 | tf_op jit(solution)/shard_map/value_grad/ppermute | solution.py:129
  96.9 4.7 %collective-permute-done.27 = bf16[128,1024]{1,0:T(8,128)(2,1)S(1)} collective-permute-done((bf16[128,1024]{1,0:T(8,128)(2,1)S(1)}, bf16[128,1024]{1,0:T(8,128)(2,1)S(1)}, u32[]{:S(2)}, u32[]{:S(2)}) %collective-permute-start.27) | collective-permute-done | bytes 262176 | tf_op jit(solution)/shard_map/value_grad/ppermute | solution.py:129
  101.6 2.6 %fusion.7 = f32[1280,1024]{1,0:T(8,128)S(1)} fusion(bf16[128,1280]{1,0:T(8,128)(2,1)S(1)} %collective-permute-done.6, bf16[128,1280]{1,0:T(8,128)(2,1)} %collective-permute-done.5, bf16[128,1280]{1,0:T(8,128)(2,1)} %collective-permute-done.4, bf16[128,1280]{1,0:T(8,128)(2,1)S(1)} %copy-done.3, bf16[128,1024]{1,0:T(8,128)(2,1)S(1)} %collective-permute-done.27, ...), kind=kOutput, calls=%fused_computation.27 | convolution fusion | flops 1351614464 | bytes 7602176 | tf_op jit(solution)/shard_map/weight_grad/dot_general | solution.py:185
  104.6 1.6 convolution_convert_fusion
  106.5 2.1 collective-permute-start.29
  108.6 2.6 %fusion.19 = (bf16[512,1024]{1,0:T(8,128)(2,1)S(1)}, f32[512,1024]{1,0:T(8,128)S(1)}) fusion(bf16[1280,1024]{1,0:T(8,128)(2,1)S(1)} %bitcast.63, bf16[128,1280]{1,0:T(8,128)(2,1)S(1)} %collective-permute-done.6, bf16[128,1280]{1,0:T(8,128)(2,1)} %collective-permute-done.5, bf16[128,1280]{1,0:T(8,128)(2,1)} %collective-permute-done.4, ...), kind=kOutput, calls=%fused_computation.54 | convolution fusion | flops 1347944448 | bytes 7077888 | tf_op jit(solution)/shard_map/values/dot_general | solution.py:175
  111.3 2.1 collective-permute-start.10
  114.5 1.6 collective-permute-start.12
  116.9 19.2 %collective-permute-done.10 = bf16[128,1024]{1,0:T(8,128)(2,1)S(1)} collective-permute-done((bf16[128,1024]{1,0:T(8,128)(2,1)S(1)}, bf16[128,1024]{1,0:T(8,128)(2,1)S(1)}, u32[]{:S(2)}, u32[]{:S(2)}) %collective-permute-start.10) | collective-permute-done | bytes 262176 | tf_op jit(solution)/shard_map/values/ppermute | solution.py:129
  137.1 1.6 collective-permute-start.33
  138.7 2.1 collective-permute-start.34
  141.1 5.6 %collective-permute-done.32 = bf16[160,1024]{1,0:T(8,128)(2,1)S(1)} collective-permute-done((bf16[160,1024]{1,0:T(8,128)(2,1)S(1)}, bf16[160,1024]{1,0:T(8,128)(2,1)S(1)}, u32[]{:S(2)}, u32[]{:S(2)}) %collective-permute-start.32) | collective-permute-done | bytes 327712 | tf_op jit(solution)/shard_map/weight_grad/ppermute | solution.py:141
  146.7 1.3 collective-permute-start.13
  148.0 5.1 %collective-permute-done.33 = bf16[160,1024]{1,0:T(8,128)(2,1)S(1)} collective-permute-done((bf16[160,1024]{1,0:T(8,128)(2,1)S(1)}, bf16[160,1024]{1,0:T(8,128)(2,1)S(1)}, u32[]{:S(2)}, u32[]{:S(2)}) %collective-permute-start.33) | collective-permute-done | bytes 327712 | tf_op jit(solution)/shard_map/weight_grad/ppermute | solution.py:141
  153.1 3.7 %collective-permute-start.14 = (bf16[128,1024]{1,0:T(8,128)(2,1)S(1)}, bf16[128,1024]{1,0:T(8,128)(2,1)S(1)}, u32[]{:S(2)}, u32[]{:S(2)}) collective-permute-start(bf16[128,1024]{1,0:T(8,128)(2,1)S(1)} %fusion.3.v4), channel_id=1, source_target_pairs={{0,3},{1,4},{2,5},{3,6},{4,7},{8,11},{9,12},{10,13},{11,14},{12,15... | collective-permute-start | bytes 786440 | tf_op jit(solution)/shard_map/values/ppermute | solution.py:121
  157.0 1.7 collective-permute-start.35
  158.8 3.7 %collective-permute-start.15 = (bf16[128,1024]{1,0:T(8,128)(2,1)S(1)}, bf16[128,1024]{1,0:T(8,128)(2,1)S(1)}, u32[]{:S(2)}, u32[]{:S(2)}) collective-permute-start(bf16[128,1024]{1,0:T(8,128)(2,1)S(1)} %fusion.3.v4), channel_id=1, source_target_pairs={{0,2},{1,3},{2,4},{3,5},{4,6},{5,7},{8,10},{9,11},{10,12},{11,13},... | collective-permute-start | bytes 786440 | tf_op jit(solution)/shard_map/values/ppermute | solution.py:121
  162.6 4.8 %collective-permute-done.35 = bf16[40,1024]{1,0:T(8,128)(2,1)S(1)} collective-permute-done((bf16[40,1024]{1,0:T(8,128)(2,1)S(1)}, bf16[40,1024]{1,0:T(8,128)(2,1)S(1)}, u32[]{:S(2)}, u32[]{:S(2)}) %collective-permute-start.35) | collective-permute-done | bytes 81952 | tf_op jit(solution)/shard_map/weight_grad/ppermute | solution.py:137
  167.4 3.2 %collective-permute-start.16 = (bf16[128,1024]{1,0:T(8,128)(2,1)S(1)}, bf16[128,1024]{1,0:T(8,128)(2,1)S(1)}, u32[]{:S(2)}, u32[]{:S(2)}) collective-permute-start(bf16[128,1024]{1,0:T(8,128)(2,1)S(1)} %fusion.3.v4), channel_id=1, source_target_pairs={{0,1},{1,2},{2,3},{3,4},{4,5},{5,6},{6,7},{8,9},{9,10},{10,11},{11... | collective-permute-start | bytes 786440 | tf_op jit(solution)/shard_map/values/ppermute | solution.py:121
  170.7 4.4 %collective-permute-done.37 = bf16[40,1024]{1,0:T(8,128)(2,1)S(1)} collective-permute-done((bf16[40,1024]{1,0:T(8,128)(2,1)S(1)}, bf16[40,1024]{1,0:T(8,128)(2,1)S(1)}, u32[]{:S(2)}, u32[]{:S(2)}) %collective-permute-start.37) | collective-permute-done | bytes 81952 | tf_op jit(solution)/shard_map/weight_grad/ppermute | solution.py:137
  176.0 2.7 %collective-permute-done.16.v3 = bf16[128,1024]{1,0:T(8,128)(2,1)S(1)} collective-permute-done((bf16[128,1024]{1,0:T(8,128)(2,1)S(1)}, bf16[128,1024]{1,0:T(8,128)(2,1)S(1)}, u32[]{:S(2)}, u32[]{:S(2)}) %collective-permute-start.16) | collective-permute-done | bytes 262176 | tf_op jit(solution)/shard_map/values/ppermute | solution.py:121
  179.5 16.8 %grads.1 = (bf16[128,8192]{1,0:T(8,128)(2,1)}, bf16[128,8192]{1,0:T(8,128)(2,1)}, bf16[128,1024]{1,0:T(8,128)(2,1)}, bf16[128,1024]{1,0:T(8,128)(2,1)}, bf16[128...) custom-call(bf16[8,640,1024]{2,1,0:T(8,128)(2,1)} %get-tuple-element.21.e, ...), custom_call_target="tpu_custom_call" | custom-call | flops 5368709120 | bytes 18874368 | tf_op jit(solution)/shard_map/grads/pallas_call | solution.py:110
  198.9 1.9 collective-permute-start.19
  200.8 3.0 %collective-permute-start.20 = (bf16[128,1024]{1,0:T(8,128)(2,1)}, bf16[128,1024]{1,0:T(8,128)(2,1)S(1)}, u32[]{:S(2)}, u32[]{:S(2)}) collective-permute-start(bf16[128,1024]{1,0:T(8,128)(2,1)} %get-tuple-element.31), channel_id=1, source_target_pairs={{1,0},{2,1},{3,2},{4,3},{5,4},{6,5},{7,6},{9,8},{10,9},{11,10},{12... | collective-permute-start | bytes 786440 | tf_op jit(solution)/shard_map/key_grad/ppermute | solution.py:125
  203.8 5.5 %collective-permute-start.39 = (bf16[40,1024]{1,0:T(8,128)(2,1)S(1)}, bf16[40,1024]{1,0:T(8,128)(2,1)S(1)}, u32[]{:S(2)}, u32[]{:S(2)}) collective-permute-start(bf16[40,1024]{1,0:T(8,128)(2,1)S(1)} %get-tuple-element.38), channel_id=1, source_target_pairs={{0,4},{1,5},{2,6},{3,7},{4,0},{5,1},{6,2},{7,3},{8,12},{9,13},{10,... | collective-permute-start | bytes 245768 | tf_op jit(solution)/shard_map/weight_grad/ppermute | solution.py:137
  209.4 15.3 %collective-permute-done.39 = bf16[40,1024]{1,0:T(8,128)(2,1)S(1)} collective-permute-done((bf16[40,1024]{1,0:T(8,128)(2,1)S(1)}, bf16[40,1024]{1,0:T(8,128)(2,1)S(1)}, u32[]{:S(2)}, u32[]{:S(2)}) %collective-permute-start.39) | collective-permute-done | bytes 81952 | tf_op jit(solution)/shard_map/weight_grad/ppermute | solution.py:137
  224.7 4.4 %collective-permute-done.40 = bf16[40,1024]{1,0:T(8,128)(2,1)S(1)} collective-permute-done((bf16[40,1024]{1,0:T(8,128)(2,1)S(1)}, bf16[40,1024]{1,0:T(8,128)(2,1)S(1)}, u32[]{:S(2)}, u32[]{:S(2)}) %collective-permute-start.40) | collective-permute-done | bytes 81952 | tf_op jit(solution)/shard_map/weight_grad/ppermute | solution.py:137
  229.3 1.9 add_convert_fusion.1
  231.3 6.5 %collective-permute-done.41 = bf16[4,40,1024]{2,1,0:T(8,128)(2,1)S(1)} collective-permute-done((bf16[4,40,1024]{2,1,0:T(8,128)(2,1)S(1)}, bf16[4,40,1024]{2,1,0:T(8,128)(2,1)S(1)}, u32[]{:S(2)}, u32[]{:S(2)}) %collective-permute-start.41) | collective-permute-done | bytes 327712 | tf_op jit(solution)/shard_map/weight_grad/ppermute | solution.py:137
  (101 shorter events, 22.0 us)
Async XLA Ops:
  0.6 15.2 %collective-permute-start = (bf16[128,1024]{1,0:T(8,128)(2,1)}, bf16[128,1024]{1,0:T(8,128)(2,1)S(1)}, u32[]{:S(2)}, u32[]{:S(2)}) collective-permute-start(bf16[128,1024]{1,0:T(8,128)(2,1)} %k4.3), channel_id=1, source_target_pairs={{0,4},{1,5},{2,6},{3,7},{8,12},{9,13},{10,14},{11,15},{16,20},{17,... | collective-permute-start | bytes 786440 | tf_op jit(solution)/shard_map/keys_forward/ppermute | solution.py:121
  4.7 12.5 %collective-permute-start.1 = (bf16[128,1024]{1,0:T(8,128)(2,1)}, bf16[128,1024]{1,0:T(8,128)(2,1)S(1)}, u32[]{:S(2)}, u32[]{:S(2)}) collective-permute-start(bf16[128,1024]{1,0:T(8,128)(2,1)} %k4.3), channel_id=1, source_target_pairs={{0,3},{1,4},{2,5},{3,6},{4,7},{8,11},{9,12},{10,13},{11,14},{12,15... | collective-permute-start | bytes 786440 | tf_op jit(solution)/shard_map/keys_forward/ppermute | solution.py:121
  8.7 14.9 %collective-permute-start.2 = (bf16[128,1024]{1,0:T(8,128)(2,1)}, bf16[128,1024]{1,0:T(8,128)(2,1)S(1)}, u32[]{:S(2)}, u32[]{:S(2)}) collective-permute-start(bf16[128,1024]{1,0:T(8,128)(2,1)} %k4.3), channel_id=1, source_target_pairs={{0,2},{1,3},{2,4},{3,5},{4,6},{5,7},{8,10},{9,11},{10,12},{11,13},... | collective-permute-start | bytes 786440 | tf_op jit(solution)/shard_map/keys_forward/ppermute | solution.py:121
  11.8 20.9 %collective-permute-start.3 = (bf16[128,1024]{1,0:T(8,128)(2,1)}, bf16[128,1024]{1,0:T(8,128)(2,1)S(1)}, u32[]{:S(2)}, u32[]{:S(2)}) collective-permute-start(bf16[128,1024]{1,0:T(8,128)(2,1)} %k4.3), channel_id=1, source_target_pairs={{0,1},{1,2},{2,3},{3,4},{4,5},{5,6},{6,7},{8,9},{9,10},{10,11},{11... | collective-permute-start | bytes 786440 | tf_op jit(solution)/shard_map/keys_forward/ppermute | solution.py:121
  14.3 71.2 %collective-permute-start.7 = (bf16[320,1024]{1,0:T(8,128)(2,1)}, bf16[320,1024]{1,0:T(8,128)(2,1)}, u32[]{:S(2)}, u32[]{:S(2)}) collective-permute-start(bf16[320,1024]{1,0:T(8,128)(2,1)} %param.7), channel_id=1, source_target_pairs={{0,8},{8,0},{16,24},{24,16},{32,40},{40,32},{48,56},{56,48},{64,72... | collective-permute-start | bytes 1966088 | tf_op jit(solution)/shard_map/weight_rows/ppermute | solution.py:133
  15.8 38.1 %copy-start.1 = (bf16[128,5120]{1,0:T(8,128)(2,1)S(1)}, bf16[128,5120]{1,0:T(8,128)(2,1)}, u32[]{:S(2)}) copy-start(bf16[128,5120]{1,0:T(8,128)(2,1)} %param.6) | copy-start | bytes 3932164
  15.8 16.9 %copy-start.7 = (bf16[128,1024]{1,0:T(8,128)(2,1)}, bf16[128,1024]{1,0:T(8,128)(2,1)S(1)}, u32[]{:S(2)}) copy-start(bf16[128,1024]{1,0:T(8,128)(2,1)S(1)} %collective-permute-done.k0) | copy-start | bytes 786436
  15.8 72.5 %collective-permute-start.8 = (bf16[320,1024]{1,0:T(8,128)(2,1)}, bf16[320,1024]{1,0:T(8,128)(2,1)}, u32[]{:S(2)}, u32[]{:S(2)}) collective-permute-start(bf16[320,1024]{1,0:T(8,128)(2,1)} %param.7), channel_id=1, source_target_pairs={{0,16},{8,24},{16,0},{24,8},{32,48},{40,56},{48,32},{56,40},{64,80... | collective-permute-start | bytes 1966088 | tf_op jit(solution)/shard_map/weight_rows/ppermute | solution.py:133
  49.2 13.0 %collective-permute-start.21 = (bf16[128,1024]{1,0:T(8,128)(2,1)}, bf16[128,1024]{1,0:T(8,128)(2,1)S(1)}, u32[]{:S(2)}, u32[]{:S(2)}) collective-permute-start(bf16[128,1024]{1,0:T(8,128)(2,1)} %get-tuple-element.33), channel_id=1, source_target_pairs={{4,0},{5,1},{6,2},{7,3},{12,8},{13,9},{14,10},{15,11},{20,16},{21,... | collective-permute-start | bytes 786440 | tf_op jit(solution)/shard_map/value_grad/ppermute | solution.py:125
  50.5 15.2 %collective-permute-start.22 = (bf16[128,1024]{1,0:T(8,128)(2,1)}, bf16[128,1024]{1,0:T(8,128)(2,1)S(1)}, u32[]{:S(2)}, u32[]{:S(2)}) collective-permute-start(bf16[128,1024]{1,0:T(8,128)(2,1)} %get-tuple-element.34), channel_id=1, source_target_pairs={{3,0},{4,1},{5,2},{6,3},{7,4},{11,8},{12,9},{13,10},{14,11},{15,12... | collective-permute-start | bytes 786440 | tf_op jit(solution)/shard_map/value_grad/ppermute | solution.py:125
  51.8 21.7 %copy-start.2 = (bf16[320,1024]{1,0:T(8,128)(2,1)S(1)}, bf16[320,1024]{1,0:T(8,128)(2,1)}, u32[]{:S(2)}) copy-start(bf16[320,1024]{1,0:T(8,128)(2,1)} %param.7) | copy-start | bytes 1966084
  51.8 19.4 %collective-permute-start.23 = (bf16[128,1024]{1,0:T(8,128)(2,1)}, bf16[128,1024]{1,0:T(8,128)(2,1)S(1)}, u32[]{:S(2)}, u32[]{:S(2)}) collective-permute-start(bf16[128,1024]{1,0:T(8,128)(2,1)} %get-tuple-element.35), channel_id=1, source_target_pairs={{2,0},{3,1},{4,2},{5,3},{6,4},{7,5},{10,8},{11,9},{12,10},{13,11},... | collective-permute-start | bytes 786440 | tf_op jit(solution)/shard_map/value_grad/ppermute | solution.py:125
  62.1 11.5 %collective-permute-start.24 = (bf16[128,1024]{1,0:T(8,128)(2,1)}, bf16[128,1024]{1,0:T(8,128)(2,1)}, u32[]{:S(2)}, u32[]{:S(2)}) collective-permute-start(bf16[128,1024]{1,0:T(8,128)(2,1)} %get-tuple-element.36), channel_id=1, source_target_pairs={{1,0},{2,1},{3,2},{4,3},{5,4},{6,5},{7,6},{9,8},{10,9},{11,10},{12... | collective-permute-start | bytes 786440 | tf_op jit(solution)/shard_map/value_grad/ppermute | solution.py:125
  65.7 10.9 %collective-permute-start.4 = (bf16[128,1280]{1,0:T(8,128)(2,1)}, bf16[128,1280]{1,0:T(8,128)(2,1)}, u32[]{:S(2)}, u32[]{:S(2)}) collective-permute-start(bf16[128,1280]{1,0:T(8,128)(2,1)} %get-tuple-element.47), channel_id=1, source_target_pairs={{0,32},{8,40},{16,48},{24,56},{32,64},{40,72},{48,80},{56,88},{64,... | collective-permute-start | bytes 983048 | tf_op jit(solution)/shard_map/hidden_columns/ppermute | solution.py:129
  71.9 12.4 %collective-permute-start.5 = (bf16[128,1280]{1,0:T(8,128)(2,1)}, bf16[128,1280]{1,0:T(8,128)(2,1)}, u32[]{:S(2)}, u32[]{:S(2)}) collective-permute-start(bf16[128,1280]{1,0:T(8,128)(2,1)} %get-tuple-element.49), channel_id=1, source_target_pairs={{0,64},{8,72},{16,80},{24,88},{32,96},{40,104},{48,112},{56,120},{... | collective-permute-start | bytes 983048 | tf_op jit(solution)/shard_map/hidden_columns/ppermute | solution.py:129
  73.7 17.7 %collective-permute-start.6 = (bf16[128,1280]{1,0:T(8,128)(2,1)}, bf16[128,1280]{1,0:T(8,128)(2,1)S(1)}, u32[]{:S(2)}, u32[]{:S(2)}) collective-permute-start(bf16[128,1280]{1,0:T(8,128)(2,1)} %get-tuple-element.48), channel_id=1, source_target_pairs={{0,96},{8,104},{16,112},{24,120},{32,0},{40,8},{48,16},{56,24},{64... | collective-permute-start | bytes 983048 | tf_op jit(solution)/shard_map/hidden_columns/ppermute | solution.py:129
  73.7 27.9 %copy-start.3 = (bf16[128,1280]{1,0:T(8,128)(2,1)S(1)}, bf16[128,1280]{1,0:T(8,128)(2,1)}, u32[]{:S(2)}) copy-start(bf16[128,1280]{1,0:T(8,128)(2,1)} %get-tuple-element.46) | copy-start | bytes 983044
  76.6 14.7 %collective-permute-start.25 = (bf16[128,1024]{1,0:T(8,128)(2,1)S(1)}, bf16[128,1024]{1,0:T(8,128)(2,1)S(1)}, u32[]{:S(2)}, u32[]{:S(2)}) collective-permute-start(bf16[128,1024]{1,0:T(8,128)(2,1)S(1)} %add_convert_fusion), channel_id=1, source_target_pairs={{0,32},{8,40},{16,48},{24,56},{32,64},{40,72},{48,80},{56,88},{64,... | collective-permute-start | bytes 786440 | tf_op jit(solution)/shard_map/value_grad/ppermute | solution.py:129
  84.3 12.6 %collective-permute-start.26 = (bf16[128,1024]{1,0:T(8,128)(2,1)S(1)}, bf16[128,1024]{1,0:T(8,128)(2,1)S(1)}, u32[]{:S(2)}, u32[]{:S(2)}) collective-permute-start(bf16[128,1024]{1,0:T(8,128)(2,1)S(1)} %add_convert_fusion), channel_id=1, source_target_pairs={{0,64},{8,72},{16,80},{24,88},{32,96},{40,104},{48,112},{56,120},{... | collective-permute-start | bytes 786440 | tf_op jit(solution)/shard_map/value_grad/ppermute | solution.py:129
  85.6 16.0 %collective-permute-start.27 = (bf16[128,1024]{1,0:T(8,128)(2,1)S(1)}, bf16[128,1024]{1,0:T(8,128)(2,1)S(1)}, u32[]{:S(2)}, u32[]{:S(2)}) collective-permute-start(bf16[128,1024]{1,0:T(8,128)(2,1)S(1)} %add_convert_fusion), channel_id=1, source_target_pairs={{0,96},{8,104},{16,112},{24,120},{32,0},{40,8},{48,16},{56,24},{64... | collective-permute-start | bytes 786440 | tf_op jit(solution)/shard_map/value_grad/ppermute | solution.py:129
  88.3 16.2 %collective-permute-start.9 = (bf16[320,1024]{1,0:T(8,128)(2,1)}, bf16[320,1024]{1,0:T(8,128)(2,1)S(1)}, u32[]{:S(2)}, u32[]{:S(2)}) collective-permute-start(bf16[320,1024]{1,0:T(8,128)(2,1)} %collective-permute-done.8), channel_id=1, source_target_pairs={{0,8},{8,0},{16,24},{24,16},{32,40},{40,32},{48,56},{56,48},{64,72... | collective-permute-start | bytes 1966088 | tf_op jit(solution)/shard_map/weight_rows/ppermute | solution.py:133
  104.4 10.1 %collective-permute-start.31 = (bf16[2,320,1024]{2,1,0:T(8,128)(2,1)S(1)}, bf16[2,320,1024]{2,1,0:T(8,128)(2,1)S(1)}, u32[]{:S(2)}, u32[]{:S(2)}) collective-permute-start(bf16[2,320,1024]{2,1,0:T(8,128)(2,1)S(1)} %fusion), channel_id=1, source_target_pairs={{0,8},{8,0},{16,24},{24,16},{32,40},{40,32},{48,56},{56,48},{64,72... | collective-permute-start | bytes 3932168 | tf_op jit(solution)/shard_map/weight_grad/ppermute | solution.py:133
  106.4 34.5 %collective-permute-start.28 = (bf16[128,1280]{1,0:T(8,128)(2,1)S(1)}, bf16[128,1280]{1,0:T(8,128)(2,1)S(1)}, u32[]{:S(2)}, u32[]{:S(2)}) collective-permute-start(bf16[128,1280]{1,0:T(8,128)(2,1)S(1)} %get-tuple-element.44), channel_id=1, source_target_pairs={{0,96},{8,104},{16,112},{24,120},{32,0},{40,8},{48,16},{56,24},{64... | collective-permute-start | bytes 983048 | tf_op jit(solution)/shard_map/input_grad/ppermute | solution.py:129
  106.5 52.3 %collective-permute-start.29 = (bf16[128,1280]{1,0:T(8,128)(2,1)S(1)}, bf16[128,1280]{1,0:T(8,128)(2,1)S(1)}, u32[]{:S(2)}, u32[]{:S(2)}) collective-permute-start(bf16[128,1280]{1,0:T(8,128)(2,1)S(1)} %get-tuple-element.43), channel_id=1, source_target_pairs={{0,64},{8,72},{16,80},{24,88},{32,96},{40,104},{48,112},{56,120},{... | collective-permute-start | bytes 983048 | tf_op jit(solution)/shard_map/input_grad/ppermute | solution.py:129
  111.3 24.8 %collective-permute-start.10 = (bf16[128,1024]{1,0:T(8,128)(2,1)S(1)}, bf16[128,1024]{1,0:T(8,128)(2,1)S(1)}, u32[]{:S(2)}, u32[]{:S(2)}) collective-permute-start(bf16[128,1024]{1,0:T(8,128)(2,1)S(1)} %get-tuple-element.50), channel_id=1, source_target_pairs={{0,96},{8,104},{16,112},{24,120},{32,0},{40,8},{48,16},{56,24},{64... | collective-permute-start | bytes 786440 | tf_op jit(solution)/shard_map/values/ppermute | solution.py:129
  113.3 23.8 %collective-permute-start.11 = (bf16[128,1024]{1,0:T(8,128)(2,1)S(1)}, bf16[128,1024]{1,0:T(8,128)(2,1)S(1)}, u32[]{:S(2)}, u32[]{:S(2)}) collective-permute-start(bf16[128,1024]{1,0:T(8,128)(2,1)S(1)} %get-tuple-element.52), channel_id=1, source_target_pairs={{0,64},{8,72},{16,80},{24,88},{32,96},{40,104},{48,112},{56,120},{... | collective-permute-start | bytes 786440 | tf_op jit(solution)/shard_map/values/ppermute | solution.py:129
  114.5 24.1 %collective-permute-start.12 = (bf16[128,1024]{1,0:T(8,128)(2,1)S(1)}, bf16[128,1024]{1,0:T(8,128)(2,1)S(1)}, u32[]{:S(2)}, u32[]{:S(2)}) collective-permute-start(bf16[128,1024]{1,0:T(8,128)(2,1)S(1)} %get-tuple-element.51), channel_id=1, source_target_pairs={{0,32},{8,40},{16,48},{24,56},{32,64},{40,72},{48,80},{56,88},{64,... | collective-permute-start | bytes 786440 | tf_op jit(solution)/shard_map/values/ppermute | solution.py:129
  136.1 10.6 %collective-permute-start.32 = (bf16[160,1024]{1,0:T(8,128)(2,1)S(1)}, bf16[160,1024]{1,0:T(8,128)(2,1)S(1)}, u32[]{:S(2)}, u32[]{:S(2)}) collective-permute-start(bf16[160,1024]{1,0:T(8,128)(2,1)S(1)} %get-tuple-element.39), channel_id=1, source_target_pairs={{0,16},{1,17},{2,18},{3,19},{4,20},{5,21},{6,22},{7,23},{8,24},{9,... | collective-permute-start | bytes 983048 | tf_op jit(solution)/shard_map/weight_grad/ppermute | solution.py:141
  137.1 16.0 %collective-permute-start.33 = (bf16[160,1024]{1,0:T(8,128)(2,1)S(1)}, bf16[160,1024]{1,0:T(8,128)(2,1)S(1)}, u32[]{:S(2)}, u32[]{:S(2)}) collective-permute-start(bf16[160,1024]{1,0:T(8,128)(2,1)S(1)} %get-tuple-element.41), channel_id=1, source_target_pairs={{0,1},{1,0},{2,3},{3,2},{4,5},{5,4},{6,7},{7,6},{8,9},{9,8},{10,11... | collective-permute-start | bytes 983048 | tf_op jit(solution)/shard_map/weight_grad/ppermute | solution.py:141
  138.7 18.1 %collective-permute-start.34 = (bf16[160,1024]{1,0:T(8,128)(2,1)S(1)}, bf16[160,1024]{1,0:T(8,128)(2,1)S(1)}, u32[]{:S(2)}, u32[]{:S(2)}) collective-permute-start(bf16[160,1024]{1,0:T(8,128)(2,1)S(1)} %get-tuple-element.40), channel_id=1, source_target_pairs={{0,17},{1,16},{2,19},{3,18},{4,21},{5,20},{6,23},{7,22},{8,25},{9,... | collective-permute-start | bytes 983048 | tf_op jit(solution)/shard_map/weight_grad/ppermute | solution.py:141
  140.9 29.8 %copy-start.6 = (bf16[128,1024]{1,0:T(8,128)(2,1)}, bf16[128,1024]{1,0:T(8,128)(2,1)S(1)}, u32[]{:S(2)}) copy-start(bf16[128,1024]{1,0:T(8,128)(2,1)S(1)} %fusion.3.v4) | copy-start | bytes 786436
  140.9 17.9 %collective-permute-start.30 = (bf16[128,1280]{1,0:T(8,128)(2,1)S(1)}, bf16[128,1280]{1,0:T(8,128)(2,1)S(1)}, u32[]{:S(2)}, u32[]{:S(2)}) collective-permute-start(bf16[128,1280]{1,0:T(8,128)(2,1)S(1)} %get-tuple-element.42), channel_id=1, source_target_pairs={{0,32},{8,40},{16,48},{24,56},{32,64},{40,72},{48,80},{56,88},{64,... | collective-permute-start | bytes 983048 | tf_op jit(solution)/shard_map/input_grad/ppermute | solution.py:129
  146.7 29.3 %collective-permute-start.13 = (bf16[128,1024]{1,0:T(8,128)(2,1)S(1)}, bf16[128,1024]{1,0:T(8,128)(2,1)S(1)}, u32[]{:S(2)}, u32[]{:S(2)}) collective-permute-start(bf16[128,1024]{1,0:T(8,128)(2,1)S(1)} %fusion.3.v4), channel_id=1, source_target_pairs={{0,4},{1,5},{2,6},{3,7},{8,12},{9,13},{10,14},{11,15},{16,20},{17,... | collective-permute-start | bytes 786440 | tf_op jit(solution)/shard_map/values/ppermute | solution.py:121
  153.1 22.9 %collective-permute-start.14 = (bf16[128,1024]{1,0:T(8,128)(2,1)S(1)}, bf16[128,1024]{1,0:T(8,128)(2,1)S(1)}, u32[]{:S(2)}, u32[]{:S(2)}) collective-permute-start(bf16[128,1024]{1,0:T(8,128)(2,1)S(1)} %fusion.3.v4), channel_id=1, source_target_pairs={{0,3},{1,4},{2,5},{3,6},{4,7},{8,11},{9,12},{10,13},{11,14},{12,15... | collective-permute-start | bytes 786440 | tf_op jit(solution)/shard_map/values/ppermute | solution.py:121
  157.0 10.3 %collective-permute-start.35 = (bf16[40,1024]{1,0:T(8,128)(2,1)S(1)}, bf16[40,1024]{1,0:T(8,128)(2,1)S(1)}, u32[]{:S(2)}, u32[]{:S(2)}) collective-permute-start(bf16[40,1024]{1,0:T(8,128)(2,1)S(1)} %get-tuple-element.53), channel_id=1, source_target_pairs={{0,2},{1,3},{2,0},{3,1},{4,6},{5,7},{6,4},{7,5},{8,10},{9,11},{10,... | collective-permute-start | bytes 245768 | tf_op jit(solution)/shard_map/weight_grad/ppermute | solution.py:137
  158.8 11.8 %collective-permute-start.36 = (bf16[40,1024]{1,0:T(8,128)(2,1)S(1)}, bf16[40,1024]{1,0:T(8,128)(2,1)S(1)}, u32[]{:S(2)}, u32[]{:S(2)}) collective-permute-start(bf16[40,1024]{1,0:T(8,128)(2,1)S(1)} %get-tuple-element.55), channel_id=1, source_target_pairs={{0,4},{1,5},{2,6},{3,7},{4,0},{5,1},{6,2},{7,3},{8,12},{9,13},{10,... | collective-permute-start | bytes 245768 | tf_op jit(solution)/shard_map/weight_grad/ppermute | solution.py:137
  158.8 17.2 %collective-permute-start.15 = (bf16[128,1024]{1,0:T(8,128)(2,1)S(1)}, bf16[128,1024]{1,0:T(8,128)(2,1)S(1)}, u32[]{:S(2)}, u32[]{:S(2)}) collective-permute-start(bf16[128,1024]{1,0:T(8,128)(2,1)S(1)} %fusion.3.v4), channel_id=1, source_target_pairs={{0,2},{1,3},{2,4},{3,5},{4,6},{5,7},{8,10},{9,11},{10,12},{11,13},... | collective-permute-start | bytes 786440 | tf_op jit(solution)/shard_map/values/ppermute | solution.py:121
  167.4 11.4 %collective-permute-start.16 = (bf16[128,1024]{1,0:T(8,128)(2,1)S(1)}, bf16[128,1024]{1,0:T(8,128)(2,1)S(1)}, u32[]{:S(2)}, u32[]{:S(2)}) collective-permute-start(bf16[128,1024]{1,0:T(8,128)(2,1)S(1)} %fusion.3.v4), channel_id=1, source_target_pairs={{0,1},{1,2},{2,3},{3,4},{4,5},{5,6},{6,7},{8,9},{9,10},{10,11},{11... | collective-permute-start | bytes 786440 | tf_op jit(solution)/shard_map/values/ppermute | solution.py:121
  170.6 4.5 %collective-permute-start.37 = (bf16[40,1024]{1,0:T(8,128)(2,1)S(1)}, bf16[40,1024]{1,0:T(8,128)(2,1)S(1)}, u32[]{:S(2)}, u32[]{:S(2)}) collective-permute-start(bf16[40,1024]{1,0:T(8,128)(2,1)S(1)} %get-tuple-element.54), channel_id=1, source_target_pairs={{0,6},{1,7},{2,4},{3,5},{4,2},{5,3},{6,0},{7,1},{8,14},{9,15},{10,... | collective-permute-start | bytes 245768 | tf_op jit(solution)/shard_map/weight_grad/ppermute | solution.py:137
  170.7 25.6 %copy-start = (bf16[128,5120]{1,0:T(8,128)(2,1)}, bf16[128,5120]{1,0:T(8,128)(2,1)S(1)}, u32[]{:S(2)}) copy-start(bf16[128,5120]{1,0:T(8,128)(2,1)S(1)} %constant_dynamic-update-slice_fusion) | copy-start | bytes 3932164
  175.2 28.6 %collective-permute-start.38 = (bf16[40,1024]{1,0:T(8,128)(2,1)S(1)}, bf16[40,1024]{1,0:T(8,128)(2,1)S(1)}, u32[]{:S(2)}, u32[]{:S(2)}) collective-permute-start(bf16[40,1024]{1,0:T(8,128)(2,1)S(1)} %get-tuple-element.38), channel_id=1, source_target_pairs={{0,2},{1,3},{2,0},{3,1},{4,6},{5,7},{6,4},{7,5},{8,10},{9,11},{10,... | collective-permute-start | bytes 245768 | tf_op jit(solution)/shard_map/weight_grad/ppermute | solution.py:137
  196.3 32.9 %collective-permute-start.17 = (bf16[128,1024]{1,0:T(8,128)(2,1)}, bf16[128,1024]{1,0:T(8,128)(2,1)S(1)}, u32[]{:S(2)}, u32[]{:S(2)}) collective-permute-start(bf16[128,1024]{1,0:T(8,128)(2,1)} %get-tuple-element.28), channel_id=1, source_target_pairs={{4,0},{5,1},{6,2},{7,3},{12,8},{13,9},{14,10},{15,11},{20,16},{21,... | collective-permute-start | bytes 786440 | tf_op jit(solution)/shard_map/key_grad/ppermute | solution.py:125
  197.6 31.7 %collective-permute-start.18 = (bf16[128,1024]{1,0:T(8,128)(2,1)}, bf16[128,1024]{1,0:T(8,128)(2,1)S(1)}, u32[]{:S(2)}, u32[]{:S(2)}) collective-permute-start(bf16[128,1024]{1,0:T(8,128)(2,1)} %get-tuple-element.29), channel_id=1, source_target_pairs={{3,0},{4,1},{5,2},{6,3},{7,4},{11,8},{12,9},{13,10},{14,11},{15,12... | collective-permute-start | bytes 786440 | tf_op jit(solution)/shard_map/key_grad/ppermute | solution.py:125
  198.9 30.4 %collective-permute-start.19 = (bf16[128,1024]{1,0:T(8,128)(2,1)}, bf16[128,1024]{1,0:T(8,128)(2,1)S(1)}, u32[]{:S(2)}, u32[]{:S(2)}) collective-permute-start(bf16[128,1024]{1,0:T(8,128)(2,1)} %get-tuple-element.30), channel_id=1, source_target_pairs={{2,0},{3,1},{4,2},{5,3},{6,4},{7,5},{10,8},{11,9},{12,10},{13,11},... | collective-permute-start | bytes 786440 | tf_op jit(solution)/shard_map/key_grad/ppermute | solution.py:125
  200.8 28.4 %collective-permute-start.20 = (bf16[128,1024]{1,0:T(8,128)(2,1)}, bf16[128,1024]{1,0:T(8,128)(2,1)S(1)}, u32[]{:S(2)}, u32[]{:S(2)}) collective-permute-start(bf16[128,1024]{1,0:T(8,128)(2,1)} %get-tuple-element.31), channel_id=1, source_target_pairs={{1,0},{2,1},{3,2},{4,3},{5,4},{6,5},{7,6},{9,8},{10,9},{11,10},{12... | collective-permute-start | bytes 786440 | tf_op jit(solution)/shard_map/key_grad/ppermute | solution.py:125
  203.8 20.9 %collective-permute-start.39 = (bf16[40,1024]{1,0:T(8,128)(2,1)S(1)}, bf16[40,1024]{1,0:T(8,128)(2,1)S(1)}, u32[]{:S(2)}, u32[]{:S(2)}) collective-permute-start(bf16[40,1024]{1,0:T(8,128)(2,1)S(1)} %get-tuple-element.38), channel_id=1, source_target_pairs={{0,4},{1,5},{2,6},{3,7},{4,0},{5,1},{6,2},{7,3},{8,12},{9,13},{10,... | collective-permute-start | bytes 245768 | tf_op jit(solution)/shard_map/weight_grad/ppermute | solution.py:137
  224.7 4.4 %collective-permute-start.40 = (bf16[40,1024]{1,0:T(8,128)(2,1)S(1)}, bf16[40,1024]{1,0:T(8,128)(2,1)S(1)}, u32[]{:S(2)}, u32[]{:S(2)}) collective-permute-start(bf16[40,1024]{1,0:T(8,128)(2,1)S(1)} %get-tuple-element.38), channel_id=1, source_target_pairs={{0,6},{1,7},{2,4},{3,5},{4,2},{5,3},{6,0},{7,1},{8,14},{9,15},{10,... | collective-permute-start | bytes 245768 | tf_op jit(solution)/shard_map/weight_grad/ppermute | solution.py:137
  229.1 8.7 %collective-permute-start.41 = (bf16[4,40,1024]{2,1,0:T(8,128)(2,1)S(1)}, bf16[4,40,1024]{2,1,0:T(8,128)(2,1)S(1)}, u32[]{:S(2)}, u32[]{:S(2)}) collective-permute-start(bf16[4,40,1024]{2,1,0:T(8,128)(2,1)S(1)} %bitcast_dynamic-update-slice_fusion.6), channel_id=1, source_target_pairs={{0,1},{1,0},{2,3},{3,2},{4,5},{5,4},{6,7},{7,6},{8,9},{9,8},{10,11... | collective-permute-start | bytes 983048 | tf_op jit(solution)/shard_map/weight_grad/ppermute | solution.py:137
  (9 other events, 40.6 us)

commit v2 on v1

v2 whole, which is shorter than its diff:
```python
import functools
import math

import jax
import jax.numpy as jnp
from jax import lax
from jax.experimental import pallas as pl
from jax.experimental.pallas import tpu as pltpu
from jax.sharding import PartitionSpec as P

HD = 128
KV = 8
G = 8
CH = 5
SC = HD**-0.5
L2 = SC * math.log2(math.e)
bf = jnp.bfloat16
f32 = jnp.float32
VL = 56 * 1024 * 1024

def probs_kernel(meta, q, do, k0, k1, k2, k3, k4, *rest):
    e_out, qt_out, dot_out, li_out, v0, v1, v2, v3, v4, bias = rest[-10:]
    rows = q.shape[0]
    @pl.when(pl.program_id(0)==0)
    def _():
        s=meta[KV]
        r=lax.broadcasted_iota(jnp.int32,(1,rows),1)
        pos=r+s*rows
        start=jnp.zeros((1,rows),jnp.int32)
        total=meta[0]
        for d in range(1,8):
            start=jnp.where(pos>=total,total,start)
            total=total+meta[d]
        low=start-(s-(CH-1))*rows
        j=lax.broadcasted_iota(jnp.int32,(CH*rows,rows),0)
        ok=(j>=low)&(j<=r+(CH-1)*rows)
        bias[...]=jnp.where(ok,0.0,-1e30)
    for h in range(G):
        qt_out[0,:,h*rows:(h+1)*rows]=q[:,h*HD:(h+1)*HD].T
    ks=(k0,k1,k2,k3,k4)
    W=2
    n=W*rows
    for p in range(G//W):
        cols=slice(p*n,(p+1)*n)
        qt=qt_out[0,:,cols]
        ts=[]
        for c in range(CH):
            b=bias[c*rows:(c+1)*rows,:]
            b=jnp.concatenate([b]*W,axis=1)
            ts.append(jnp.dot(ks[c][...],qt,preferred_element_type=f32)*L2+b)
        m=functools.reduce(jnp.maximum,[jnp.max(t,axis=0,keepdims=True) for t in ts])
        l=jnp.zeros((1,n),f32)
        for c in range(CH):
            e=jnp.exp2(ts[c]-m)
            l=l+jnp.sum(e,axis=0,keepdims=True)
            e_out[0,c*rows:(c+1)*rows,cols]=e.astype(bf)
        li=1.0/l
        li_out[0,:,cols]=jnp.broadcast_to(li,(8,n))
        dt=jnp.concatenate([do[:,h*HD:(h+1)*HD].T for h in range(p*W,(p+1)*W)],axis=1)
        dot_out[0,:,cols]=(dt.astype(f32)*li).astype(bf)
    dall=dot_out[0]
    for c,v in enumerate((v0,v1,v2,v3,v4)):
        v[...]=lax.dot_general(e_out[0,c*rows:(c+1)*rows,:],dall,(((1,),(1,)),((),())),preferred_element_type=f32).astype(v.dtype)

def probs_call(meta, q, do, ks, first, heads, held):
    rows = q.shape[0]
    wide = G * rows
    S = jax.ShapeDtypeStruct

    def narrow():
        return pl.BlockSpec((rows, HD), lambda j: (0, j + first))

    def broad():
        return pl.BlockSpec((rows, G * HD), lambda j: (0, j + first))

    def whole(a, b):
        return pl.BlockSpec((1, a, b), lambda j: (j + first, 0, 0))

    outs = [S((KV, CH * rows, wide), bf), S((KV, HD, wide), bf), S((KV, HD, wide), bf), S((KV, 8, wide), f32)]
    outs += [S((rows, KV * HD), bf)] * (CH - 1) + [S((rows, KV * HD), f32)]
    ins = [pl.BlockSpec(memory_space=pltpu.SMEM), broad(), broad()] + [narrow() for _ in range(CH)]
    return pl.pallas_call(
        probs_kernel,
        grid=(heads,),
        in_specs=ins + [pl.BlockSpec(memory_space=pl.ANY) for _ in held],
        out_specs=[whole(CH * rows, wide), whole(HD, wide), whole(HD, wide), whole(8, wide)] + [narrow() for _ in range(CH)],
        out_shape=outs,
        scratch_shapes=[pltpu.VMEM((CH * rows, rows), f32)],
        input_output_aliases={len(ins) + i: i for i in range(len(held))},
        compiler_params=pltpu.CompilerParams(vmem_limit_bytes=VL),
        cost_estimate=pl.CostEstimate(
            flops=4 * heads * CH * rows * wide * HD,
            bytes_accessed=heads * CH * rows * wide * 2 + heads * rows * 8192,
            transcendentals=heads * CH * rows * wide,
        ),
    )(meta, q, do, *ks, *held)


def grads_kernel(e,qt,dott,li,k0,k1,k2,k3,k4,v0,v1,v2,v3,v4,out,dq,g0,g1,g2,g3,g4,ds):
    rows=out.shape[0]
    ks=(k0,k1,k2,k3,k4); vs=(v0,v1,v2,v3,v4)
    W=2; n=W*rows
    kt=jnp.concatenate([k[...].T for k in ks],axis=1)
    vt=jnp.concatenate([v[...].T for v in vs],axis=1)
    for p in range(G//W):
        cols=slice(p*n,(p+1)*n)
        o=jnp.dot(vt,e[0,:,cols],preferred_element_type=f32)*li[0,0:1,cols]
        ob=o.astype(bf)
        dt=dott[0,:,cols]
        delta=jnp.sum(dt.astype(f32)*o,axis=0,keepdims=True)
        for c in range(CH):
            dp=jnp.dot(vs[c][...],dt,preferred_element_type=f32)
            ds[c*rows:(c+1)*rows,cols]=(e[0,c*rows:(c+1)*rows,cols].astype(f32)*(dp-delta)).astype(bf)
        dqt=(jnp.dot(kt,ds[:,cols],preferred_element_type=f32)*SC).astype(bf)
        for w in range(W):
            h=p*W+w
            out[:,h*HD:(h+1)*HD]=ob[:,w*rows:(w+1)*rows].T
            dq[:,h*HD:(h+1)*HD]=dqt[:,w*rows:(w+1)*rows].T
    qall=qt[0]
    for c,g in enumerate((g0,g1,g2,g3,g4)):
        g[...]=(lax.dot_general(ds[c*rows:(c+1)*rows,:],qall,(((1,),(1,)),((),())),preferred_element_type=f32)*SC).astype(g.dtype)

def grads_call(e,qt,dott,li,ks,vs):
    rows=ks[0].shape[0]; wide=G*rows
    bs=lambda: pl.BlockSpec((rows,HD),lambda j:(0,j))
    bw=lambda: pl.BlockSpec((rows,G*HD),lambda j:(0,j))
    b3=lambda a,b: pl.BlockSpec((1,a,b),lambda j:(j,0,0))
    S=jax.ShapeDtypeStruct
    return pl.pallas_call(grads_kernel,grid=(KV,),
        in_specs=[b3(CH*rows,wide),b3(HD,wide),b3(HD,wide),b3(8,wide)]+[bs() for _ in range(2*CH)],
        out_specs=[bw(),bw()]+[bs() for _ in range(CH)],
        out_shape=[S((rows,KV*G*HD),bf)]*2+[S((rows,KV*HD),bf)]*(CH-1)+[S((rows,KV*HD),f32)],
        scratch_shapes=[pltpu.VMEM((CH*rows,wide),bf)],
        compiler_params=pltpu.CompilerParams(vmem_limit_bytes=VL),
        cost_estimate=pl.CostEstimate(flops=2*4*KV*CH*rows*wide*HD,bytes_accessed=KV*CH*rows*wide*2+8*rows*8192,transcendentals=0),
        )(e,qt,dott,li,*ks,*vs)


def forward(x, k):
    return lax.ppermute(x, ("x", "zh"), [(i, i + k) for i in range(8 - k)])


def backward(x, k):
    return lax.ppermute(x, ("x", "zh"), [(i + k, i) for i in range(8 - k)])


def flip(x, axis):
    return lax.ppermute(x, axis, [(0, 1), (1, 0)])


def along_y(x, k):
    return lax.ppermute(x, "y", [(i, (i + k) % 4) for i in range(4)])


def ordered(own, other, index, axis):
    first = index == 0
    return jnp.stack([jnp.where(first, own, other), jnp.where(first, other, own)], axis=axis)


def body(hidden, weight, query, key, cot, lengths):
    rows = hidden.shape[0]
    high, width = weight.shape
    y, zl, core = (lax.axis_index(n) for n in ("y", "zl", "core"))
    seq = lax.axis_index(("x", "zh"))
    depth = hidden.shape[1] // 4
    meta = jnp.concatenate([lengths[0], seq.astype(jnp.int32)[None]])
    with jax.named_scope("keys_forward"):
        ks = [forward(key, CH - 1 - c) for c in range(CH - 1)] + [key]
    with jax.named_scope("hidden_columns"):
        hid = lax.all_to_all(hidden.reshape(rows, 4, depth), "y", 1, 0, tiled=True).reshape(4 * rows, depth)
    with jax.named_scope("weight_rows"):
        wz = ordered(weight, flip(weight, "zl"), zl, 0)
        wz, ks, hid = lax.optimization_barrier((wz, ks, hid))
        wu = ordered(wz, flip(wz, "core"), core, 1).reshape(depth, width)
    with jax.named_scope("probs"):
        held = probs_call(meta, query, cot, ks, 0, KV // 2, [])
    with jax.named_scope("values"):
        part = jnp.dot(hid, wu, preferred_element_type=f32).astype(bf).reshape(4, rows, width)
        part, held = lax.optimization_barrier((part, held))
        part = lax.all_to_all(part, "y", 0, 0, tiled=True)
        values = jnp.sum(part.astype(f32), axis=0).astype(bf)
    with jax.named_scope("probs"):
        e, qt, dott, li, *dv = probs_call(meta, query, cot, ks, KV // 2, KV // 2, held)
    with jax.named_scope("values_forward"):
        vs = [forward(values, CH - 1 - c) for c in range(CH - 1)] + [values]
    with jax.named_scope("value_grad"):
        dv = [backward(dv[c], CH - 1 - c) for c in range(CH - 1)] + [dv[-1]]
        dv, vs[2], vs[3] = lax.optimization_barrier((dv, vs[2], vs[3]))
        vgrad = sum(d.astype(f32) for d in dv).astype(bf)
        vy = jnp.broadcast_to(vgrad[None], (4,) + vgrad.shape)
        vy = lax.all_to_all(vy, "y", 0, 0, tiled=True).reshape(4 * rows, width)
        vy, vs[0], vs[1] = lax.optimization_barrier((vy, vs[0], vs[1]))
    with jax.named_scope("weight_grad"):
        g = lax.dot_general(hid, vy, (((0,), (0,)), ((), ())), preferred_element_type=f32).astype(bf)

        def half(c):
            return jnp.concatenate([lax.dynamic_slice_in_dim(g, (2 * i + c) * high, high) for i in range(2)])

        g = half(core).astype(f32) + flip(half(1 - core), "core").astype(f32)
        g = g.astype(bf).reshape(16, high // 8, width)
    with jax.named_scope("input_grad"):
        ig = lax.dot_general(vy, wu, (((1,), (1,)), ((), ())), preferred_element_type=f32).astype(bf)
    g, ig, vs = lax.optimization_barrier((g, ig, vs))
    with jax.named_scope("grads"):
        out, dq, *dk = grads_call(e, qt, dott, li, ks, vs)
    with jax.named_scope("input_grad"):
        blocks = [lax.dynamic_slice_in_dim(ig, (y - k) % 4 * rows, rows) for k in range(4)]
        igs = [blocks[0]] + [along_y(blocks[k], 4 - k) for k in (1, 2, 3)]
    with jax.named_scope("weight_grad"):
        g = lax.all_to_all(g, ("zl", "x", "zh"), 0, 0, tiled=True)
        g = jnp.sum(g.astype(f32), axis=0).astype(bf)
    g, igs, dk = lax.optimization_barrier((g, igs, dk))
    with jax.named_scope("key_grad"):
        kgrad = (dk[-1] + sum(backward(dk[c], CH - 1 - c).astype(f32) for c in range(CH - 1))).astype(bf)
    with jax.named_scope("weight_grad"):
        g = jnp.broadcast_to(g[None], (8,) + g.shape)
        wgrad = lax.all_to_all(g, ("x", "zh"), 0, 0, tiled=True).reshape(weight.shape).astype(f32)
    with jax.named_scope("input_grad"):
        input_grad = jnp.zeros(hidden.shape, bf)
        for k in range(4):
            input_grad = lax.dynamic_update_slice_in_dim(input_grad, igs[k], (y + k) % 4 * depth, axis=1)
    return out, dq, kgrad, input_grad, wgrad


def solution(mesh):
    fine = jax.sharding.Mesh(mesh.devices.reshape(4, 2, 2, 4, 2), ("y", "zl", "core", "x", "zh"))
    tok = P(("y", "zl", "core", "x", "zh"), None)
    own = P(("y", "zl", "core"), None)
    return jax.shard_map(
        body,
        mesh=fine,
        in_specs=(tok, own, tok, tok, tok, own),
        out_specs=(tok, tok, tok, tok, own),
        check_vma=False,
    )
```

time: 240 us -> 199 us (0.83)
  the two profiles are of different devices: /device:TPU:26 before, /device:TPU:67 now
where the time goes in v2:
time: 199 us; the launch traced here: 198 us
  starting transfers between devices  77.3 us (39%)
  waiting for transfers between devices  61.3 us (31%)
  Pallas kernels  34.7 us (17%)
  local copies, waits for them, and re-layouts  9.79 us (5%)
  other arithmetic  7.09 us (4%)
  matrix products  6.84 us (3%)
    ppermute x8, waiting for transfers between devices, backward(): return lax.ppermute(x, ('x', 'zh'), [(i + k, i) for i in range(8 - k)])  36 us
    ppermute x8, starting transfers between devices, forward(): return lax.ppermute(x, ('x', 'zh'), [(i, i + k) for i in range(8 - k)])  24.9 us
    ppermute x8, waiting for transfers between devices, forward(): return lax.ppermute(x, ('x', 'zh'), [(i, i + k) for i in range(8 - k)])  20 us
    pallas_call x2, Pallas kernels, probs_call(): pl.pallas_call(probs_kernel, grid=(heads,), in_specs=ins + [pl.BlockSpec(...  17.9 us
    ppermute x8, starting transfers between devices, backward(): return lax.ppermute(x, ('x', 'zh'), [(i + k, i) for i in range(8 - k)])  17.4 us
    pallas_call x1, Pallas kernels, grads_call(): pl.pallas_call(grads_kernel, grid=(KV,), in_specs=[b3(CH * rows, wide), b...  16.8 us
    all_to_all x1, starting transfers between devices, body(): g = lax.all_to_all(g, ('zl', 'x', 'zh'), 0, 0, tiled=True)  7.44 us
    all_to_all x1, starting transfers between devices, body(): lax.all_to_all(g, ('x', 'zh'), 0, 0, tiled=True).reshape(weight.shape)  6.65 us
  transfers between devices with their start and end apart: 27, of which 13 were waited for; matrix products, arithmetic and copies ran while one was open for 5% of the time, Pallas kernels for 18%

profile of v2, /device:TPU:67, one launch (start us, length us, event | category | flops | bytes accessed | tf_op | source)
XLA Modules:
  0.0 198.2 jit_solution(15558706748185796564)
XLA Ops:
  0.6 1.4 collective-permute-start
  2.1 2.4 %copy.21 = bf16[128,5120]{0,1:T(8,128)(2,1)} copy(bf16[128,5120]{1,0:T(8,128)(2,1)} %param.6) | data formatting | bytes 2621440 | tf_op args[0]
  4.5 4.3 %all-to-all-start = ((bf16[128,4,1280]{0,2,1:T(8,128)(2,1)}), bf16[128,4,1280]{0,2,1:T(8,128)(2,1)S(1)}, u32[]{:S(2)}, u32[]{:S(2)}) async-start(bf16[128,4,1280]{0,2,1:T(8,128)(2,1)} %bitcast.4), calls=%async_computation | async-start | bytes 2621440 | tf_op jit(solution)/shard_map/hidden_columns/all_to_all | solution.py:170
  8.8 3.8 %collective-permute-start.1 = (bf16[128,1024]{1,0:T(8,128)(2,1)S(1)}, bf16[128,1024]{1,0:T(8,128)(2,1)S(1)}, u32[]{:S(2)}, u32[]{:S(2)}) collective-permute-start(bf16[128,1024]{1,0:T(8,128)(2,1)S(1)} %copy-done.5), channel_id=1, source_target_pairs={{0,4},{1,5},{2,6},{3,7},{8,12},{9,13},{10,14},{11,15},{16,20},{17,... | collective-permute-start | bytes 786440 | tf_op jit(solution)/shard_map/keys_forward/ppermute | solution.py:140
  12.6 1.9 collective-permute-start.2
  14.5 1.9 collective-permute-start.3
  16.4 4.0 %collective-permute-start.4 = (bf16[128,1024]{1,0:T(8,128)(2,1)S(1)}, bf16[128,1024]{1,0:T(8,128)(2,1)}, u32[]{:S(2)}, u32[]{:S(2)}) collective-permute-start(bf16[128,1024]{1,0:T(8,128)(2,1)S(1)} %copy-done.5), channel_id=1, source_target_pairs={{0,1},{1,2},{2,3},{3,4},{4,5},{5,6},{6,7},{8,9},{9,10},{10,11},{11... | collective-permute-start | bytes 786440 | tf_op jit(solution)/shard_map/keys_forward/ppermute | solution.py:140
  20.6 4.9 %all-to-all-done = bf16[128,4,1280]{0,2,1:T(8,128)(2,1)S(1)} async-done(((bf16[128,4,1280]{0,2,1:T(8,128)(2,1)}), bf16[128,4,1280]{0,2,1:T(8,128)(2,1)S(1)}, u32[]{:S(2)}, u32[]{:S(2)}) %all-to-all-start) | async-done | bytes 1310752 | tf_op jit(solution)/shard_map/hidden_columns/all_to_all | solution.py:170
  25.5 1.4 copy.22
  26.9 3.7 %collective-permute-done.3.k2 = bf16[128,1024]{1,0:T(8,128)(2,1)} collective-permute-done((bf16[128,1024]{1,0:T(8,128)(2,1)S(1)}, bf16[128,1024]{1,0:T(8,128)(2,1)}, u32[]{:S(2)}, u32[]{:S(2)}) %collective-permute-start.3) | collective-permute-done | bytes 262176 | tf_op jit(solution)/shard_map/keys_forward/ppermute | solution.py:140
  30.7 5.6 %collective-permute-done.4.k3 = bf16[128,1024]{1,0:T(8,128)(2,1)} collective-permute-done((bf16[128,1024]{1,0:T(8,128)(2,1)S(1)}, bf16[128,1024]{1,0:T(8,128)(2,1)}, u32[]{:S(2)}, u32[]{:S(2)}) %collective-permute-start.4) | collective-permute-done | bytes 262176 | tf_op jit(solution)/shard_map/keys_forward/ppermute | solution.py:140
  37.4 8.9 %probs.2 = (bf16[8,640,1024]{2,1,0:T(8,128)(2,1)}, bf16[8,128,1024]{2,1,0:T(8,128)(2,1)}, bf16[8,128,1024]{2,1,0:T(8,128)(2,1)}, f32[8,8,1024]{2,1,0:T(8,128)}, ...) custom-call(s32[9]{0:T(128)} %pad_add_fusion.meta, ...), custom_call_target="tpu_custom_call" | custom-call | flops 1342177280 | bytes 9437184 | tf_op jit(solution)/shard_map/probs/pallas_call | solution.py:82
  46.8 1.3 copy-done.3
  48.1 2.5 %convolution_convert_fusion.2 = bf16[512,1024]{1,0:T(8,128)(2,1)} fusion(bf16[512,1280]{1,0:T(8,128)(2,1)S(1)} %bitcast.33, bf16[1280,1024]{1,0:T(8,128)(2,1)S(1)} %bitcast.31), kind=kOutput, calls=%fused_computation.4 | convolution fusion | flops 1342701568 | bytes 4980736 | tf_op jit(solution)/shard_map/values/dot_general | solution.py:178
  50.6 4.2 %all-to-all-start.1 = ((bf16[4,128,1024]{2,1,0:T(8,128)(2,1)}), bf16[4,128,1024]{2,1,0:T(8,128)(2,1)S(1)}, u32[]{:S(2)}, u32[]{:S(2)}) async-start(bf16[4,128,1024]{2,1,0:T(8,128)(2,1)} %bitcast.37), calls=%async_computation.1 | async-start | bytes 2097152 | tf_op jit(solution)/shard_map/values/all_to_all | solution.py:180
  54.8 9.0 %probs.3 = (bf16[8,640,1024]{2,1,0:T(8,128)(2,1)}, bf16[8,128,1024]{2,1,0:T(8,128)(2,1)}, bf16[8,128,1024]{2,1,0:T(8,128)(2,1)}, f32[8,8,1024]{2,1,0:T(8,128)}, ...) custom-call(s32[9]{0:T(128)} %pad_add_fusion.meta, ...), custom_call_target="tpu_custom_call", output_to_operand_aliasing={{0}: (8, {}), {1}: (9, {}), {2}: (10, {}), {3}: (11, {}), {... | custom-call | flops 1342177280 | bytes 9437184 | tf_op jit(solution)/shard_map/probs/pallas_call | solution.py:82
  63.9 1.4 collective-permute-start.6
  65.3 1.9 collective-permute-start.7
  67.2 1.9 collective-permute-start.8
  69.2 5.1 %collective-permute-start.9 = (bf16[128,1024]{1,0:T(8,128)(2,1)}, bf16[128,1024]{1,0:T(8,128)(2,1)}, u32[]{:S(2)}, u32[]{:S(2)}) collective-permute-start(bf16[128,1024]{1,0:T(8,128)(2,1)} %get-tuple-element.106), channel_id=1, source_target_pairs={{1,0},{2,1},{3,2},{4,3},{5,4},{6,5},{7,6},{9,8},{10,9},{11,10},{12... | collective-permute-start | bytes 786440 | tf_op jit(solution)/shard_map/value_grad/ppermute | solution.py:144
  74.5 4.4 %collective-permute-start.10 = (bf16[128,1024]{1,0:T(8,128)(2,1)S(1)}, bf16[128,1024]{1,0:T(8,128)(2,1)S(1)}, u32[]{:S(2)}, u32[]{:S(2)}) collective-permute-start(bf16[128,1024]{1,0:T(8,128)(2,1)S(1)} %reduce_sum.24.v4), channel_id=1, source_target_pairs={{0,2},{1,3},{2,4},{3,5},{4,6},{5,7},{8,10},{9,11},{10,12},{11,13},... | collective-permute-start | bytes 786440 | tf_op jit(solution)/shard_map/values_forward/ppermute | solution.py:140
  79.0 5.8 %collective-permute-start.11 = (bf16[128,1024]{1,0:T(8,128)(2,1)S(1)}, bf16[128,1024]{1,0:T(8,128)(2,1)S(1)}, u32[]{:S(2)}, u32[]{:S(2)}) collective-permute-start(bf16[128,1024]{1,0:T(8,128)(2,1)S(1)} %reduce_sum.24.v4), channel_id=1, source_target_pairs={{0,1},{1,2},{2,3},{3,4},{4,5},{5,6},{6,7},{8,9},{9,10},{10,11},{11... | collective-permute-start | bytes 786440 | tf_op jit(solution)/shard_map/values_forward/ppermute | solution.py:140
  84.8 2.5 %collective-permute-done.8 = bf16[128,1024]{1,0:T(8,128)(2,1)} collective-permute-done((bf16[128,1024]{1,0:T(8,128)(2,1)}, bf16[128,1024]{1,0:T(8,128)(2,1)}, u32[]{:S(2)}, u32[]{:S(2)}) %collective-permute-start.8) | collective-permute-done | bytes 262176 | tf_op jit(solution)/shard_map/value_grad/ppermute | solution.py:144
  87.3 9.2 %collective-permute-done.9 = bf16[128,1024]{1,0:T(8,128)(2,1)} collective-permute-done((bf16[128,1024]{1,0:T(8,128)(2,1)}, bf16[128,1024]{1,0:T(8,128)(2,1)}, u32[]{:S(2)}, u32[]{:S(2)}) %collective-permute-start.9) | collective-permute-done | bytes 262176 | tf_op jit(solution)/shard_map/value_grad/ppermute | solution.py:144
  96.5 1.5 add_convert_fusion.2
  98.0 1.1 broadcast_in_dim.9
  99.1 4.2 %all-to-all-start.2 = ((bf16[4,128,1024]{2,1,0:T(8,128)(2,1)}), bf16[4,128,1024]{2,1,0:T(8,128)(2,1)S(1)}, u32[]{:S(2)}, u32[]{:S(2)}) async-start(bf16[4,128,1024]{2,1,0:T(8,128)(2,1)} %broadcast_in_dim.9), calls=%async_computation.2 | async-start | bytes 2097152 | tf_op jit(solution)/shard_map/value_grad/all_to_all | solution.py:191
  103.3 1.3 collective-permute-start.12
  104.6 1.9 collective-permute-start.13
  106.5 3.0 %collective-permute-done.12.v0 = bf16[128,1024]{1,0:T(8,128)(2,1)S(1)} collective-permute-done((bf16[128,1024]{1,0:T(8,128)(2,1)S(1)}, bf16[128,1024]{1,0:T(8,128)(2,1)S(1)}, u32[]{:S(2)}, u32[]{:S(2)}) %collective-permute-start.12) | collective-permute-done | bytes 262176 | tf_op jit(solution)/shard_map/values_forward/ppermute | solution.py:140
  109.5 7.7 %collective-permute-done.13.v1 = bf16[128,1024]{1,0:T(8,128)(2,1)S(1)} collective-permute-done((bf16[128,1024]{1,0:T(8,128)(2,1)S(1)}, bf16[128,1024]{1,0:T(8,128)(2,1)S(1)}, u32[]{:S(2)}, u32[]{:S(2)}) %collective-permute-start.13) | collective-permute-done | bytes 262176 | tf_op jit(solution)/shard_map/values_forward/ppermute | solution.py:140
  117.5 1.6 convolution_convert_fusion
  119.4 2.4 %collective-permute-start.14 = (bf16[640,1024]{1,0:T(8,128)(2,1)S(1)}, bf16[640,1024]{1,0:T(8,128)(2,1)S(1)}, u32[]{:S(2)}, u32[]{:S(2)}) collective-permute-start(bf16[640,1024]{1,0:T(8,128)(2,1)S(1)} %pad_maximum_fusion.2), channel_id=1, source_target_pairs={{0,8},{8,0},{1,9},{9,1},{2,10},{10,2},{3,11},{11,3},{4,12},{12,4},... | collective-permute-start | bytes 3932168 | tf_op jit(solution)/shard_map/weight_grad/ppermute | solution.py:148
  121.8 2.8 %convolution_convert_fusion.1 = bf16[512,1280]{1,0:T(8,128)(2,1)S(1)} fusion(bf16[512,1024]{1,0:T(8,128)(2,1)} %bitcast.36, bf16[1280,1024]{1,0:T(8,128)(2,1)S(1)} %bitcast.32), kind=kOutput, calls=%fused_computation.1 | convolution fusion | flops 1342832640 | bytes 4980736 | tf_op jit(solution)/shard_map/input_grad/dot_general | solution.py:202
  124.6 1.6 add_convert_fusion
  126.2 7.4 %all-to-all-start.3 = ((bf16[16,40,1024]{2,1,0:T(8,128)(2,1)}), bf16[16,40,1024]{2,1,0:T(8,128)(2,1)S(1)}, u32[]{:S(2)}, u32[]{:S(2)}) async-start(bf16[16,40,1024]{2,1,0:T(8,128)(2,1)} %bitcast.14), calls=%async_computation.3 | async-start | bytes 2621440 | tf_op jit(solution)/shard_map/weight_grad/all_to_all | solution.py:210
  134.6 2.7 %collective-permute-start.15 = (bf16[128,1280]{1,0:T(8,128)(2,1)}, bf16[128,1280]{1,0:T(8,128)(2,1)S(1)}, u32[]{:S(2)}, u32[]{:S(2)}) collective-permute-start(bf16[128,1280]{1,0:T(8,128)(2,1)} %get-tuple-element.151), channel_id=1, source_target_pairs={{0,96},{32,0},{64,32},{96,64},{1,97},{33,1},{65,33},{97,65},{2,98}... | collective-permute-start | bytes 983048 | tf_op jit(solution)/shard_map/input_grad/ppermute | solution.py:152
  138.4 16.8 %grads.1 = (bf16[128,8192]{1,0:T(8,128)(2,1)}, bf16[128,8192]{1,0:T(8,128)(2,1)}, bf16[128,1024]{1,0:T(8,128)(2,1)}, bf16[128,1024]{1,0:T(8,128)(2,1)}, bf16[128...) custom-call(bf16[8,640,1024]{2,1,0:T(8,128)(2,1)} %get-tuple-element.99.e, ...), custom_call_target="tpu_custom_call" | custom-call | flops 5368709120 | bytes 18874368 | tf_op jit(solution)/shard_map/grads/pallas_call | solution.py:129
  156.7 6.6 %all-to-all-start.4 = ((bf16[8,40,1024]{2,1,0:T(8,128)(2,1)}), bf16[8,40,1024]{2,1,0:T(8,128)(2,1)S(1)}, u32[]{:S(2)}, u32[]{:S(2)}) async-start(bf16[8,40,1024]{2,1,0:T(8,128)(2,1)} %broadcast_in_dim.21), calls=%async_computation.4 | async-start | bytes 1310720 | tf_op jit(solution)/shard_map/weight_grad/all_to_all | solution.py:217
  163.4 1.3 collective-permute-start.18
  164.6 1.9 collective-permute-start.19
  166.6 1.9 collective-permute-start.20
  168.5 1.9 collective-permute-start.21
  171.7 4.0 %collective-permute-done.18 = bf16[128,1024]{1,0:T(8,128)(2,1)S(1)} collective-permute-done((bf16[128,1024]{1,0:T(8,128)(2,1)}, bf16[128,1024]{1,0:T(8,128)(2,1)S(1)}, u32[]{:S(2)}, u32[]{:S(2)}) %collective-permute-start.18) | collective-permute-done | bytes 262176 | tf_op jit(solution)/shard_map/key_grad/ppermute | solution.py:144
  175.8 5.3 %collective-permute-done.19 = bf16[128,1024]{1,0:T(8,128)(2,1)S(1)} collective-permute-done((bf16[128,1024]{1,0:T(8,128)(2,1)}, bf16[128,1024]{1,0:T(8,128)(2,1)S(1)}, u32[]{:S(2)}, u32[]{:S(2)}) %collective-permute-start.19) | collective-permute-done | bytes 262176 | tf_op jit(solution)/shard_map/key_grad/ppermute | solution.py:144
  181.1 7.6 %collective-permute-done.20 = bf16[128,1024]{1,0:T(8,128)(2,1)S(1)} collective-permute-done((bf16[128,1024]{1,0:T(8,128)(2,1)}, bf16[128,1024]{1,0:T(8,128)(2,1)S(1)}, u32[]{:S(2)}, u32[]{:S(2)}) %collective-permute-start.20) | collective-permute-done | bytes 262176 | tf_op jit(solution)/shard_map/key_grad/ppermute | solution.py:144
  188.7 7.3 %collective-permute-done.21 = bf16[128,1024]{1,0:T(8,128)(2,1)S(1)} collective-permute-done((bf16[128,1024]{1,0:T(8,128)(2,1)S(1)}, bf16[128,1024]{1,0:T(8,128)(2,1)S(1)}, u32[]{:S(2)}, u32[]{:S(2)}) %collective-permute-start.21) | collective-permute-done | bytes 262176 | tf_op jit(solution)/shard_map/key_grad/ppermute | solution.py:144
  196.9 1.2 bitcast_convert_fusion
  (83 shorter events, 8.3 us)
Async XLA Ops:
  0.6 19.8 %collective-permute-start = (bf16[320,1024]{1,0:T(8,128)(2,1)}, bf16[320,1024]{1,0:T(8,128)(2,1)S(1)}, u32[]{:S(2)}, u32[]{:S(2)}) collective-permute-start(bf16[320,1024]{1,0:T(8,128)(2,1)} %param.7), channel_id=1, source_target_pairs={{0,16},{16,0},{1,17},{17,1},{2,18},{18,2},{3,19},{19,3},{4,20},{20... | collective-permute-start | bytes 1966088 | tf_op jit(solution)/shard_map/weight_rows/ppermute | solution.py:148
  4.5 4.3 %copy-start.5 = (bf16[128,1024]{1,0:T(8,128)(2,1)S(1)}, bf16[128,1024]{1,0:T(8,128)(2,1)}, u32[]{:S(2)}) copy-start(bf16[128,1024]{1,0:T(8,128)(2,1)} %k4.2) | copy-start | bytes 786436
  4.5 15.9 %copy-start.9 = (bf16[320,1024]{1,0:T(8,128)(2,1)S(1)}, bf16[320,1024]{1,0:T(8,128)(2,1)}, u32[]{:S(2)}) copy-start(bf16[320,1024]{1,0:T(8,128)(2,1)} %param.7) | copy-start | bytes 1966084
  4.5 21.0 %all-to-all-start = ((bf16[128,4,1280]{0,2,1:T(8,128)(2,1)}), bf16[128,4,1280]{0,2,1:T(8,128)(2,1)S(1)}, u32[]{:S(2)}, u32[]{:S(2)}) async-start(bf16[128,4,1280]{0,2,1:T(8,128)(2,1)} %bitcast.4), calls=%async_computation | async-start | bytes 2621440 | tf_op jit(solution)/shard_map/hidden_columns/all_to_all | solution.py:170
  8.8 18.1 %collective-permute-start.1 = (bf16[128,1024]{1,0:T(8,128)(2,1)S(1)}, bf16[128,1024]{1,0:T(8,128)(2,1)S(1)}, u32[]{:S(2)}, u32[]{:S(2)}) collective-permute-start(bf16[128,1024]{1,0:T(8,128)(2,1)S(1)} %copy-done.5), channel_id=1, source_target_pairs={{0,4},{1,5},{2,6},{3,7},{8,12},{9,13},{10,14},{11,15},{16,20},{17,... | collective-permute-start | bytes 786440 | tf_op jit(solution)/shard_map/keys_forward/ppermute | solution.py:140
  12.6 14.4 %collective-permute-start.2 = (bf16[128,1024]{1,0:T(8,128)(2,1)S(1)}, bf16[128,1024]{1,0:T(8,128)(2,1)S(1)}, u32[]{:S(2)}, u32[]{:S(2)}) collective-permute-start(bf16[128,1024]{1,0:T(8,128)(2,1)S(1)} %copy-done.5), channel_id=1, source_target_pairs={{0,3},{1,4},{2,5},{3,6},{4,7},{8,11},{9,12},{10,13},{11,14},{12,15... | collective-permute-start | bytes 786440 | tf_op jit(solution)/shard_map/keys_forward/ppermute | solution.py:140
  14.5 16.2 %collective-permute-start.3 = (bf16[128,1024]{1,0:T(8,128)(2,1)S(1)}, bf16[128,1024]{1,0:T(8,128)(2,1)}, u32[]{:S(2)}, u32[]{:S(2)}) collective-permute-start(bf16[128,1024]{1,0:T(8,128)(2,1)S(1)} %copy-done.5), channel_id=1, source_target_pairs={{0,2},{1,3},{2,4},{3,5},{4,6},{5,7},{8,10},{9,11},{10,12},{11,13},... | collective-permute-start | bytes 786440 | tf_op jit(solution)/shard_map/keys_forward/ppermute | solution.py:140
  16.4 19.9 %collective-permute-start.4 = (bf16[128,1024]{1,0:T(8,128)(2,1)S(1)}, bf16[128,1024]{1,0:T(8,128)(2,1)}, u32[]{:S(2)}, u32[]{:S(2)}) collective-permute-start(bf16[128,1024]{1,0:T(8,128)(2,1)S(1)} %copy-done.5), channel_id=1, source_target_pairs={{0,1},{1,2},{2,3},{3,4},{4,5},{5,6},{6,7},{8,9},{9,10},{10,11},{11... | collective-permute-start | bytes 786440 | tf_op jit(solution)/shard_map/keys_forward/ppermute | solution.py:140
  25.5 11.3 %copy-start.23 = (s32[1,8]{1,0:T(1,128)S(1)}, s32[1,8]{1,0:T(1,128)}, u32[]{:S(2)}) copy-start(s32[1,8]{1,0:T(1,128)} %param.11) | copy-start | bytes 100
  26.9 10.5 %copy-start.6 = (bf16[128,1024]{1,0:T(8,128)(2,1)}, bf16[128,1024]{1,0:T(8,128)(2,1)S(1)}, u32[]{:S(2)}) copy-start(bf16[128,1024]{1,0:T(8,128)(2,1)S(1)} %collective-permute-done.1.k0) | copy-start | bytes 786436
  26.9 10.5 %copy-start.7 = (bf16[128,1024]{1,0:T(8,128)(2,1)}, bf16[128,1024]{1,0:T(8,128)(2,1)S(1)}, u32[]{:S(2)}) copy-start(bf16[128,1024]{1,0:T(8,128)(2,1)S(1)} %collective-permute-done.2.k1) | copy-start | bytes 786436
  36.3 10.0 %collective-permute-start.5 = (bf16[2,320,1024]{2,1,0:T(8,128)(2,1)S(1)}, bf16[2,320,1024]{2,1,0:T(8,128)(2,1)S(1)}, u32[]{:S(2)}, u32[]{:S(2)}) collective-permute-start(bf16[2,320,1024]{2,1,0:T(8,128)(2,1)S(1)} %pad_maximum_fusion.1), channel_id=1, source_target_pairs={{0,8},{8,0},{1,9},{9,1},{2,10},{10,2},{3,11},{11,3},{4,12},{12,4},... | collective-permute-start | bytes 3932168 | tf_op jit(solution)/shard_map/weight_rows/ppermute | solution.py:148
  46.5 1.6 copy-start.3
  46.8 3.8 %copy-start = (bf16[2,2,320,1024]{3,2,1,0:T(8,128)(2,1)}, bf16[2,2,320,1024]{3,2,1,0:T(8,128)(2,1)S(1)}, u32[]{:S(2)}) copy-start(bf16[2,2,320,1024]{3,2,1,0:T(8,128)(2,1)S(1)} %pad_maximum_fusion) | copy-start | bytes 7864324
  50.6 23.7 %all-to-all-start.1 = ((bf16[4,128,1024]{2,1,0:T(8,128)(2,1)}), bf16[4,128,1024]{2,1,0:T(8,128)(2,1)S(1)}, u32[]{:S(2)}, u32[]{:S(2)}) async-start(bf16[4,128,1024]{2,1,0:T(8,128)(2,1)} %bitcast.37), calls=%async_computation.1 | async-start | bytes 2097152 | tf_op jit(solution)/shard_map/values/all_to_all | solution.py:180
  63.9 32.6 %copy-start.2 = (f32[128,1024]{1,0:T(8,128)S(1)}, f32[128,1024]{1,0:T(8,128)}, u32[]{:S(2)}) copy-start(f32[128,1024]{1,0:T(8,128)} %get-tuple-element.113) | copy-start | bytes 1572868
  63.9 15.1 %collective-permute-start.6 = (bf16[128,1024]{1,0:T(8,128)(2,1)}, bf16[128,1024]{1,0:T(8,128)(2,1)S(1)}, u32[]{:S(2)}, u32[]{:S(2)}) collective-permute-start(bf16[128,1024]{1,0:T(8,128)(2,1)} %get-tuple-element.103), channel_id=1, source_target_pairs={{4,0},{5,1},{6,2},{7,3},{12,8},{13,9},{14,10},{15,11},{20,16},{21,... | collective-permute-start | bytes 786440 | tf_op jit(solution)/shard_map/value_grad/ppermute | solution.py:144
  65.3 19.4 %collective-permute-start.7 = (bf16[128,1024]{1,0:T(8,128)(2,1)}, bf16[128,1024]{1,0:T(8,128)(2,1)}, u32[]{:S(2)}, u32[]{:S(2)}) collective-permute-start(bf16[128,1024]{1,0:T(8,128)(2,1)} %get-tuple-element.104), channel_id=1, source_target_pairs={{3,0},{4,1},{5,2},{6,3},{7,4},{11,8},{12,9},{13,10},{14,11},{15,12... | collective-permute-start | bytes 786440 | tf_op jit(solution)/shard_map/value_grad/ppermute | solution.py:144
  67.2 20.0 %collective-permute-start.8 = (bf16[128,1024]{1,0:T(8,128)(2,1)}, bf16[128,1024]{1,0:T(8,128)(2,1)}, u32[]{:S(2)}, u32[]{:S(2)}) collective-permute-start(bf16[128,1024]{1,0:T(8,128)(2,1)} %get-tuple-element.105), channel_id=1, source_target_pairs={{2,0},{3,1},{4,2},{5,3},{6,4},{7,5},{10,8},{11,9},{12,10},{13,11},... | collective-permute-start | bytes 786440 | tf_op jit(solution)/shard_map/value_grad/ppermute | solution.py:144
  69.2 27.3 %collective-permute-start.9 = (bf16[128,1024]{1,0:T(8,128)(2,1)}, bf16[128,1024]{1,0:T(8,128)(2,1)}, u32[]{:S(2)}, u32[]{:S(2)}) collective-permute-start(bf16[128,1024]{1,0:T(8,128)(2,1)} %get-tuple-element.106), channel_id=1, source_target_pairs={{1,0},{2,1},{3,2},{4,3},{5,4},{6,5},{7,6},{9,8},{10,9},{11,10},{12... | collective-permute-start | bytes 786440 | tf_op jit(solution)/shard_map/value_grad/ppermute | solution.py:144
  74.5 30.1 %copy-start.17 = (bf16[128,1024]{1,0:T(8,128)(2,1)}, bf16[128,1024]{1,0:T(8,128)(2,1)S(1)}, u32[]{:S(2)}) copy-start(bf16[128,1024]{1,0:T(8,128)(2,1)S(1)} %reduce_sum.24.v4) | copy-start | bytes 786436
  74.5 21.9 %collective-permute-start.10 = (bf16[128,1024]{1,0:T(8,128)(2,1)S(1)}, bf16[128,1024]{1,0:T(8,128)(2,1)S(1)}, u32[]{:S(2)}, u32[]{:S(2)}) collective-permute-start(bf16[128,1024]{1,0:T(8,128)(2,1)S(1)} %reduce_sum.24.v4), channel_id=1, source_target_pairs={{0,2},{1,3},{2,4},{3,5},{4,6},{5,7},{8,10},{9,11},{10,12},{11,13},... | collective-permute-start | bytes 786440 | tf_op jit(solution)/shard_map/values_forward/ppermute | solution.py:140
  79.0 17.5 %collective-permute-start.11 = (bf16[128,1024]{1,0:T(8,128)(2,1)S(1)}, bf16[128,1024]{1,0:T(8,128)(2,1)S(1)}, u32[]{:S(2)}, u32[]{:S(2)}) collective-permute-start(bf16[128,1024]{1,0:T(8,128)(2,1)S(1)} %reduce_sum.24.v4), channel_id=1, source_target_pairs={{0,1},{1,2},{2,3},{3,4},{4,5},{5,6},{6,7},{8,9},{9,10},{10,11},{11... | collective-permute-start | bytes 786440 | tf_op jit(solution)/shard_map/values_forward/ppermute | solution.py:140
  96.5 2.6 %copy-start.18 = (bf16[128,1024]{1,0:T(8,128)(2,1)}, bf16[128,1024]{1,0:T(8,128)(2,1)S(1)}, u32[]{:S(2)}) copy-start(bf16[128,1024]{1,0:T(8,128)(2,1)S(1)} %collective-permute-done.10.v2) | copy-start | bytes 786436
  96.5 2.6 %copy-start.19 = (bf16[128,1024]{1,0:T(8,128)(2,1)}, bf16[128,1024]{1,0:T(8,128)(2,1)S(1)}, u32[]{:S(2)}) copy-start(bf16[128,1024]{1,0:T(8,128)(2,1)S(1)} %collective-permute-done.11.v3) | copy-start | bytes 786436
  99.1 18.3 %all-to-all-start.2 = ((bf16[4,128,1024]{2,1,0:T(8,128)(2,1)}), bf16[4,128,1024]{2,1,0:T(8,128)(2,1)S(1)}, u32[]{:S(2)}, u32[]{:S(2)}) async-start(bf16[4,128,1024]{2,1,0:T(8,128)(2,1)} %broadcast_in_dim.9), calls=%async_computation.2 | async-start | bytes 2097152 | tf_op jit(solution)/shard_map/value_grad/all_to_all | solution.py:191
  103.3 6.2 %collective-permute-start.12 = (bf16[128,1024]{1,0:T(8,128)(2,1)S(1)}, bf16[128,1024]{1,0:T(8,128)(2,1)S(1)}, u32[]{:S(2)}, u32[]{:S(2)}) collective-permute-start(bf16[128,1024]{1,0:T(8,128)(2,1)S(1)} %reduce_sum.24.v4), channel_id=1, source_target_pairs={{0,4},{1,5},{2,6},{3,7},{8,12},{9,13},{10,14},{11,15},{16,20},{17,... | collective-permute-start | bytes 786440 | tf_op jit(solution)/shard_map/values_forward/ppermute | solution.py:140
  104.6 12.6 %collective-permute-start.13 = (bf16[128,1024]{1,0:T(8,128)(2,1)S(1)}, bf16[128,1024]{1,0:T(8,128)(2,1)S(1)}, u32[]{:S(2)}, u32[]{:S(2)}) collective-permute-start(bf16[128,1024]{1,0:T(8,128)(2,1)S(1)} %reduce_sum.24.v4), channel_id=1, source_target_pairs={{0,3},{1,4},{2,5},{3,6},{4,7},{8,11},{9,12},{10,13},{11,14},{12,15... | collective-permute-start | bytes 786440 | tf_op jit(solution)/shard_map/values_forward/ppermute | solution.py:140
  109.5 9.5 %copy-start.20 = (bf16[128,1024]{1,0:T(8,128)(2,1)}, bf16[128,1024]{1,0:T(8,128)(2,1)S(1)}, u32[]{:S(2)}) copy-start(bf16[128,1024]{1,0:T(8,128)(2,1)S(1)} %collective-permute-done.12.v0) | copy-start | bytes 786436
  117.2 1.8 copy-start.21
  117.4 1.6 copy-start.8
  119.3 2.5 %copy-start.1 = (bf16[2,2,320,1024]{3,2,1,0:T(8,128)(2,1)S(1)}, bf16[2,2,320,1024]{3,2,1,0:T(8,128)(2,1)}, u32[]{:S(2)}) copy-start(bf16[2,2,320,1024]{3,2,1,0:T(8,128)(2,1)} %copy-done) | copy-start | bytes 7864324
  119.4 5.2 %collective-permute-start.14 = (bf16[640,1024]{1,0:T(8,128)(2,1)S(1)}, bf16[640,1024]{1,0:T(8,128)(2,1)S(1)}, u32[]{:S(2)}, u32[]{:S(2)}) collective-permute-start(bf16[640,1024]{1,0:T(8,128)(2,1)S(1)} %pad_maximum_fusion.2), channel_id=1, source_target_pairs={{0,8},{8,0},{1,9},{9,1},{2,10},{10,2},{3,11},{11,3},{4,12},{12,4},... | collective-permute-start | bytes 3932168 | tf_op jit(solution)/shard_map/weight_grad/ppermute | solution.py:148
  126.2 29.0 %all-to-all-start.3 = ((bf16[16,40,1024]{2,1,0:T(8,128)(2,1)}), bf16[16,40,1024]{2,1,0:T(8,128)(2,1)S(1)}, u32[]{:S(2)}, u32[]{:S(2)}) async-start(bf16[16,40,1024]{2,1,0:T(8,128)(2,1)} %bitcast.14), calls=%async_computation.3 | async-start | bytes 2621440 | tf_op jit(solution)/shard_map/weight_grad/all_to_all | solution.py:210
  134.6 20.9 %collective-permute-start.15 = (bf16[128,1280]{1,0:T(8,128)(2,1)}, bf16[128,1280]{1,0:T(8,128)(2,1)S(1)}, u32[]{:S(2)}, u32[]{:S(2)}) collective-permute-start(bf16[128,1280]{1,0:T(8,128)(2,1)} %get-tuple-element.151), channel_id=1, source_target_pairs={{0,96},{32,0},{64,32},{96,64},{1,97},{33,1},{65,33},{97,65},{2,98}... | collective-permute-start | bytes 983048 | tf_op jit(solution)/shard_map/input_grad/ppermute | solution.py:152
  137.3 18.3 %collective-permute-start.16 = (bf16[128,1280]{1,0:T(8,128)(2,1)}, bf16[128,1280]{1,0:T(8,128)(2,1)S(1)}, u32[]{:S(2)}, u32[]{:S(2)}) collective-permute-start(bf16[128,1280]{1,0:T(8,128)(2,1)} %get-tuple-element.150), channel_id=1, source_target_pairs={{0,64},{32,96},{64,0},{96,32},{1,65},{33,97},{65,1},{97,33},{2,66}... | collective-permute-start | bytes 983048 | tf_op jit(solution)/shard_map/input_grad/ppermute | solution.py:152
  137.8 17.8 %collective-permute-start.17 = (bf16[128,1280]{1,0:T(8,128)(2,1)S(1)}, bf16[128,1280]{1,0:T(8,128)(2,1)S(1)}, u32[]{:S(2)}, u32[]{:S(2)}) collective-permute-start(bf16[128,1280]{1,0:T(8,128)(2,1)S(1)} %get-tuple-element.149), channel_id=1, source_target_pairs={{0,32},{32,64},{64,96},{96,0},{1,33},{33,65},{65,97},{97,1},{2,34}... | collective-permute-start | bytes 983048 | tf_op jit(solution)/shard_map/input_grad/ppermute | solution.py:152
  155.5 13.0 %copy-start.22 = (bf16[128,1024]{1,0:T(8,128)(2,1)S(1)}, bf16[128,1024]{1,0:T(8,128)(2,1)}, u32[]{:S(2)}) copy-start(bf16[128,1024]{1,0:T(8,128)(2,1)} %get-tuple-element.137) | copy-start | bytes 786436
  155.5 13.0 %copy-start.11 = (bf16[128,1280]{1,0:T(8,128)(2,1)}, bf16[128,1280]{1,0:T(8,128)(2,1)S(1)}, u32[]{:S(2)}) copy-start(bf16[128,1280]{1,0:T(8,128)(2,1)S(1)} %collective-permute-done.15) | copy-start | bytes 983044
  155.5 13.0 %copy-start.13 = (bf16[128,1280]{1,0:T(8,128)(2,1)}, bf16[128,1280]{1,0:T(8,128)(2,1)S(1)}, u32[]{:S(2)}) copy-start(bf16[128,1280]{1,0:T(8,128)(2,1)S(1)} %collective-permute-done.16) | copy-start | bytes 983044
  155.6 14.8 %copy-start.15 = (bf16[128,1280]{1,0:T(8,128)(2,1)}, bf16[128,1280]{1,0:T(8,128)(2,1)S(1)}, u32[]{:S(2)}) copy-start(bf16[128,1280]{1,0:T(8,128)(2,1)S(1)} %collective-permute-done.17) | copy-start | bytes 983044
  156.7 40.2 %all-to-all-start.4 = ((bf16[8,40,1024]{2,1,0:T(8,128)(2,1)}), bf16[8,40,1024]{2,1,0:T(8,128)(2,1)S(1)}, u32[]{:S(2)}, u32[]{:S(2)}) async-start(bf16[8,40,1024]{2,1,0:T(8,128)(2,1)} %broadcast_in_dim.21), calls=%async_computation.4 | async-start | bytes 1310720 | tf_op jit(solution)/shard_map/weight_grad/all_to_all | solution.py:217
  163.4 12.4 %collective-permute-start.18 = (bf16[128,1024]{1,0:T(8,128)(2,1)}, bf16[128,1024]{1,0:T(8,128)(2,1)S(1)}, u32[]{:S(2)}, u32[]{:S(2)}) collective-permute-start(bf16[128,1024]{1,0:T(8,128)(2,1)} %get-tuple-element.134), channel_id=1, source_target_pairs={{4,0},{5,1},{6,2},{7,3},{12,8},{13,9},{14,10},{15,11},{20,16},{21,... | collective-permute-start | bytes 786440 | tf_op jit(solution)/shard_map/key_grad/ppermute | solution.py:144
  164.6 16.4 %collective-permute-start.19 = (bf16[128,1024]{1,0:T(8,128)(2,1)}, bf16[128,1024]{1,0:T(8,128)(2,1)S(1)}, u32[]{:S(2)}, u32[]{:S(2)}) collective-permute-start(bf16[128,1024]{1,0:T(8,128)(2,1)} %get-tuple-element.135), channel_id=1, source_target_pairs={{3,0},{4,1},{5,2},{6,3},{7,4},{11,8},{12,9},{13,10},{14,11},{15,12... | collective-permute-start | bytes 786440 | tf_op jit(solution)/shard_map/key_grad/ppermute | solution.py:144
  166.6 22.1 %collective-permute-start.20 = (bf16[128,1024]{1,0:T(8,128)(2,1)}, bf16[128,1024]{1,0:T(8,128)(2,1)S(1)}, u32[]{:S(2)}, u32[]{:S(2)}) collective-permute-start(bf16[128,1024]{1,0:T(8,128)(2,1)} %get-tuple-element.136), channel_id=1, source_target_pairs={{2,0},{3,1},{4,2},{5,3},{6,4},{7,5},{10,8},{11,9},{12,10},{13,11},... | collective-permute-start | bytes 786440 | tf_op jit(solution)/shard_map/key_grad/ppermute | solution.py:144
  168.5 27.5 %collective-permute-start.21 = (bf16[128,1024]{1,0:T(8,128)(2,1)S(1)}, bf16[128,1024]{1,0:T(8,128)(2,1)S(1)}, u32[]{:S(2)}, u32[]{:S(2)}) collective-permute-start(bf16[128,1024]{1,0:T(8,128)(2,1)S(1)} %copy-done.22), channel_id=1, source_target_pairs={{1,0},{2,1},{3,2},{4,3},{5,4},{6,5},{7,6},{9,8},{10,9},{11,10},{12... | collective-permute-start | bytes 786440 | tf_op jit(solution)/shard_map/key_grad/ppermute | solution.py:144
  170.6 25.4 %copy-start.10 = (f32[128,1024]{1,0:T(8,128)S(1)}, f32[128,1024]{1,0:T(8,128)}, u32[]{:S(2)}) copy-start(f32[128,1024]{1,0:T(8,128)} %get-tuple-element.133) | copy-start | bytes 1572868
  171.7 26.5 %copy-start.4 = (bf16[128,5120]{1,0:T(8,128)(2,1)}, bf16[128,5120]{1,0:T(8,128)(2,1)S(1)}, u32[]{:S(2)}) copy-start(bf16[128,5120]{1,0:T(8,128)(2,1)S(1)} %constant_dynamic-update-slice_fusion) | copy-start | bytes 3932164
  (3 other events, 3.1 us)

commit v3 on v2

v3 whole, which is shorter than its diff:
```python
import functools
import math

import jax
import jax.numpy as jnp
from jax import lax
from jax.experimental import pallas as pl
from jax.experimental.pallas import tpu as pltpu
from jax.sharding import PartitionSpec as P

HD = 128
KV = 8
G = 8
CH = 5
N = 8
SC = HD**-0.5
L2 = SC * math.log2(math.e)
bf = jnp.bfloat16
f32 = jnp.float32
VL = 56 * 1024 * 1024
W = 4
FAR = 2
RB = 128
HP = 2


def key_mask(meta, rows, first, chunks):
    s = meta[KV]
    r = lax.broadcasted_iota(jnp.int32, (1, rows), 1)
    pos = r + s * rows
    start = jnp.zeros((1, rows), jnp.int32)
    total = meta[0]
    for d in range(1, KV):
        start = jnp.where(pos >= total, total, start)
        total = total + meta[d]
    low = start - (s - (CH - 1)) * rows
    j = lax.broadcasted_iota(jnp.int32, (chunks * rows, rows), 0) + first * rows
    return jnp.where((j >= low) & (j <= r + (CH - 1) * rows), 0.0, -1e30)


def exponentials(ks, qt, bias, e_out, cols):
    rows = bias.shape[1]
    ts = []
    for c, k in enumerate(ks):
        b = jnp.concatenate([bias[c * rows : (c + 1) * rows, :]] * W, axis=1)
        ts.append(jnp.dot(k[...], qt, preferred_element_type=f32) * L2 + b)
    m = functools.reduce(jnp.maximum, [jnp.max(t, axis=0, keepdims=True) for t in ts])
    l = jnp.zeros_like(m)
    for c, t in enumerate(ts):
        e = jnp.exp2(t - m)
        l = l + jnp.sum(e, axis=0, keepdims=True)
        e_out[0, c * rows : (c + 1) * rows, cols] = e.astype(bf)
    return m, l


def near_kernel(meta, q, do, k2, k3, k4, e_out, qt_out, dt_out, stat, bias):
    rows = q.shape[0]

    @pl.when(pl.program_id(0) == 0)
    def _():
        bias[...] = key_mask(meta, rows, FAR, CH - FAR)

    n = W * rows
    for p in range(G // W):
        cols = slice(p * n, (p + 1) * n)
        for h in range(p * W, (p + 1) * W):
            qt_out[0, :, h * rows : (h + 1) * rows] = q[:, h * HD : (h + 1) * HD].T
            dt_out[0, :, h * rows : (h + 1) * rows] = do[:, h * HD : (h + 1) * HD].T
        m, l = exponentials((k2, k3, k4), qt_out[0, :, cols], bias, e_out, cols)
        stat[0, 0:1, cols] = m
        stat[0, 1:2, cols] = l


def far_kernel(meta, qt, dt, e1, stat, k01, e_out, a_out, v01, v2, v3, v4, bias, d1, d2):
    rows = v2.shape[0]

    @pl.when(pl.program_id(0) == 0)
    def _():
        bias[...] = key_mask(meta, rows, 0, FAR)

    n = W * rows
    for p in range(G // W):
        cols = slice(p * n, (p + 1) * n)
        m2, l2 = exponentials((k01.at[0], k01.at[1]), qt[0, :, cols], bias, e_out, cols)
        m1, l1 = stat[0, 0:1, cols], stat[0, 1:2, cols]
        m = jnp.maximum(m1, m2)
        w1, w2 = jnp.exp2(m1 - m), jnp.exp2(m2 - m)
        inv = 1.0 / (l1 * w1 + l2 * w2)
        a1, a2 = w1 * inv, w2 * inv
        a_out[0, 0:1, cols] = a1
        a_out[0, 1:2, cols] = a2
        d = dt[0, :, cols].astype(f32)
        d1[:, cols] = (d * a1).astype(bf)
        d2[:, cols] = (d * a2).astype(bf)
    nt = (((1,), (1,)), ((), ()))
    for c, v in enumerate((v01.at[0], v01.at[1], v2, v3, v4)):
        if c < FAR:
            e, d = e_out[0, c * rows : (c + 1) * rows, :], d2[...]
        else:
            e, d = e1[0, (c - FAR) * rows : (c - FAR + 1) * rows, :], d1[...]
        v[...] = lax.dot_general(e, d, nt, preferred_element_type=f32).astype(v.dtype)


def grads_kernel(qt, dt, e1, e2, a, k01, k2, k3, k4, v01, v2, v3, v4, out, dq, g0, g1, g2, g3, g4, ds):
    rows = out.shape[0]
    ks = (k01.at[0], k01.at[1], k2, k3, k4)
    vs = (v01.at[0], v01.at[1], v2, v3, v4)
    n = W * rows
    kt = jnp.concatenate([k[...].T for k in ks], axis=1)
    vt1 = jnp.concatenate([v[...].T for v in vs[FAR:]], axis=1)
    vt2 = jnp.concatenate([v[...].T for v in vs[:FAR]], axis=1)
    for p in range(G // W):
        cols = slice(p * n, (p + 1) * n)
        a1, a2 = a[0, 0:1, cols], a[0, 1:2, cols]
        o = jnp.dot(vt1, e1[0, :, cols], preferred_element_type=f32) * a1
        o = o + jnp.dot(vt2, e2[0, :, cols], preferred_element_type=f32) * a2
        ob = o.astype(bf)
        d = dt[0, :, cols].astype(f32)
        d1, d2 = (d * a1).astype(bf), (d * a2).astype(bf)
        delta1 = jnp.sum(d1.astype(f32) * o, axis=0, keepdims=True)
        delta2 = jnp.sum(d2.astype(f32) * o, axis=0, keepdims=True)
        for c in range(CH):
            if c < FAR:
                dd, delta, e = d2, delta2, e2[0, c * rows : (c + 1) * rows, cols]
            else:
                dd, delta, e = d1, delta1, e1[0, (c - FAR) * rows : (c - FAR + 1) * rows, cols]
            dp = jnp.dot(vs[c][...], dd, preferred_element_type=f32)
            ds[c * rows : (c + 1) * rows, cols] = (e.astype(f32) * (dp - delta)).astype(bf)
        dqt = (jnp.dot(kt, ds[:, cols], preferred_element_type=f32) * SC).astype(bf)
        for w in range(W):
            h = p * W + w
            out[:, h * HD : (h + 1) * HD] = ob[:, w * rows : (w + 1) * rows].T
            dq[:, h * HD : (h + 1) * HD] = dqt[:, w * rows : (w + 1) * rows].T
    qall = qt[0]
    for c, g in enumerate((g0, g1, g2, g3, g4)):
        dk = lax.dot_general(
            ds[c * rows : (c + 1) * rows, :], qall, (((1,), (1,)), ((), ())), preferred_element_type=f32
        )
        g[...] = (dk * SC).astype(g.dtype)


def view(ref, kind, h):
    if kind == "m":
        return ref
    if kind == "p":
        return ref.at[:, :, pl.ds(h * HD, HD)]
    if kind in ("n", "o"):
        return ref.at[:, pl.ds(h * HD, HD)]
    if kind == "b":
        return ref.at[:, pl.ds(h * G * HD, G * HD)]
    return ref.at[pl.ds(h, 1)]


def call(kernel, args, ins, outs, scratch, products, exps):
    rows = RB
    wide = G * rows
    kinds = ins + outs
    dtypes = {"e1": ((KV, (CH - FAR) * rows, wide), bf), "e2": ((KV, FAR * rows, wide), bf), "t": ((KV, HD, wide), bf)}
    dtypes |= {"s": ((KV, 8, wide), f32), "b": ((rows, KV * G * HD), bf), "n": ((rows, KV * HD), bf)}
    dtypes |= {"o": ((rows, KV * HD), f32), "p": ((FAR, rows, KV * HD), bf)}

    def spec(kind):
        if kind == "m":
            return pl.BlockSpec(memory_space=pltpu.SMEM)
        if kind == "p":
            return pl.BlockSpec((FAR, rows, HP * HD), lambda j: (0, 0, j))
        if kind in ("n", "o"):
            return pl.BlockSpec((rows, HP * HD), lambda j: (0, j))
        if kind == "b":
            return pl.BlockSpec((rows, HP * G * HD), lambda j: (0, j))
        return pl.BlockSpec((HP,) + dtypes[kind][0][1:], lambda j: (j, 0, 0))

    def heads(*refs):
        for h in range(HP):
            kernel(*[view(r, k, h) for r, k in zip(refs, kinds)], *refs[len(kinds) :])

    return pl.pallas_call(
        heads,
        grid=(KV // HP,),
        in_specs=[spec(k) for k in ins],
        out_specs=[spec(k) for k in outs],
        out_shape=[jax.ShapeDtypeStruct(*dtypes[k]) for k in outs],
        scratch_shapes=scratch,
        compiler_params=pltpu.CompilerParams(vmem_limit_bytes=VL),
        cost_estimate=pl.CostEstimate(
            flops=products * 2 * KV * rows * wide * HD, bytes_accessed=16 << 20, transcendentals=exps * KV * rows * wide
        ),
    )(*args)


def near_call(meta, q, do, ks):
    scratch = [pltpu.VMEM(((CH - FAR) * RB, RB), f32)]
    ins = ["m", "b", "b"] + ["n"] * (CH - FAR)
    return call(near_kernel, (meta, q, do, *ks), ins, ["e1", "t", "t", "s"], scratch, CH - FAR, CH - FAR)


def far_call(meta, near, ks):
    e1, qt, dt, stat = near
    scratch = [pltpu.VMEM((FAR * RB, RB), f32)] + [pltpu.VMEM((HD, G * RB), bf)] * 2
    ins = ["m", "t", "t", "e1", "s", "p"]
    outs = ["e2", "s", "p", "n", "n", "o"]
    return call(far_kernel, (meta, qt, dt, e1, stat, ks), ins, outs, scratch, FAR + CH, FAR)


def grads_call(near, e2, a, ks, vs):
    e1, qt, dt, _ = near
    scratch = [pltpu.VMEM((CH * RB, G * RB), bf)]
    ins = ["t", "t", "e1", "e2", "s"] + ["p", "n", "n", "n"] * 2
    outs = ["b", "b"] + ["n"] * (CH - 1) + ["o"]
    return call(grads_kernel, (qt, dt, e1, e2, a, *ks, *vs), ins, outs, scratch, 4 * CH, 0)


def forward(x, k):
    return lax.ppermute(x, ("x", "zh"), [(i, i + k) for i in range(N - k)])


def backward(x, k):
    return lax.ppermute(x, ("x", "zh"), [(i + k, i) for i in range(N - k)])


def flip(x, axis):
    return lax.ppermute(x, axis, [(0, 1), (1, 0)])


def along_y(x, k):
    return lax.ppermute(x, "y", [(i, (i + k) % 4) for i in range(4)])


def over_seq(x):
    return lax.all_to_all(x, ("x", "zh"), 0, 0, tiled=True)


def ordered(own, other, index, axis):
    first = index == 0
    return jnp.stack([jnp.where(first, own, other), jnp.where(first, other, own)], axis=axis)


def relay_sum(parts, got):
    _, two, one, own = parts
    two = (two.astype(f32) + got[0].astype(f32)).astype(bf)
    one = (one.astype(f32) + got[1].astype(f32)).astype(bf)
    return own, backward(two, 2), backward(one, 1)


def turned(x, start, rows):
    n = x.shape[0] // rows
    return jnp.concatenate([lax.dynamic_slice_in_dim(x, (start - k) % n * rows, rows) for k in range(n)])


def body(hidden, weight, query, key, cot, lengths):
    rows = hidden.shape[0]
    high, width = weight.shape
    y, zl, core = (lax.axis_index(n) for n in ("y", "zl", "core"))
    seq = lax.axis_index(("x", "zh"))
    depth = hidden.shape[1] // 4
    meta = jnp.concatenate([lengths[0], seq.astype(jnp.int32)[None]])
    with jax.named_scope("keys"):
        k2, k3 = forward(key, 2), forward(key, 1)
    with jax.named_scope("hidden_columns"):
        hid = lax.all_to_all(hidden.reshape(rows, 4, depth), "y", 1, 0, tiled=True).reshape(4 * rows, depth)
    with jax.named_scope("weight_rows"):
        wz = flip(weight, "zl")
        wz, k2, k3, hid = lax.optimization_barrier((wz, k2, k3, hid))
        wz = ordered(weight, wz, zl, 0)
        wu = ordered(wz, flip(wz, "core"), core, 1).reshape(depth, width)
    with jax.named_scope("keys"):
        k01 = forward(jnp.stack([k2, k3]), 2)
    with jax.named_scope("probs_near"):
        near = near_call(meta, query, cot, (k2, k3, key))
    with jax.named_scope("values"):
        wu, k01 = lax.optimization_barrier((wu, k01))
        part = jnp.dot(hid, wu, preferred_element_type=f32).astype(bf).reshape(4, rows, width)
        part, near = lax.optimization_barrier((part, near))
        part = lax.all_to_all(part, "y", 0, 0, tiled=True)
        values = jnp.sum(part.astype(f32), axis=0).astype(bf)
    with jax.named_scope("probs_far"):
        e2, a, *dv = far_call(meta, near, k01)
    with jax.named_scope("values_forward"):
        v2, v3 = forward(values, 2), forward(values, 1)
        v01 = forward(jnp.stack([v2, v3]), 2)
    with jax.named_scope("value_grad"):
        dv = relay_sum(dv, backward(dv[0], 2))
        dv, v01, v2, v3 = lax.optimization_barrier((dv, v01, v2, v3))
        vgrad = sum(d.astype(f32) for d in dv).astype(bf)
        vys = [vgrad] + [along_y(vgrad, k) for k in (1, 2, 3)]
        vy = jnp.concatenate(vys)
        vs = (v01, v2, v3, values)
    with jax.named_scope("weight_grad"):
        turned_hid = turned(hid, y, rows)
        g = lax.dot_general(turned_hid, vy, (((0,), (0,)), ((), ())), preferred_element_type=f32).astype(bf)

        def half(c):
            return jnp.concatenate([lax.dynamic_slice_in_dim(g, (2 * i + c) * high, high) for i in range(2)])

        g = half(core).astype(f32) + flip(half(1 - core), "core").astype(f32)
        g = g.astype(bf).reshape(2 * N, high // N, width)
    with jax.named_scope("input_grad"):
        ig = lax.dot_general(vy, wu, (((1,), (1,)), ((), ())), preferred_element_type=f32).astype(bf)
        g, ig, vs = lax.optimization_barrier((g, ig, vs))
        igs = [ig[k * rows : (k + 1) * rows] for k in range(4)]
        igs = [igs[0]] + [along_y(igs[k], 4 - k) for k in (1, 2, 3)]
    with jax.named_scope("weight_grad"):
        g = lax.all_to_all(g, ("zl", "x", "zh"), 0, 0, tiled=True)
        g = jnp.sum(g.astype(f32), axis=0).astype(bf)
    with jax.named_scope("grads"):
        out, dq, *dk = grads_call(near, e2, a, (k01, k2, k3, key), vs)
        g, dk, igs = lax.optimization_barrier((g, dk, igs))
    with jax.named_scope("key_grad"):
        dk = [backward(dk[c], CH - 1 - c) for c in range(CH - 1)] + [dk[-1]]
        kgrad = sum(d.astype(f32) for d in dk).astype(bf)
    with jax.named_scope("weight_grad"):
        g = jnp.broadcast_to(g[None], (N,) + g.shape)
        wgrad = over_seq(g).reshape(weight.shape).astype(f32)
    with jax.named_scope("input_grad"):
        input_grad = jnp.zeros(hidden.shape, bf)
        for k in range(4):
            input_grad = lax.dynamic_update_slice_in_dim(input_grad, igs[k], (y + k) % 4 * depth, axis=1)
    return out, dq, kgrad, input_grad, wgrad


def solution(mesh):
    fine = jax.sharding.Mesh(mesh.devices.reshape(4, 2, 2, 4, 2), ("y", "zl", "core", "x", "zh"))
    tok = P(("y", "zl", "core", "x", "zh"), None)
    own = P(("y", "zl", "core"), None)
    return jax.shard_map(
        body,
        mesh=fine,
        in_specs=(tok, own, tok, tok, tok, own),
        out_specs=(tok, tok, tok, tok, own),
        check_vma=False,
    )
```

time: 199 us -> 199 us (level)
  other arithmetic: 7.09 us -> 12.1 us
  starting transfers between devices: 77.3 us -> 73.5 us
  local copies, waits for them, and re-layouts: 9.79 us -> 6.48 us
  waiting for transfers between devices: 61.3 us -> 64.2 us
    ppermute x16 -> x13, waiting for transfers between devices: 56 us -> 42.6 us  [the longest x7 31 us: backward(): return lax.ppermute(x, ('x', 'zh'), [(i + k, i) for i in range(N - k)])]
    ppermute x3 -> x6, waiting for transfers between devices: 0.1 us -> 8.76 us  [along_y(): return lax.ppermute(x, 'y', [(i, (i + k) % 4) for i in range(4)])]
    ppermute x16 -> x13, starting transfers between devices: 42.4 us -> 34.2 us  [the longest x7 17.8 us: backward(): return lax.ppermute(x, ('x', 'zh'), [(i + k, i) for i in range(N - k)])]
    all_to_all x1, waiting for transfers between devices: 4.86 us -> 10.3 us  [body(): lax.all_to_all(hidden.reshape(rows, 4, depth), 'y', 1, 0, tiled=True)]
    ppermute x3 -> x6, starting transfers between devices: 3.83 us -> 8.42 us  [along_y(): return lax.ppermute(x, 'y', [(i, (i + k) % 4) for i in range(4)])]
    ppermute x3, starting transfers between devices: 4.27 us -> 8.74 us  [flip(): return lax.ppermute(x, axis, [(0, 1), (1, 0)])]
    all_to_all x2 -> x1, starting transfers between devices: 10.8 us -> 6.65 us  [over_seq(): return lax.all_to_all(x, ('x', 'zh'), 0, 0, tiled=True)]
    another operation x4, other arithmetic: 0.63 us -> 4.08 us  [ordered(): jnp.stack([jnp.where(first, own, other), jnp.where(first, other, own)], a...]
  transfers between devices with their start and end apart: 27 -> 26, of which waited for: 13 -> 16; matrix products, arithmetic and copies ran while one was open for 5% -> 5% of each run, Pallas kernels for 18% -> 18%
where the time goes in v3:
time: 199 us; the launch traced here: 198 us
  starting transfers between devices  73.5 us (37%)
  waiting for transfers between devices  64.2 us (32%)
  Pallas kernels  34.6 us (17%)
  other arithmetic  12.1 us (6%)
  local copies, waits for them, and re-layouts  6.48 us (3%)
  matrix products  5.63 us (3%)
    pallas_call x3, Pallas kernels, call(): pl.pallas_call(heads, grid=(KV // HP,), in_specs=[spec(k) for k in ins],...  34.6 us
    ppermute x7, waiting for transfers between devices, backward(): return lax.ppermute(x, ('x', 'zh'), [(i + k, i) for i in range(N - k)])  31 us
    ppermute x7, starting transfers between devices, backward(): return lax.ppermute(x, ('x', 'zh'), [(i + k, i) for i in range(N - k)])  17.8 us
    ppermute x6, starting transfers between devices, forward(): return lax.ppermute(x, ('x', 'zh'), [(i, i + k) for i in range(N - k)])  16.4 us
    ppermute x6, waiting for transfers between devices, forward(): return lax.ppermute(x, ('x', 'zh'), [(i, i + k) for i in range(N - k)])  11.6 us
    all_to_all x1, waiting for transfers between devices, body(): lax.all_to_all(hidden.reshape(rows, 4, depth), 'y', 1, 0, tiled=True)  10.3 us
    ppermute x6, waiting for transfers between devices, along_y(): return lax.ppermute(x, 'y', [(i, (i + k) % 4) for i in range(4)])  8.76 us
    ppermute x3, starting transfers between devices, flip(): return lax.ppermute(x, axis, [(0, 1), (1, 0)])  8.74 us
  transfers between devices with their start and end apart: 26, of which 16 were waited for; matrix products, arithmetic and copies ran while one was open for 5% of the time, Pallas kernels for 18%

profile of v3, /device:TPU:67, one launch (start us, length us, event | category | flops | bytes accessed | tf_op | source)
XLA Modules:
  0.0 197.6 jit_solution(14819112975382418407)
XLA Ops:
  0.6 2.4 %copy.12 = bf16[128,5120]{0,1:T(8,128)(2,1)} copy(bf16[128,5120]{1,0:T(8,128)(2,1)} %param.6) | data formatting | bytes 2621440 | tf_op args[0]
  3.1 4.3 %all-to-all-start = ((bf16[128,4,1280]{0,2,1:T(8,128)(2,1)}), bf16[128,4,1280]{0,2,1:T(8,128)(2,1)S(1)}, u32[]{:S(2)}, u32[]{:S(2)}) async-start(bf16[128,4,1280]{0,2,1:T(8,128)(2,1)} %bitcast), calls=%async_computation | async-start | bytes 2621440 | tf_op jit(solution)/shard_map/hidden_columns/all_to_all | solution.py:260
  7.4 1.3 collective-permute-start
  8.7 3.1 %collective-permute-start.1 = (bf16[128,1024]{1,0:T(8,128)(2,1)}, bf16[128,1024]{1,0:T(8,128)(2,1)S(1)}, u32[]{:S(2)}, u32[]{:S(2)}) collective-permute-start(bf16[128,1024]{1,0:T(8,128)(2,1)} %refs_8_.1), channel_id=1, source_target_pairs={{0,2},{1,3},{2,4},{3,5},{4,6},{5,7},{8,10},{9,11},{10,12},{11,13},... | collective-permute-start | bytes 786440 | tf_op jit(solution)/shard_map/keys/ppermute | solution.py:214
  11.8 2.2 %collective-permute-start.2 = (bf16[128,1024]{1,0:T(8,128)(2,1)}, bf16[128,1024]{1,0:T(8,128)(2,1)}, u32[]{:S(2)}, u32[]{:S(2)}) collective-permute-start(bf16[128,1024]{1,0:T(8,128)(2,1)} %refs_8_.1), channel_id=1, source_target_pairs={{0,1},{1,2},{2,3},{3,4},{4,5},{5,6},{6,7},{8,9},{9,10},{10,11},{11... | collective-permute-start | bytes 786440 | tf_op jit(solution)/shard_map/keys/ppermute | solution.py:214
  14.1 10.3 %all-to-all-done = bf16[128,4,1280]{0,2,1:T(8,128)(2,1)S(1)} async-done(((bf16[128,4,1280]{0,2,1:T(8,128)(2,1)}), bf16[128,4,1280]{0,2,1:T(8,128)(2,1)S(1)}, u32[]{:S(2)}, u32[]{:S(2)}) %all-to-all-start) | async-done | bytes 1310752 | tf_op jit(solution)/shard_map/hidden_columns/all_to_all | solution.py:260
  25.0 2.9 %collective-permute-done.2.refs_4_.refs_7_ = bf16[128,1024]{1,0:T(8,128)(2,1)} collective-permute-done((bf16[128,1024]{1,0:T(8,128)(2,1)}, bf16[128,1024]{1,0:T(8,128)(2,1)}, u32[]{:S(2)}, u32[]{:S(2)}) %collective-permute-start.2) | collective-permute-done | bytes 262176 | tf_op jit(solution)/shard_map/keys/ppermute | solution.py:214
  30.7 1.9 collective-permute-start.3
  34.2 3.1 %collective-permute-start.4 = (bf16[2,128,1024]{2,1,0:T(8,128)(2,1)S(1)}, bf16[2,128,1024]{2,1,0:T(8,128)(2,1)S(1)}, u32[]{:S(2)}, u32[]{:S(2)}) collective-permute-start(bf16[2,128,1024]{2,1,0:T(8,128)(2,1)S(1)} %pad_maximum_fusion.4), channel_id=1, source_target_pairs={{0,2},{1,3},{2,4},{3,5},{4,6},{5,7},{8,10},{9,11},{10,12},{11,13},... | collective-permute-start | bytes 1572872 | tf_op jit(solution)/shard_map/keys/ppermute | solution.py:214
  37.3 9.2 %probs_near.1 = (bf16[8,384,1024]{2,1,0:T(8,128)(2,1)}, bf16[8,128,1024]{2,1,0:T(8,128)(2,1)}, bf16[8,128,1024]{2,1,0:T(8,128)(2,1)}, f32[8,8,1024]{2,1,0:T(8,128)}) custom-call(s32[9]{0:T(128)} %pad_add_fusion.refs_0_, bf16[128,8192]{1,0:T(8,128)(2,1)} %refs_1_.1, bf16[128,8192]{1,0:T(8,128)(2,1)} %refs_2_.1, bf16[128,1024]{1,0:T(8,128)(2,1)} %copy-done.14, ...), custom_call_target="tpu_custom_call" | custom-call | flops 805306368 | bytes 16777216 | tf_op jit(solution)/shard_map/probs_near/pallas_call | solution.py:177
  46.5 1.5 select_bitcast_fusion.1
  48.2 1.4 collective-permute-done.4.refs_5_
  49.6 2.5 %convolution_convert_fusion.2 = bf16[512,1024]{1,0:T(8,128)(2,1)} fusion(bf16[512,1280]{1,0:T(8,128)(2,1)S(1)} %bitcast.40, bf16[1280,1024]{1,0:T(8,128)(2,1)S(1)} %bitcast.43), kind=kOutput, calls=%fused_computation.4 | convolution fusion | flops 1342701568 | bytes 4980736 | tf_op jit(solution)/shard_map/values/dot_general | solution.py:272
  52.1 4.2 %all-to-all-start.1 = ((bf16[4,128,1024]{2,1,0:T(8,128)(2,1)}), bf16[4,128,1024]{2,1,0:T(8,128)(2,1)S(1)}, u32[]{:S(2)}, u32[]{:S(2)}) async-start(bf16[4,128,1024]{2,1,0:T(8,128)(2,1)} %bitcast.12), calls=%async_computation.1 | async-start | bytes 2097152 | tf_op jit(solution)/shard_map/values/all_to_all | solution.py:274
  56.4 11.2 %probs_far.1 = (bf16[8,256,1024]{2,1,0:T(8,128)(2,1)}, f32[8,8,1024]{2,1,0:T(8,128)}, bf16[2,128,1024]{2,1,0:T(8,128)(2,1)}, bf16[128,1024]{1,0:T(8,128)(2,1)}, ...) custom-call(s32[9]{0:T(128)} %pad_add_fusion.refs_0_, bf16[8,128,1024]{2,1,0:T(8,128)(2,1)} %get-tuple-element.64.refs_1_.refs_0_, ...), custom_call_target="tpu_custom_call" | custom-call | flops 1879048192 | bytes 16777216 | tf_op jit(solution)/shard_map/probs_far/pallas_call | solution.py:177
  67.6 1.9 collective-permute-start.5
  70.6 3.1 %collective-permute-start.8 = (bf16[128,1024]{1,0:T(8,128)(2,1)S(1)}, bf16[128,1024]{1,0:T(8,128)(2,1)S(1)}, u32[]{:S(2)}, u32[]{:S(2)}) collective-permute-start(bf16[128,1024]{1,0:T(8,128)(2,1)S(1)} %reduce_sum.24.refs_12_), channel_id=1, source_target_pairs={{0,2},{1,3},{2,4},{3,5},{4,6},{5,7},{8,10},{9,11},{10,12},{11,13},... | collective-permute-start | bytes 786440 | tf_op jit(solution)/shard_map/values_forward/ppermute | solution.py:214
  73.8 1.9 collective-permute-start.9
  75.7 2.7 %collective-permute-done.8.refs_10_ = bf16[128,1024]{1,0:T(8,128)(2,1)S(1)} collective-permute-done((bf16[128,1024]{1,0:T(8,128)(2,1)S(1)}, bf16[128,1024]{1,0:T(8,128)(2,1)S(1)}, u32[]{:S(2)}, u32[]{:S(2)}) %collective-permute-start.8) | collective-permute-done | bytes 262176 | tf_op jit(solution)/shard_map/values_forward/ppermute | solution.py:214
  78.3 4.6 %collective-permute-done.9.refs_11_ = bf16[128,1024]{1,0:T(8,128)(2,1)S(1)} collective-permute-done((bf16[128,1024]{1,0:T(8,128)(2,1)S(1)}, bf16[128,1024]{1,0:T(8,128)(2,1)S(1)}, u32[]{:S(2)}, u32[]{:S(2)}) %collective-permute-start.9) | collective-permute-done | bytes 262176 | tf_op jit(solution)/shard_map/values_forward/ppermute | solution.py:214
  83.0 2.9 %collective-permute-start.10 = (bf16[2,128,1024]{2,1,0:T(8,128)(2,1)S(1)}, bf16[2,128,1024]{2,1,0:T(8,128)(2,1)}, u32[]{:S(2)}, u32[]{:S(2)}) collective-permute-start(bf16[2,128,1024]{2,1,0:T(8,128)(2,1)S(1)} %pad_maximum_fusion.5), channel_id=1, source_target_pairs={{0,2},{1,3},{2,4},{3,5},{4,6},{5,7},{8,10},{9,11},{10,12},{11,13},... | collective-permute-start | bytes 1572872 | tf_op jit(solution)/shard_map/values_forward/ppermute | solution.py:214
  86.0 2.0 %fusion.7 = (bf16[128,1024]{1,0:T(8,128)(2,1)}, bf16[128,1024]{1,0:T(8,128)(2,1)}) fusion(bf16[128,1024]{1,0:T(8,128)(2,1)} %get-tuple-element.74, bf16[2,128,1024]{2,1,0:T(8,128)(2,1)S(1)} %collective-permute-done.5, bf16[128,1024]{1,0:T(8,128)(2,1)} %get-tuple-element.72), kind=kLoop, calls=%fused_computation.23 | loop fusion | flops 1048576 | bytes 1572864 | tf_op jit(solution)/shard_map/value_grad/convert_element_type | solution.py:241
  88.0 3.3 %collective-permute-start.6 = (bf16[128,1024]{1,0:T(8,128)(2,1)}, bf16[128,1024]{1,0:T(8,128)(2,1)S(1)}, u32[]{:S(2)}, u32[]{:S(2)}) collective-permute-start(bf16[128,1024]{1,0:T(8,128)(2,1)} %get-tuple-element.122), channel_id=1, source_target_pairs={{2,0},{3,1},{4,2},{5,3},{6,4},{7,5},{10,8},{11,9},{12,10},{13,11},... | collective-permute-start | bytes 786440 | tf_op jit(solution)/shard_map/value_grad/ppermute | solution.py:218
  91.3 5.6 %collective-permute-start.7 = (bf16[128,1024]{1,0:T(8,128)(2,1)}, bf16[128,1024]{1,0:T(8,128)(2,1)S(1)}, u32[]{:S(2)}, u32[]{:S(2)}) collective-permute-start(bf16[128,1024]{1,0:T(8,128)(2,1)} %get-tuple-element.121), channel_id=1, source_target_pairs={{1,0},{2,1},{3,2},{4,3},{5,4},{6,5},{7,6},{9,8},{10,9},{11,10},{12... | collective-permute-start | bytes 786440 | tf_op jit(solution)/shard_map/value_grad/ppermute | solution.py:218
  97.0 6.8 %collective-permute-done.7 = bf16[128,1024]{1,0:T(8,128)(2,1)S(1)} collective-permute-done((bf16[128,1024]{1,0:T(8,128)(2,1)}, bf16[128,1024]{1,0:T(8,128)(2,1)S(1)}, u32[]{:S(2)}, u32[]{:S(2)}) %collective-permute-start.7) | collective-permute-done | bytes 262176 | tf_op jit(solution)/shard_map/value_grad/ppermute | solution.py:218
  103.9 1.6 collective-permute-start.11
  105.4 2.4 %collective-permute-start.12 = (bf16[128,1024]{1,0:T(8,128)(2,1)S(1)}, bf16[128,1024]{1,0:T(8,128)(2,1)S(1)}, u32[]{:S(2)}, u32[]{:S(2)}) collective-permute-start(bf16[128,1024]{1,0:T(8,128)(2,1)S(1)} %add_convert_fusion.2), channel_id=1, source_target_pairs={{0,64},{32,96},{64,0},{96,32},{1,65},{33,97},{65,1},{97,33},{2,66}... | collective-permute-start | bytes 786440 | tf_op jit(solution)/shard_map/value_grad/ppermute | solution.py:226
  107.8 1.2 collective-permute-start.13
  109.1 1.3 collective-permute-done.11
  110.4 5.0 %collective-permute-done.12 = bf16[128,1024]{1,0:T(8,128)(2,1)S(1)} collective-permute-done((bf16[128,1024]{1,0:T(8,128)(2,1)S(1)}, bf16[128,1024]{1,0:T(8,128)(2,1)S(1)}, u32[]{:S(2)}, u32[]{:S(2)}) %collective-permute-start.12) | collective-permute-done | bytes 262176 | tf_op jit(solution)/shard_map/value_grad/ppermute | solution.py:226
  115.4 1.6 convolution_convert_fusion
  117.4 5.5 %collective-permute-start.14 = (bf16[640,1024]{1,0:T(8,128)(2,1)S(1)}, bf16[640,1024]{1,0:T(8,128)(2,1)S(1)}, u32[]{:S(2)}, u32[]{:S(2)}) collective-permute-start(bf16[640,1024]{1,0:T(8,128)(2,1)S(1)} %pad_maximum_fusion.2), channel_id=1, source_target_pairs={{0,8},{8,0},{1,9},{9,1},{2,10},{10,2},{3,11},{11,3},{4,12},{12,4},... | collective-permute-start | bytes 3932168 | tf_op jit(solution)/shard_map/weight_grad/ppermute | solution.py:222
  122.9 1.6 convolution_convert_fusion.1
  125.5 1.6 add_convert_fusion
  127.2 6.9 %all-to-all-start.2 = ((bf16[16,40,1024]{2,1,0:T(8,128)(2,1)}), bf16[16,40,1024]{2,1,0:T(8,128)(2,1)S(1)}, u32[]{:S(2)}, u32[]{:S(2)}) async-start(bf16[16,40,1024]{2,1,0:T(8,128)(2,1)} %bitcast.19), calls=%async_computation.2 | async-start | bytes 2621440 | tf_op jit(solution)/shard_map/weight_grad/all_to_all | solution.py:303
  135.0 1.9 collective-permute-start.15
  138.3 14.2 %grads.1 = (bf16[128,8192]{1,0:T(8,128)(2,1)}, bf16[128,8192]{1,0:T(8,128)(2,1)}, bf16[128,1024]{1,0:T(8,128)(2,1)}, bf16[128,1024]{1,0:T(8,128)(2,1)}, bf16[128...) custom-call(bf16[8,128,1024]{2,1,0:T(8,128)(2,1)} %get-tuple-element.64.refs_1_.refs_0_, ...), custom_call_target="tpu_custom_call" | custom-call | flops 5368709120 | bytes 16777216 | tf_op jit(solution)/shard_map/grads/pallas_call | solution.py:177
  152.8 2.4 %collective-permute-done.17 = bf16[128,1280]{1,0:T(8,128)(2,1)S(1)} collective-permute-done((bf16[128,1280]{1,0:T(8,128)(2,1)S(1)}, bf16[128,1280]{1,0:T(8,128)(2,1)S(1)}, u32[]{:S(2)}, u32[]{:S(2)}) %collective-permute-start.17) | collective-permute-done | bytes 327712 | tf_op jit(solution)/shard_map/input_grad/ppermute | solution.py:226
  156.2 6.6 %all-to-all-start.3 = ((bf16[8,40,1024]{2,1,0:T(8,128)(2,1)}), bf16[8,40,1024]{2,1,0:T(8,128)(2,1)S(1)}, u32[]{:S(2)}, u32[]{:S(2)}) async-start(bf16[8,40,1024]{2,1,0:T(8,128)(2,1)} %broadcast_in_dim.14), calls=%async_computation.3 | async-start | bytes 1310720 | tf_op jit(solution)/shard_map/weight_grad/all_to_all | solution.py:230
  162.8 1.3 collective-permute-start.18
  164.1 1.9 collective-permute-start.19
  166.1 1.9 collective-permute-start.20
  168.0 1.9 collective-permute-start.21
  171.2 6.3 %collective-permute-done.18 = bf16[128,1024]{1,0:T(8,128)(2,1)S(1)} collective-permute-done((bf16[128,1024]{1,0:T(8,128)(2,1)}, bf16[128,1024]{1,0:T(8,128)(2,1)S(1)}, u32[]{:S(2)}, u32[]{:S(2)}) %collective-permute-start.18) | collective-permute-done | bytes 262176 | tf_op jit(solution)/shard_map/key_grad/ppermute | solution.py:218
  177.5 5.6 %collective-permute-done.19 = bf16[128,1024]{1,0:T(8,128)(2,1)S(1)} collective-permute-done((bf16[128,1024]{1,0:T(8,128)(2,1)}, bf16[128,1024]{1,0:T(8,128)(2,1)S(1)}, u32[]{:S(2)}, u32[]{:S(2)}) %collective-permute-start.19) | collective-permute-done | bytes 262176 | tf_op jit(solution)/shard_map/key_grad/ppermute | solution.py:218
  183.1 5.5 %collective-permute-done.20 = bf16[128,1024]{1,0:T(8,128)(2,1)S(1)} collective-permute-done((bf16[128,1024]{1,0:T(8,128)(2,1)}, bf16[128,1024]{1,0:T(8,128)(2,1)S(1)}, u32[]{:S(2)}, u32[]{:S(2)}) %collective-permute-start.20) | collective-permute-done | bytes 262176 | tf_op jit(solution)/shard_map/key_grad/ppermute | solution.py:218
  188.6 6.9 %collective-permute-done.21 = bf16[128,1024]{1,0:T(8,128)(2,1)S(1)} collective-permute-done((bf16[128,1024]{1,0:T(8,128)(2,1)S(1)}, bf16[128,1024]{1,0:T(8,128)(2,1)S(1)}, u32[]{:S(2)}, u32[]{:S(2)}) %collective-permute-start.21) | collective-permute-done | bytes 262176 | tf_op jit(solution)/shard_map/key_grad/ppermute | solution.py:218
  196.4 1.2 bitcast_convert_fusion
  (74 shorter events, 13.7 us)
Async XLA Ops:
  3.1 4.3 %copy-start.3 = (bf16[320,1024]{1,0:T(8,128)(2,1)S(1)}, bf16[320,1024]{1,0:T(8,128)(2,1)}, u32[]{:S(2)}) copy-start(bf16[320,1024]{1,0:T(8,128)(2,1)} %param.7) | copy-start | bytes 1966084
  3.1 21.3 %all-to-all-start = ((bf16[128,4,1280]{0,2,1:T(8,128)(2,1)}), bf16[128,4,1280]{0,2,1:T(8,128)(2,1)S(1)}, u32[]{:S(2)}, u32[]{:S(2)}) async-start(bf16[128,4,1280]{0,2,1:T(8,128)(2,1)} %bitcast), calls=%async_computation | async-start | bytes 2621440 | tf_op jit(solution)/shard_map/hidden_columns/all_to_all | solution.py:260
  7.4 21.0 %collective-permute-start = (bf16[320,1024]{1,0:T(8,128)(2,1)S(1)}, bf16[320,1024]{1,0:T(8,128)(2,1)}, u32[]{:S(2)}, u32[]{:S(2)}) collective-permute-start(bf16[320,1024]{1,0:T(8,128)(2,1)S(1)} %copy-done.3), channel_id=1, source_target_pairs={{0,16},{16,0},{1,17},{17,1},{2,18},{18,2},{3,19},{19,3},{4,20},{20... | collective-permute-start | bytes 1966088 | tf_op jit(solution)/shard_map/weight_rows/ppermute | solution.py:222
  8.7 16.3 %collective-permute-start.1 = (bf16[128,1024]{1,0:T(8,128)(2,1)}, bf16[128,1024]{1,0:T(8,128)(2,1)S(1)}, u32[]{:S(2)}, u32[]{:S(2)}) collective-permute-start(bf16[128,1024]{1,0:T(8,128)(2,1)} %refs_8_.1), channel_id=1, source_target_pairs={{0,2},{1,3},{2,4},{3,5},{4,6},{5,7},{8,10},{9,11},{10,12},{11,13},... | collective-permute-start | bytes 786440 | tf_op jit(solution)/shard_map/keys/ppermute | solution.py:214
  11.8 16.1 %collective-permute-start.2 = (bf16[128,1024]{1,0:T(8,128)(2,1)}, bf16[128,1024]{1,0:T(8,128)(2,1)}, u32[]{:S(2)}, u32[]{:S(2)}) collective-permute-start(bf16[128,1024]{1,0:T(8,128)(2,1)} %refs_8_.1), channel_id=1, source_target_pairs={{0,1},{1,2},{2,3},{3,4},{4,5},{5,6},{6,7},{8,9},{9,10},{10,11},{11... | collective-permute-start | bytes 786440 | tf_op jit(solution)/shard_map/keys/ppermute | solution.py:214
  25.0 8.2 %copy-start.14 = (bf16[128,1024]{1,0:T(8,128)(2,1)}, bf16[128,1024]{1,0:T(8,128)(2,1)S(1)}, u32[]{:S(2)}) copy-start(bf16[128,1024]{1,0:T(8,128)(2,1)S(1)} %collective-permute-done.1.refs_3_.refs_6_) | copy-start | bytes 786436
  29.6 3.1 %copy-start.18 = (s32[1,8]{1,0:T(1,128)S(1)}, s32[1,8]{1,0:T(1,128)}, u32[]{:S(2)}) copy-start(s32[1,8]{1,0:T(1,128)} %param.11) | copy-start | bytes 100
  30.7 15.7 %collective-permute-start.3 = (bf16[2,320,1024]{2,1,0:T(8,128)(2,1)}, bf16[2,320,1024]{2,1,0:T(8,128)(2,1)}, u32[]{:S(2)}, u32[]{:S(2)}) collective-permute-start(bf16[2,320,1024]{2,1,0:T(8,128)(2,1)} %pad_maximum_fusion.1), channel_id=1, source_target_pairs={{0,8},{8,0},{1,9},{9,1},{2,10},{10,2},{3,11},{11,3},{4,12},{12,4},... | collective-permute-start | bytes 3932168 | tf_op jit(solution)/shard_map/weight_rows/ppermute | solution.py:222
  34.2 15.4 %collective-permute-start.4 = (bf16[2,128,1024]{2,1,0:T(8,128)(2,1)S(1)}, bf16[2,128,1024]{2,1,0:T(8,128)(2,1)S(1)}, u32[]{:S(2)}, u32[]{:S(2)}) collective-permute-start(bf16[2,128,1024]{2,1,0:T(8,128)(2,1)S(1)} %pad_maximum_fusion.4), channel_id=1, source_target_pairs={{0,2},{1,3},{2,4},{3,5},{4,6},{5,7},{8,10},{9,11},{10,12},{11,13},... | collective-permute-start | bytes 1572872 | tf_op jit(solution)/shard_map/keys/ppermute | solution.py:214
  48.2 3.9 %copy-start = (bf16[2,2,320,1024]{3,2,1,0:T(8,128)(2,1)}, bf16[2,2,320,1024]{3,2,1,0:T(8,128)(2,1)S(1)}, u32[]{:S(2)}) copy-start(bf16[2,2,320,1024]{3,2,1,0:T(8,128)(2,1)S(1)} %pad_maximum_fusion) | copy-start | bytes 7864324
  49.6 2.5 %copy-start.4 = (bf16[2,128,1024]{2,1,0:T(8,128)(2,1)}, bf16[2,128,1024]{2,1,0:T(8,128)(2,1)S(1)}, u32[]{:S(2)}) copy-start(bf16[2,128,1024]{2,1,0:T(8,128)(2,1)S(1)} %collective-permute-done.4.refs_5_) | copy-start | bytes 1572868
  52.1 18.3 %all-to-all-start.1 = ((bf16[4,128,1024]{2,1,0:T(8,128)(2,1)}), bf16[4,128,1024]{2,1,0:T(8,128)(2,1)S(1)}, u32[]{:S(2)}, u32[]{:S(2)}) async-start(bf16[4,128,1024]{2,1,0:T(8,128)(2,1)} %bitcast.12), calls=%async_computation.1 | async-start | bytes 2097152 | tf_op jit(solution)/shard_map/values/all_to_all | solution.py:274
  67.6 18.4 %collective-permute-start.5 = (bf16[2,128,1024]{2,1,0:T(8,128)(2,1)}, bf16[2,128,1024]{2,1,0:T(8,128)(2,1)S(1)}, u32[]{:S(2)}, u32[]{:S(2)}) collective-permute-start(bf16[2,128,1024]{2,1,0:T(8,128)(2,1)} %get-tuple-element.73), channel_id=1, source_target_pairs={{2,0},{3,1},{4,2},{5,3},{6,4},{7,5},{10,8},{11,9},{12,10},{13,11},... | collective-permute-start | bytes 1572872 | tf_op jit(solution)/shard_map/value_grad/ppermute | solution.py:218
  70.6 17.4 %copy-start.13 = (bf16[128,1024]{1,0:T(8,128)(2,1)}, bf16[128,1024]{1,0:T(8,128)(2,1)S(1)}, u32[]{:S(2)}) copy-start(bf16[128,1024]{1,0:T(8,128)(2,1)S(1)} %reduce_sum.24.refs_12_) | copy-start | bytes 786436
  70.6 7.7 %collective-permute-start.8 = (bf16[128,1024]{1,0:T(8,128)(2,1)S(1)}, bf16[128,1024]{1,0:T(8,128)(2,1)S(1)}, u32[]{:S(2)}, u32[]{:S(2)}) collective-permute-start(bf16[128,1024]{1,0:T(8,128)(2,1)S(1)} %reduce_sum.24.refs_12_), channel_id=1, source_target_pairs={{0,2},{1,3},{2,4},{3,5},{4,6},{5,7},{8,10},{9,11},{10,12},{11,13},... | collective-permute-start | bytes 786440 | tf_op jit(solution)/shard_map/values_forward/ppermute | solution.py:214
  73.8 9.2 %collective-permute-start.9 = (bf16[128,1024]{1,0:T(8,128)(2,1)S(1)}, bf16[128,1024]{1,0:T(8,128)(2,1)S(1)}, u32[]{:S(2)}, u32[]{:S(2)}) collective-permute-start(bf16[128,1024]{1,0:T(8,128)(2,1)S(1)} %reduce_sum.24.refs_12_), channel_id=1, source_target_pairs={{0,1},{1,2},{2,3},{3,4},{4,5},{5,6},{6,7},{8,9},{9,10},{10,11},{11... | collective-permute-start | bytes 786440 | tf_op jit(solution)/shard_map/values_forward/ppermute | solution.py:214
  78.3 9.7 %copy-start.15 = (bf16[128,1024]{1,0:T(8,128)(2,1)}, bf16[128,1024]{1,0:T(8,128)(2,1)S(1)}, u32[]{:S(2)}) copy-start(bf16[128,1024]{1,0:T(8,128)(2,1)S(1)} %collective-permute-done.8.refs_10_) | copy-start | bytes 786436
  83.0 3.0 %copy-start.16 = (bf16[128,1024]{1,0:T(8,128)(2,1)}, bf16[128,1024]{1,0:T(8,128)(2,1)S(1)}, u32[]{:S(2)}) copy-start(bf16[128,1024]{1,0:T(8,128)(2,1)S(1)} %collective-permute-done.9.refs_11_) | copy-start | bytes 786436
  83.0 20.8 %copy-start.6 = (f32[128,1024]{1,0:T(8,128)S(1)}, f32[128,1024]{1,0:T(8,128)}, u32[]{:S(2)}) copy-start(f32[128,1024]{1,0:T(8,128)} %get-tuple-element.76) | copy-start | bytes 1572868
  83.0 20.7 %collective-permute-start.10 = (bf16[2,128,1024]{2,1,0:T(8,128)(2,1)S(1)}, bf16[2,128,1024]{2,1,0:T(8,128)(2,1)}, u32[]{:S(2)}, u32[]{:S(2)}) collective-permute-start(bf16[2,128,1024]{2,1,0:T(8,128)(2,1)S(1)} %pad_maximum_fusion.5), channel_id=1, source_target_pairs={{0,2},{1,3},{2,4},{3,5},{4,6},{5,7},{8,10},{9,11},{10,12},{11,13},... | collective-permute-start | bytes 1572872 | tf_op jit(solution)/shard_map/values_forward/ppermute | solution.py:214
  88.0 8.9 %collective-permute-start.6 = (bf16[128,1024]{1,0:T(8,128)(2,1)}, bf16[128,1024]{1,0:T(8,128)(2,1)S(1)}, u32[]{:S(2)}, u32[]{:S(2)}) collective-permute-start(bf16[128,1024]{1,0:T(8,128)(2,1)} %get-tuple-element.122), channel_id=1, source_target_pairs={{2,0},{3,1},{4,2},{5,3},{6,4},{7,5},{10,8},{11,9},{12,10},{13,11},... | collective-permute-start | bytes 786440 | tf_op jit(solution)/shard_map/value_grad/ppermute | solution.py:218
  91.3 12.5 %collective-permute-start.7 = (bf16[128,1024]{1,0:T(8,128)(2,1)}, bf16[128,1024]{1,0:T(8,128)(2,1)S(1)}, u32[]{:S(2)}, u32[]{:S(2)}) collective-permute-start(bf16[128,1024]{1,0:T(8,128)(2,1)} %get-tuple-element.121), channel_id=1, source_target_pairs={{1,0},{2,1},{3,2},{4,3},{5,4},{6,5},{7,6},{9,8},{10,9},{11,10},{12... | collective-permute-start | bytes 786440 | tf_op jit(solution)/shard_map/value_grad/ppermute | solution.py:218
  103.9 6.5 %collective-permute-start.11 = (bf16[128,1024]{1,0:T(8,128)(2,1)S(1)}, bf16[128,1024]{1,0:T(8,128)(2,1)S(1)}, u32[]{:S(2)}, u32[]{:S(2)}) collective-permute-start(bf16[128,1024]{1,0:T(8,128)(2,1)S(1)} %add_convert_fusion.2), channel_id=1, source_target_pairs={{0,32},{32,64},{64,96},{96,0},{1,33},{33,65},{65,97},{97,1},{2,34}... | collective-permute-start | bytes 786440 | tf_op jit(solution)/shard_map/value_grad/ppermute | solution.py:226
  105.4 10.0 %collective-permute-start.12 = (bf16[128,1024]{1,0:T(8,128)(2,1)S(1)}, bf16[128,1024]{1,0:T(8,128)(2,1)S(1)}, u32[]{:S(2)}, u32[]{:S(2)}) collective-permute-start(bf16[128,1024]{1,0:T(8,128)(2,1)S(1)} %add_convert_fusion.2), channel_id=1, source_target_pairs={{0,64},{32,96},{64,0},{96,32},{1,65},{33,97},{65,1},{97,33},{2,66}... | collective-permute-start | bytes 786440 | tf_op jit(solution)/shard_map/value_grad/ppermute | solution.py:226
  107.8 7.6 %collective-permute-start.13 = (bf16[128,1024]{1,0:T(8,128)(2,1)S(1)}, bf16[128,1024]{1,0:T(8,128)(2,1)S(1)}, u32[]{:S(2)}, u32[]{:S(2)}) collective-permute-start(bf16[128,1024]{1,0:T(8,128)(2,1)S(1)} %add_convert_fusion.2), channel_id=1, source_target_pairs={{0,96},{32,0},{64,32},{96,64},{1,97},{33,1},{65,33},{97,65},{2,98}... | collective-permute-start | bytes 786440 | tf_op jit(solution)/shard_map/value_grad/ppermute | solution.py:226
  117.2 5.6 %copy-start.1 = (bf16[2,2,320,1024]{3,2,1,0:T(8,128)(2,1)S(1)}, bf16[2,2,320,1024]{3,2,1,0:T(8,128)(2,1)}, u32[]{:S(2)}) copy-start(bf16[2,2,320,1024]{3,2,1,0:T(8,128)(2,1)} %copy-done) | copy-start | bytes 7864324
  117.4 8.2 %collective-permute-start.14 = (bf16[640,1024]{1,0:T(8,128)(2,1)S(1)}, bf16[640,1024]{1,0:T(8,128)(2,1)S(1)}, u32[]{:S(2)}, u32[]{:S(2)}) collective-permute-start(bf16[640,1024]{1,0:T(8,128)(2,1)S(1)} %pad_maximum_fusion.2), channel_id=1, source_target_pairs={{0,8},{8,0},{1,9},{9,1},{2,10},{10,2},{3,11},{11,3},{4,12},{12,4},... | collective-permute-start | bytes 3932168 | tf_op jit(solution)/shard_map/weight_grad/ppermute | solution.py:222
  127.2 25.3 %all-to-all-start.2 = ((bf16[16,40,1024]{2,1,0:T(8,128)(2,1)}), bf16[16,40,1024]{2,1,0:T(8,128)(2,1)S(1)}, u32[]{:S(2)}, u32[]{:S(2)}) async-start(bf16[16,40,1024]{2,1,0:T(8,128)(2,1)} %bitcast.19), calls=%async_computation.2 | async-start | bytes 2621440 | tf_op jit(solution)/shard_map/weight_grad/all_to_all | solution.py:303
  135.0 17.8 %collective-permute-start.15 = (bf16[128,1280]{1,0:T(8,128)(2,1)}, bf16[128,1280]{1,0:T(8,128)(2,1)S(1)}, u32[]{:S(2)}, u32[]{:S(2)}) collective-permute-start(bf16[128,1280]{1,0:T(8,128)(2,1)} %get-tuple-element.113), channel_id=1, source_target_pairs={{0,96},{32,0},{64,32},{96,64},{1,97},{33,1},{65,33},{97,65},{2,98}... | collective-permute-start | bytes 983048 | tf_op jit(solution)/shard_map/input_grad/ppermute | solution.py:226
  136.9 15.9 %collective-permute-start.16 = (bf16[128,1280]{1,0:T(8,128)(2,1)}, bf16[128,1280]{1,0:T(8,128)(2,1)S(1)}, u32[]{:S(2)}, u32[]{:S(2)}) collective-permute-start(bf16[128,1280]{1,0:T(8,128)(2,1)} %get-tuple-element.112), channel_id=1, source_target_pairs={{0,64},{32,96},{64,0},{96,32},{1,65},{33,97},{65,1},{97,33},{2,66}... | collective-permute-start | bytes 983048 | tf_op jit(solution)/shard_map/input_grad/ppermute | solution.py:226
  137.7 17.5 %collective-permute-start.17 = (bf16[128,1280]{1,0:T(8,128)(2,1)S(1)}, bf16[128,1280]{1,0:T(8,128)(2,1)S(1)}, u32[]{:S(2)}, u32[]{:S(2)}) collective-permute-start(bf16[128,1280]{1,0:T(8,128)(2,1)S(1)} %get-tuple-element.111), channel_id=1, source_target_pairs={{0,32},{32,64},{64,96},{96,0},{1,33},{33,65},{65,97},{97,1},{2,34}... | collective-permute-start | bytes 983048 | tf_op jit(solution)/shard_map/input_grad/ppermute | solution.py:226
  152.8 15.2 %copy-start.17 = (bf16[128,1024]{1,0:T(8,128)(2,1)S(1)}, bf16[128,1024]{1,0:T(8,128)(2,1)}, u32[]{:S(2)}) copy-start(bf16[128,1024]{1,0:T(8,128)(2,1)} %get-tuple-element.98) | copy-start | bytes 786436
  152.8 15.2 %copy-start.7 = (bf16[128,1280]{1,0:T(8,128)(2,1)}, bf16[128,1280]{1,0:T(8,128)(2,1)S(1)}, u32[]{:S(2)}) copy-start(bf16[128,1280]{1,0:T(8,128)(2,1)S(1)} %collective-permute-done.15) | copy-start | bytes 983044
  152.8 15.2 %copy-start.9 = (bf16[128,1280]{1,0:T(8,128)(2,1)}, bf16[128,1280]{1,0:T(8,128)(2,1)S(1)}, u32[]{:S(2)}) copy-start(bf16[128,1280]{1,0:T(8,128)(2,1)S(1)} %collective-permute-done.16) | copy-start | bytes 983044
  155.3 12.8 %copy-start.11 = (bf16[128,1280]{1,0:T(8,128)(2,1)}, bf16[128,1280]{1,0:T(8,128)(2,1)S(1)}, u32[]{:S(2)}) copy-start(bf16[128,1280]{1,0:T(8,128)(2,1)S(1)} %collective-permute-done.17) | copy-start | bytes 983044
  156.2 40.2 %all-to-all-start.3 = ((bf16[8,40,1024]{2,1,0:T(8,128)(2,1)}), bf16[8,40,1024]{2,1,0:T(8,128)(2,1)S(1)}, u32[]{:S(2)}, u32[]{:S(2)}) async-start(bf16[8,40,1024]{2,1,0:T(8,128)(2,1)} %broadcast_in_dim.14), calls=%async_computation.3 | async-start | bytes 1310720 | tf_op jit(solution)/shard_map/weight_grad/all_to_all | solution.py:230
  162.8 14.7 %collective-permute-start.18 = (bf16[128,1024]{1,0:T(8,128)(2,1)}, bf16[128,1024]{1,0:T(8,128)(2,1)S(1)}, u32[]{:S(2)}, u32[]{:S(2)}) collective-permute-start(bf16[128,1024]{1,0:T(8,128)(2,1)} %get-tuple-element.95), channel_id=1, source_target_pairs={{4,0},{5,1},{6,2},{7,3},{12,8},{13,9},{14,10},{15,11},{20,16},{21,... | collective-permute-start | bytes 786440 | tf_op jit(solution)/shard_map/key_grad/ppermute | solution.py:218
  164.1 19.0 %collective-permute-start.19 = (bf16[128,1024]{1,0:T(8,128)(2,1)}, bf16[128,1024]{1,0:T(8,128)(2,1)S(1)}, u32[]{:S(2)}, u32[]{:S(2)}) collective-permute-start(bf16[128,1024]{1,0:T(8,128)(2,1)} %get-tuple-element.96), channel_id=1, source_target_pairs={{3,0},{4,1},{5,2},{6,3},{7,4},{11,8},{12,9},{13,10},{14,11},{15,12... | collective-permute-start | bytes 786440 | tf_op jit(solution)/shard_map/key_grad/ppermute | solution.py:218
  166.1 22.6 %collective-permute-start.20 = (bf16[128,1024]{1,0:T(8,128)(2,1)}, bf16[128,1024]{1,0:T(8,128)(2,1)S(1)}, u32[]{:S(2)}, u32[]{:S(2)}) collective-permute-start(bf16[128,1024]{1,0:T(8,128)(2,1)} %get-tuple-element.97), channel_id=1, source_target_pairs={{2,0},{3,1},{4,2},{5,3},{6,4},{7,5},{10,8},{11,9},{12,10},{13,11},... | collective-permute-start | bytes 786440 | tf_op jit(solution)/shard_map/key_grad/ppermute | solution.py:218
  168.0 27.4 %collective-permute-start.21 = (bf16[128,1024]{1,0:T(8,128)(2,1)S(1)}, bf16[128,1024]{1,0:T(8,128)(2,1)S(1)}, u32[]{:S(2)}, u32[]{:S(2)}) collective-permute-start(bf16[128,1024]{1,0:T(8,128)(2,1)S(1)} %copy-done.17), channel_id=1, source_target_pairs={{1,0},{2,1},{3,2},{4,3},{5,4},{6,5},{7,6},{9,8},{10,9},{11,10},{12... | collective-permute-start | bytes 786440 | tf_op jit(solution)/shard_map/key_grad/ppermute | solution.py:218
  170.0 1.0 copy-start.8
  170.0 1.1 copy-start.10
  170.1 1.1 copy-start.12
  170.1 25.4 %copy-start.5 = (f32[128,1024]{1,0:T(8,128)S(1)}, f32[128,1024]{1,0:T(8,128)}, u32[]{:S(2)}) copy-start(f32[128,1024]{1,0:T(8,128)} %get-tuple-element.99) | copy-start | bytes 1572868
  171.2 26.4 %copy-start.2 = (bf16[128,5120]{1,0:T(8,128)(2,1)}, bf16[128,5120]{1,0:T(8,128)(2,1)S(1)}, u32[]{:S(2)}) copy-start(bf16[128,5120]{1,0:T(8,128)(2,1)S(1)} %constant_dynamic-update-slice_fusion) | copy-start | bytes 3932164

commit v4 on v3

v4 whole, which is shorter than its diff:
```python
import functools
import math

import jax
import jax.numpy as jnp
from jax import lax
from jax.experimental import pallas as pl
from jax.experimental.pallas import tpu as pltpu
from jax.sharding import PartitionSpec as P

HD = 128
KV = 8
G = 8
CH = 5
N = 8
SC = HD**-0.5
L2 = SC * math.log2(math.e)
bf = jnp.bfloat16
f32 = jnp.float32
VL = 56 * 1024 * 1024
W = 8
FAR = 2
RB = 128
WP = 4


def probs_kernel(meta, q, do, k01, k2, k3, k4, e_out, qt_out, dt_out, li_out, v01, v2, v3, v4, bias):
    rows = q.shape[0]
    ks = (k01.at[0], k01.at[1], k2, k3, k4)

    @pl.when(pl.program_id(0) == 0)
    def _():
        s = meta[KV]
        r = lax.broadcasted_iota(jnp.int32, (1, rows), 1)
        pos = r + s * rows
        start = jnp.zeros((1, rows), jnp.int32)
        total = meta[0]
        for d in range(1, KV):
            start = jnp.where(pos >= total, total, start)
            total = total + meta[d]
        low = start - (s - (CH - 1)) * rows
        j = lax.broadcasted_iota(jnp.int32, (CH * rows, rows), 0)
        bias[...] = jnp.where((j >= low) & (j <= r + (CH - 1) * rows), 0.0, -1e30)

    n = WP * rows
    for p in range(G // WP):
        cols = slice(p * n, (p + 1) * n)
        for h in range(p * WP, (p + 1) * WP):
            qt_out[0, :, h * rows : (h + 1) * rows] = q[:, h * HD : (h + 1) * HD].T
        qt = qt_out[0, :, cols]
        ts = []
        for c, k in enumerate(ks):
            b = jnp.concatenate([bias[c * rows : (c + 1) * rows, :]] * WP, axis=1)
            ts.append(jnp.dot(k[...], qt, preferred_element_type=f32) * L2 + b)
        m = functools.reduce(jnp.maximum, [jnp.max(t, axis=0, keepdims=True) for t in ts])
        l = jnp.zeros_like(m)
        for c, t in enumerate(ts):
            e = jnp.exp2(t - m)
            l = l + jnp.sum(e, axis=0, keepdims=True)
            e_out[0, c * rows : (c + 1) * rows, cols] = e.astype(bf)
        li = 1.0 / l
        li_out[0, 0:1, cols] = li
        dt = jnp.concatenate([do[:, h * HD : (h + 1) * HD].T for h in range(p * WP, (p + 1) * WP)], axis=1)
        dt_out[0, :, cols] = (dt.astype(f32) * li).astype(bf)
    dall = dt_out[0]
    nt = (((1,), (1,)), ((), ()))
    for c, v in enumerate((v01.at[0], v01.at[1], v2, v3, v4)):
        e = e_out[0, c * rows : (c + 1) * rows, :]
        v[...] = lax.dot_general(e, dall, nt, preferred_element_type=f32).astype(v.dtype)


def grads_kernel(qt, dt, e, li, k01, k2, k3, k4, v01, v2, v3, v4, out, dq, g0, g1, g2, g3, g4, ds):
    rows = out.shape[0]
    ks = (k01.at[0], k01.at[1], k2, k3, k4)
    vs = (v01.at[0], v01.at[1], v2, v3, v4)
    n = W * rows
    kt = jnp.concatenate([k[...].T for k in ks], axis=1)
    vt = jnp.concatenate([v[...].T for v in vs], axis=1)
    for p in range(G // W):
        cols = slice(p * n, (p + 1) * n)
        o = jnp.dot(vt, e[0, :, cols], preferred_element_type=f32) * li[0, 0:1, cols]
        ob = o.astype(bf)
        d = dt[0, :, cols]
        delta = jnp.sum(d.astype(f32) * o, axis=0, keepdims=True)
        for c in range(CH):
            part = slice(c * rows, (c + 1) * rows)
            dp = jnp.dot(vs[c][...], d, preferred_element_type=f32)
            ds[part, cols] = (e[0, part, cols].astype(f32) * (dp - delta)).astype(bf)
        dqt = (jnp.dot(kt, ds[:, cols], preferred_element_type=f32) * SC).astype(bf)
        for w in range(W):
            h = p * W + w
            out[:, h * HD : (h + 1) * HD] = ob[:, w * rows : (w + 1) * rows].T
            dq[:, h * HD : (h + 1) * HD] = dqt[:, w * rows : (w + 1) * rows].T
    nt = (((1,), (1,)), ((), ()))
    for c, g in enumerate((g0, g1, g2, g3, g4)):
        dk = lax.dot_general(ds[c * rows : (c + 1) * rows, :], qt[0], nt, preferred_element_type=f32)
        g[...] = (dk * SC).astype(g.dtype)


def view(ref, kind, h):
    if kind == "m":
        return ref
    if kind == "p":
        return ref.at[:, :, pl.ds(h * HD, HD)]
    if kind in ("n", "o"):
        return ref.at[:, pl.ds(h * HD, HD)]
    if kind == "b":
        return ref.at[:, pl.ds(h * G * HD, G * HD)]
    return ref.at[pl.ds(h, 1)]


def call(kernel, args, ins, outs, scratch, products, exps, hp):
    rows = RB
    wide = G * rows
    kinds = ins + outs
    dtypes = {"e": ((KV, CH * rows, wide), bf), "t": ((KV, HD, wide), bf)}
    dtypes |= {"s": ((KV, 8, wide), f32), "b": ((rows, KV * G * HD), bf), "n": ((rows, KV * HD), bf)}
    dtypes |= {"o": ((rows, KV * HD), f32), "p": ((FAR, rows, KV * HD), bf)}

    def spec(kind):
        if kind == "m":
            return pl.BlockSpec(memory_space=pltpu.SMEM)
        if kind == "p":
            return pl.BlockSpec((FAR, rows, hp * HD), lambda j: (0, 0, j))
        if kind in ("n", "o"):
            return pl.BlockSpec((rows, hp * HD), lambda j: (0, j))
        if kind == "b":
            return pl.BlockSpec((rows, hp * G * HD), lambda j: (0, j))
        return pl.BlockSpec((hp,) + dtypes[kind][0][1:], lambda j: (j, 0, 0))

    def heads(*refs):
        for h in range(hp):
            kernel(*[view(r, k, h) for r, k in zip(refs, kinds)], *refs[len(kinds) :])

    return pl.pallas_call(
        heads,
        grid=(KV // hp,),
        in_specs=[spec(k) for k in ins],
        out_specs=[spec(k) for k in outs],
        out_shape=[jax.ShapeDtypeStruct(*dtypes[k]) for k in outs],
        scratch_shapes=scratch,
        compiler_params=pltpu.CompilerParams(vmem_limit_bytes=VL),
        cost_estimate=pl.CostEstimate(
            flops=products * 2 * KV * rows * wide * HD, bytes_accessed=16 << 20, transcendentals=exps * KV * rows * wide
        ),
    )(*args)


def probs_call(meta, q, do, ks):
    scratch = [pltpu.VMEM((CH * RB, RB), f32)]
    ins = ["m", "b", "b", "p", "n", "n", "n"]
    outs = ["e", "t", "t", "s", "p", "n", "n", "o"]
    return call(probs_kernel, (meta, q, do, *ks), ins, outs, scratch, 2 * CH, CH, 1)


def grads_call(qt, dt, e, li, ks, vs):
    scratch = [pltpu.VMEM((CH * RB, G * RB), bf)]
    ins = ["t", "t", "e", "s"] + ["p", "n", "n", "n"] * 2
    outs = ["b", "b"] + ["n"] * (CH - 1) + ["o"]
    return call(grads_kernel, (qt, dt, e, li, *ks, *vs), ins, outs, scratch, 4 * CH, 0, 2)


def forward(x, k):
    return lax.ppermute(x, ("x", "zh"), [(i, i + k) for i in range(N - k)])


def backward(x, k):
    return lax.ppermute(x, ("x", "zh"), [(i + k, i) for i in range(N - k)])


def flip(x, axis):
    return lax.ppermute(x, axis, [(0, 1), (1, 0)])


def along_y(x, k):
    return lax.ppermute(x, "y", [(i, (i + k) % 4) for i in range(4)])


def over_seq(x):
    return lax.all_to_all(x, ("x", "zh"), 0, 0, tiled=True)


def ordered(own, other, index, axis):
    first = index == 0
    return jnp.stack([jnp.where(first, own, other), jnp.where(first, other, own)], axis=axis)


def relay_sum(parts, got):
    _, two, one, own = parts
    two = (two.astype(f32) + got[0].astype(f32)).astype(bf)
    one = (one.astype(f32) + got[1].astype(f32)).astype(bf)
    return own, backward(two, 2), backward(one, 1)


def turned(x, start, rows):
    n = x.shape[0] // rows
    return jnp.concatenate([lax.dynamic_slice_in_dim(x, (start - k) % n * rows, rows) for k in range(n)])


def body(hidden, weight, query, key, cot, lengths):
    rows = hidden.shape[0]
    high, width = weight.shape
    y, zl, core = (lax.axis_index(n) for n in ("y", "zl", "core"))
    seq = lax.axis_index(("x", "zh"))
    depth = hidden.shape[1] // 4
    meta = jnp.concatenate([lengths[0], seq.astype(jnp.int32)[None]])
    with jax.named_scope("keys"):
        k2, k3 = forward(key, 2), forward(key, 1)
    with jax.named_scope("hidden_columns"):
        hid = lax.all_to_all(hidden.reshape(rows, 4, depth), "y", 1, 0, tiled=True).reshape(4 * rows, depth)
    with jax.named_scope("weight_rows"):
        wz = flip(weight, "zl")
        wz, k2, k3, hid = lax.optimization_barrier((wz, k2, k3, hid))
        wz = ordered(weight, wz, zl, 0)
        wu = ordered(wz, flip(wz, "core"), core, 1).reshape(depth, width)
    with jax.named_scope("keys"):
        k01 = forward(jnp.stack([k2, k3]), 2)
    with jax.named_scope("values"):
        part = jnp.dot(hid, wu, preferred_element_type=f32).astype(bf).reshape(4, rows, width)
        part, k2 = lax.optimization_barrier((part, k2))
        part = lax.all_to_all(part, "y", 0, 0, tiled=True)
        values = jnp.sum(part.astype(f32), axis=0).astype(bf)
    with jax.named_scope("probs"):
        e, qt, dt, li, *dv = probs_call(meta, query, cot, (k01, k2, k3, key))
    with jax.named_scope("values_forward"):
        v2, v3 = forward(values, 2), forward(values, 1)
        v01 = forward(jnp.stack([v2, v3]), 2)
    with jax.named_scope("value_grad"):
        dv = relay_sum(dv, backward(dv[0], 2))
        dv, v01, v2, v3 = lax.optimization_barrier((dv, v01, v2, v3))
        vgrad = sum(d.astype(f32) for d in dv).astype(bf)
        vys = [vgrad] + [along_y(vgrad, k) for k in (1, 2, 3)]
        vy = jnp.concatenate(vys)
        vs = (v01, v2, v3, values)
    with jax.named_scope("weight_grad"):
        turned_hid = turned(hid, y, rows)
        g = lax.dot_general(turned_hid, vy, (((0,), (0,)), ((), ())), preferred_element_type=f32).astype(bf)

        def half(c):
            return jnp.concatenate([lax.dynamic_slice_in_dim(g, (2 * i + c) * high, high) for i in range(2)])

        g = half(core).astype(f32) + flip(half(1 - core), "core").astype(f32)
        g = g.astype(bf).reshape(2 * N, high // N, width)
    with jax.named_scope("input_grad"):
        ig = lax.dot_general(vy, wu, (((1,), (1,)), ((), ())), preferred_element_type=f32).astype(bf)
        g, ig, vs = lax.optimization_barrier((g, ig, vs))
        igs = [ig[k * rows : (k + 1) * rows] for k in range(4)]
        igs = [igs[0]] + [along_y(igs[k], 4 - k) for k in (1, 2, 3)]
    with jax.named_scope("weight_grad"):
        g = lax.all_to_all(g, ("zl", "x", "zh"), 0, 0, tiled=True)
        g = jnp.sum(g.astype(f32), axis=0).astype(bf)
    with jax.named_scope("grads"):
        out, dq, *dk = grads_call(qt, dt, e, li, (k01, k2, k3, key), vs)
        g, dk, igs = lax.optimization_barrier((g, dk, igs))
    with jax.named_scope("key_grad"):
        dk = [backward(dk[c], CH - 1 - c) for c in range(CH - 1)] + [dk[-1]]
        kgrad = sum(d.astype(f32) for d in dk).astype(bf)
    with jax.named_scope("weight_grad"):
        g = jnp.broadcast_to(g[None], (N,) + g.shape)
        wgrad = over_seq(g).reshape(weight.shape).astype(f32)
    with jax.named_scope("input_grad"):
        input_grad = jnp.zeros(hidden.shape, bf)
        for k in range(4):
            input_grad = lax.dynamic_update_slice_in_dim(input_grad, igs[k], (y + k) % 4 * depth, axis=1)
    return out, dq, kgrad, input_grad, wgrad


def solution(mesh):
    fine = jax.sharding.Mesh(mesh.devices.reshape(4, 2, 2, 4, 2), ("y", "zl", "core", "x", "zh"))
    tok = P(("y", "zl", "core", "x", "zh"), None)
    own = P(("y", "zl", "core"), None)
    return jax.shard_map(
        body,
        mesh=fine,
        in_specs=(tok, own, tok, tok, tok, own),
        out_specs=(tok, tok, tok, tok, own),
        check_vma=False,
    )
```

time: 199 us -> 197 us (0.990)
  Pallas kernels: 34.6 us -> 28.5 us
  waiting for transfers between devices: 64.2 us -> 68.9 us
    pallas_call x3 -> x2, Pallas kernels: 34.6 us -> 28.5 us  [call(): pl.pallas_call(heads, grid=(KV // hp,), in_specs=[spec(k) for k in ins],...]
    ppermute x6, waiting for transfers between devices: 11.6 us -> 14.2 us  [forward(): return lax.ppermute(x, ('x', 'zh'), [(i, i + k) for i in range(N - k)])]
  transfers between devices with their start and end apart: 26 -> 26, of which waited for: 16 -> 16; matrix products, arithmetic and copies ran while one was open for 5% -> 7% of each run, Pallas kernels for 18% -> 15%
where the time goes in v4:
time: 197 us; the launch traced here: 196 us
  starting transfers between devices  72.8 us (37%)
  waiting for transfers between devices  68.9 us (35%)
  Pallas kernels  28.5 us (14%)
  other arithmetic  12.2 us (6%)
  local copies, waits for them, and re-layouts  6.46 us (3%)
  matrix products  5.64 us (3%)
    ppermute x7, waiting for transfers between devices, backward(): return lax.ppermute(x, ('x', 'zh'), [(i + k, i) for i in range(N - k)])  32.2 us
    pallas_call x2, Pallas kernels, call(): pl.pallas_call(heads, grid=(KV // hp,), in_specs=[spec(k) for k in ins],...  28.5 us
    ppermute x7, starting transfers between devices, backward(): return lax.ppermute(x, ('x', 'zh'), [(i + k, i) for i in range(N - k)])  17.5 us
    ppermute x6, starting transfers between devices, forward(): return lax.ppermute(x, ('x', 'zh'), [(i, i + k) for i in range(N - k)])  17 us
    ppermute x6, waiting for transfers between devices, forward(): return lax.ppermute(x, ('x', 'zh'), [(i, i + k) for i in range(N - k)])  14.2 us
    ppermute x6, waiting for transfers between devices, along_y(): return lax.ppermute(x, 'y', [(i, (i + k) % 4) for i in range(4)])  10.5 us
    all_to_all x1, waiting for transfers between devices, body(): lax.all_to_all(hidden.reshape(rows, 4, depth), 'y', 1, 0, tiled=True)  10.3 us
    ppermute x6, starting transfers between devices, along_y(): return lax.ppermute(x, 'y', [(i, (i + k) % 4) for i in range(4)])  8.39 us
  transfers between devices with their start and end apart: 26, of which 16 were waited for; matrix products, arithmetic and copies ran while one was open for 7% of the time, Pallas kernels for 15%

profile of v4, /device:TPU:67, one launch (start us, length us, event | category | flops | bytes accessed | tf_op | source)
XLA Modules:
  0.0 195.7 jit_solution(10548968830406107216)
XLA Ops:
  0.6 2.4 %copy.12 = bf16[128,5120]{0,1:T(8,128)(2,1)} copy(bf16[128,5120]{1,0:T(8,128)(2,1)} %param.6) | data formatting | bytes 2621440 | tf_op args[0]
  3.1 4.3 %all-to-all-start = ((bf16[128,4,1280]{0,2,1:T(8,128)(2,1)}), bf16[128,4,1280]{0,2,1:T(8,128)(2,1)S(1)}, u32[]{:S(2)}, u32[]{:S(2)}) async-start(bf16[128,4,1280]{0,2,1:T(8,128)(2,1)} %bitcast.2), calls=%async_computation | async-start | bytes 2621440 | tf_op jit(solution)/shard_map/hidden_columns/all_to_all | solution.py:210
  7.4 1.3 collective-permute-start
  8.7 3.1 %collective-permute-start.1 = (bf16[128,1024]{1,0:T(8,128)(2,1)}, bf16[128,1024]{1,0:T(8,128)(2,1)S(1)}, u32[]{:S(2)}, u32[]{:S(2)}) collective-permute-start(bf16[128,1024]{1,0:T(8,128)(2,1)} %refs_7_.1), channel_id=1, source_target_pairs={{0,2},{1,3},{2,4},{3,5},{4,6},{5,7},{8,10},{9,11},{10,12},{11,13},... | collective-permute-start | bytes 786440 | tf_op jit(solution)/shard_map/keys/ppermute | solution.py:164
  11.8 2.2 %collective-permute-start.2 = (bf16[128,1024]{1,0:T(8,128)(2,1)}, bf16[128,1024]{1,0:T(8,128)(2,1)}, u32[]{:S(2)}, u32[]{:S(2)}) collective-permute-start(bf16[128,1024]{1,0:T(8,128)(2,1)} %refs_7_.1), channel_id=1, source_target_pairs={{0,1},{1,2},{2,3},{3,4},{4,5},{5,6},{6,7},{8,9},{9,10},{10,11},{11... | collective-permute-start | bytes 786440 | tf_op jit(solution)/shard_map/keys/ppermute | solution.py:164
  14.1 10.3 %all-to-all-done = bf16[128,4,1280]{0,2,1:T(8,128)(2,1)S(1)} async-done(((bf16[128,4,1280]{0,2,1:T(8,128)(2,1)}), bf16[128,4,1280]{0,2,1:T(8,128)(2,1)S(1)}, u32[]{:S(2)}, u32[]{:S(2)}) %all-to-all-start) | async-done | bytes 1310752 | tf_op jit(solution)/shard_map/hidden_columns/all_to_all | solution.py:210
  25.0 2.9 %collective-permute-done.2.refs_5_.refs_6_ = bf16[128,1024]{1,0:T(8,128)(2,1)} collective-permute-done((bf16[128,1024]{1,0:T(8,128)(2,1)}, bf16[128,1024]{1,0:T(8,128)(2,1)}, u32[]{:S(2)}, u32[]{:S(2)}) %collective-permute-start.2) | collective-permute-done | bytes 262176 | tf_op jit(solution)/shard_map/keys/ppermute | solution.py:164
  28.4 1.2 select_bitcast_fusion.3
  29.6 1.2 pad_maximum_fusion.1
  30.7 1.9 collective-permute-start.4
  33.6 3.1 %collective-permute-start.3 = (bf16[2,128,1024]{2,1,0:T(8,128)(2,1)S(1)}, bf16[2,128,1024]{2,1,0:T(8,128)(2,1)}, u32[]{:S(2)}, u32[]{:S(2)}) collective-permute-start(bf16[2,128,1024]{2,1,0:T(8,128)(2,1)S(1)} %pad_maximum_fusion.4), channel_id=1, source_target_pairs={{0,2},{1,3},{2,4},{3,5},{4,6},{5,7},{8,10},{9,11},{10,12},{11,13},... | collective-permute-start | bytes 1572872 | tf_op jit(solution)/shard_map/keys/ppermute | solution.py:164
  36.7 1.5 select_bitcast_fusion.1
  38.5 2.5 %convolution_convert_fusion.2 = bf16[512,1024]{1,0:T(8,128)(2,1)} fusion(bf16[512,1280]{1,0:T(8,128)(2,1)S(1)} %bitcast.40, bf16[1280,1024]{1,0:T(8,128)(2,1)S(1)} %bitcast.43), kind=kOutput, calls=%fused_computation.4 | convolution fusion | flops 1342701568 | bytes 4980736 | tf_op jit(solution)/shard_map/values/dot_general | solution.py:219
  41.0 4.4 %all-to-all-start.1 = ((bf16[4,128,1024]{2,1,0:T(8,128)(2,1)}), bf16[4,128,1024]{2,1,0:T(8,128)(2,1)S(1)}, u32[]{:S(2)}, u32[]{:S(2)}) async-start(bf16[4,128,1024]{2,1,0:T(8,128)(2,1)} %bitcast.14), calls=%async_computation.1 | async-start | bytes 2097152 | tf_op jit(solution)/shard_map/values/all_to_all | solution.py:221
  46.0 3.1 %collective-permute-done.3.refs_3_.refs_4_ = bf16[2,128,1024]{2,1,0:T(8,128)(2,1)} collective-permute-done((bf16[2,128,1024]{2,1,0:T(8,128)(2,1)S(1)}, bf16[2,128,1024]{2,1,0:T(8,128)(2,1)}, u32[]{:S(2)}, u32[]{:S(2)}) %collective-permute-start.3) | collective-permute-done | bytes 524320 | tf_op jit(solution)/shard_map/keys/ppermute | solution.py:164
  49.2 15.2 %probs.1 = (bf16[8,640,1024]{2,1,0:T(8,128)(2,1)}, bf16[8,128,1024]{2,1,0:T(8,128)(2,1)}, bf16[8,128,1024]{2,1,0:T(8,128)(2,1)}, f32[8,8,1024]{2,1,0:T(8,128)}, ...) custom-call(s32[9]{0:T(128)} %pad_add_fusion.refs_0_, ...), custom_call_target="tpu_custom_call" | custom-call | flops 2684354560 | bytes 16777216 | tf_op jit(solution)/shard_map/probs/pallas_call | solution.py:135
  64.4 1.9 collective-permute-start.5
  66.5 3.4 %collective-permute-start.8 = (bf16[128,1024]{1,0:T(8,128)(2,1)S(1)}, bf16[128,1024]{1,0:T(8,128)(2,1)S(1)}, u32[]{:S(2)}, u32[]{:S(2)}) collective-permute-start(bf16[128,1024]{1,0:T(8,128)(2,1)S(1)} %reduce_sum.24.refs_11_), channel_id=1, source_target_pairs={{0,2},{1,3},{2,4},{3,5},{4,6},{5,7},{8,10},{9,11},{10,12},{11,13},... | collective-permute-start | bytes 786440 | tf_op jit(solution)/shard_map/values_forward/ppermute | solution.py:164
  69.9 1.9 collective-permute-start.9
  71.8 3.6 %collective-permute-done.8.refs_9_ = bf16[128,1024]{1,0:T(8,128)(2,1)S(1)} collective-permute-done((bf16[128,1024]{1,0:T(8,128)(2,1)S(1)}, bf16[128,1024]{1,0:T(8,128)(2,1)S(1)}, u32[]{:S(2)}, u32[]{:S(2)}) %collective-permute-start.8) | collective-permute-done | bytes 262176 | tf_op jit(solution)/shard_map/values_forward/ppermute | solution.py:164
  75.5 4.6 %collective-permute-done.9.refs_10_ = bf16[128,1024]{1,0:T(8,128)(2,1)S(1)} collective-permute-done((bf16[128,1024]{1,0:T(8,128)(2,1)S(1)}, bf16[128,1024]{1,0:T(8,128)(2,1)S(1)}, u32[]{:S(2)}, u32[]{:S(2)}) %collective-permute-start.9) | collective-permute-done | bytes 262176 | tf_op jit(solution)/shard_map/values_forward/ppermute | solution.py:164
  80.1 3.3 %collective-permute-start.10 = (bf16[2,128,1024]{2,1,0:T(8,128)(2,1)S(1)}, bf16[2,128,1024]{2,1,0:T(8,128)(2,1)}, u32[]{:S(2)}, u32[]{:S(2)}) collective-permute-start(bf16[2,128,1024]{2,1,0:T(8,128)(2,1)S(1)} %pad_maximum_fusion.5), channel_id=1, source_target_pairs={{0,2},{1,3},{2,4},{3,5},{4,6},{5,7},{8,10},{9,11},{10,12},{11,13},... | collective-permute-start | bytes 1572872 | tf_op jit(solution)/shard_map/values_forward/ppermute | solution.py:164
  83.4 2.0 %fusion.7 = (bf16[128,1024]{1,0:T(8,128)(2,1)}, bf16[128,1024]{1,0:T(8,128)(2,1)}) fusion(bf16[128,1024]{1,0:T(8,128)(2,1)} %get-tuple-element.60, bf16[2,128,1024]{2,1,0:T(8,128)(2,1)S(1)} %collective-permute-done.5, bf16[128,1024]{1,0:T(8,128)(2,1)} %get-tuple-element.58), kind=kLoop, calls=%fused_computation.23 | loop fusion | flops 1048576 | bytes 1572864 | tf_op jit(solution)/shard_map/value_grad/convert_element_type | solution.py:191
  85.4 2.9 %collective-permute-start.6 = (bf16[128,1024]{1,0:T(8,128)(2,1)}, bf16[128,1024]{1,0:T(8,128)(2,1)S(1)}, u32[]{:S(2)}, u32[]{:S(2)}) collective-permute-start(bf16[128,1024]{1,0:T(8,128)(2,1)} %get-tuple-element.108), channel_id=1, source_target_pairs={{2,0},{3,1},{4,2},{5,3},{6,4},{7,5},{10,8},{11,9},{12,10},{13,11},... | collective-permute-start | bytes 786440 | tf_op jit(solution)/shard_map/value_grad/ppermute | solution.py:168
  88.3 5.7 %collective-permute-start.7 = (bf16[128,1024]{1,0:T(8,128)(2,1)}, bf16[128,1024]{1,0:T(8,128)(2,1)S(1)}, u32[]{:S(2)}, u32[]{:S(2)}) collective-permute-start(bf16[128,1024]{1,0:T(8,128)(2,1)} %get-tuple-element.107), channel_id=1, source_target_pairs={{1,0},{2,1},{3,2},{4,3},{5,4},{6,5},{7,6},{9,8},{10,9},{11,10},{12... | collective-permute-start | bytes 786440 | tf_op jit(solution)/shard_map/value_grad/ppermute | solution.py:168
  94.1 7.9 %collective-permute-done.7 = bf16[128,1024]{1,0:T(8,128)(2,1)S(1)} collective-permute-done((bf16[128,1024]{1,0:T(8,128)(2,1)}, bf16[128,1024]{1,0:T(8,128)(2,1)S(1)}, u32[]{:S(2)}, u32[]{:S(2)}) %collective-permute-start.7) | collective-permute-done | bytes 262176 | tf_op jit(solution)/shard_map/value_grad/ppermute | solution.py:168
  102.1 1.5 collective-permute-start.11
  103.7 2.4 %collective-permute-start.12 = (bf16[128,1024]{1,0:T(8,128)(2,1)S(1)}, bf16[128,1024]{1,0:T(8,128)(2,1)S(1)}, u32[]{:S(2)}, u32[]{:S(2)}) collective-permute-start(bf16[128,1024]{1,0:T(8,128)(2,1)S(1)} %add_convert_fusion.2), channel_id=1, source_target_pairs={{0,64},{32,96},{64,0},{96,32},{1,65},{33,97},{65,1},{97,33},{2,66}... | collective-permute-start | bytes 786440 | tf_op jit(solution)/shard_map/value_grad/ppermute | solution.py:176
  107.3 1.3 collective-permute-done.11
  108.6 5.9 %collective-permute-done.12 = bf16[128,1024]{1,0:T(8,128)(2,1)S(1)} collective-permute-done((bf16[128,1024]{1,0:T(8,128)(2,1)S(1)}, bf16[128,1024]{1,0:T(8,128)(2,1)S(1)}, u32[]{:S(2)}, u32[]{:S(2)}) %collective-permute-start.12) | collective-permute-done | bytes 262176 | tf_op jit(solution)/shard_map/value_grad/ppermute | solution.py:176
  114.6 1.6 convolution_convert_fusion
  116.5 4.5 %collective-permute-start.14 = (bf16[640,1024]{1,0:T(8,128)(2,1)S(1)}, bf16[640,1024]{1,0:T(8,128)(2,1)S(1)}, u32[]{:S(2)}, u32[]{:S(2)}) collective-permute-start(bf16[640,1024]{1,0:T(8,128)(2,1)S(1)} %pad_maximum_fusion.2), channel_id=1, source_target_pairs={{0,8},{8,0},{1,9},{9,1},{2,10},{10,2},{3,11},{11,3},{4,12},{12,4},... | collective-permute-start | bytes 3932168 | tf_op jit(solution)/shard_map/weight_grad/ppermute | solution.py:172
  121.0 1.6 convolution_convert_fusion.1
  123.6 1.6 add_convert_fusion
  125.2 6.9 %all-to-all-start.2 = ((bf16[16,40,1024]{2,1,0:T(8,128)(2,1)}), bf16[16,40,1024]{2,1,0:T(8,128)(2,1)S(1)}, u32[]{:S(2)}, u32[]{:S(2)}) async-start(bf16[16,40,1024]{2,1,0:T(8,128)(2,1)} %bitcast.19), calls=%async_computation.2 | async-start | bytes 2621440 | tf_op jit(solution)/shard_map/weight_grad/all_to_all | solution.py:250
  133.1 1.9 collective-permute-start.15
  136.3 13.3 %grads.1 = (bf16[128,8192]{1,0:T(8,128)(2,1)}, bf16[128,8192]{1,0:T(8,128)(2,1)}, bf16[128,1024]{1,0:T(8,128)(2,1)}, bf16[128,1024]{1,0:T(8,128)(2,1)}, bf16[128...) custom-call(bf16[8,128,1024]{2,1,0:T(8,128)(2,1)} %get-tuple-element.53.refs_0_, ...), custom_call_target="tpu_custom_call" | custom-call | flops 5368709120 | bytes 16777216 | tf_op jit(solution)/shard_map/grads/pallas_call | solution.py:135
  150.0 3.3 %collective-permute-done.17 = bf16[128,1280]{1,0:T(8,128)(2,1)S(1)} collective-permute-done((bf16[128,1280]{1,0:T(8,128)(2,1)S(1)}, bf16[128,1280]{1,0:T(8,128)(2,1)S(1)}, u32[]{:S(2)}, u32[]{:S(2)}) %collective-permute-start.17) | collective-permute-done | bytes 327712 | tf_op jit(solution)/shard_map/input_grad/ppermute | solution.py:176
  154.2 6.6 %all-to-all-start.3 = ((bf16[8,40,1024]{2,1,0:T(8,128)(2,1)}), bf16[8,40,1024]{2,1,0:T(8,128)(2,1)S(1)}, u32[]{:S(2)}, u32[]{:S(2)}) async-start(bf16[8,40,1024]{2,1,0:T(8,128)(2,1)} %broadcast_in_dim.14), calls=%async_computation.3 | async-start | bytes 1310720 | tf_op jit(solution)/shard_map/weight_grad/all_to_all | solution.py:180
  160.9 1.3 collective-permute-start.18
  162.2 1.9 collective-permute-start.19
  164.1 1.9 collective-permute-start.20
  166.1 1.9 collective-permute-start.21
  169.3 6.3 %collective-permute-done.18 = bf16[128,1024]{1,0:T(8,128)(2,1)S(1)} collective-permute-done((bf16[128,1024]{1,0:T(8,128)(2,1)}, bf16[128,1024]{1,0:T(8,128)(2,1)S(1)}, u32[]{:S(2)}, u32[]{:S(2)}) %collective-permute-start.18) | collective-permute-done | bytes 262176 | tf_op jit(solution)/shard_map/key_grad/ppermute | solution.py:168
  175.5 5.6 %collective-permute-done.19 = bf16[128,1024]{1,0:T(8,128)(2,1)S(1)} collective-permute-done((bf16[128,1024]{1,0:T(8,128)(2,1)}, bf16[128,1024]{1,0:T(8,128)(2,1)S(1)}, u32[]{:S(2)}, u32[]{:S(2)}) %collective-permute-start.19) | collective-permute-done | bytes 262176 | tf_op jit(solution)/shard_map/key_grad/ppermute | solution.py:168
  181.2 5.5 %collective-permute-done.20 = bf16[128,1024]{1,0:T(8,128)(2,1)S(1)} collective-permute-done((bf16[128,1024]{1,0:T(8,128)(2,1)}, bf16[128,1024]{1,0:T(8,128)(2,1)S(1)}, u32[]{:S(2)}, u32[]{:S(2)}) %collective-permute-start.20) | collective-permute-done | bytes 262176 | tf_op jit(solution)/shard_map/key_grad/ppermute | solution.py:168
  186.7 6.9 %collective-permute-done.21 = bf16[128,1024]{1,0:T(8,128)(2,1)S(1)} collective-permute-done((bf16[128,1024]{1,0:T(8,128)(2,1)S(1)}, bf16[128,1024]{1,0:T(8,128)(2,1)S(1)}, u32[]{:S(2)}, u32[]{:S(2)}) %collective-permute-start.21) | collective-permute-done | bytes 262176 | tf_op jit(solution)/shard_map/key_grad/ppermute | solution.py:168
  194.4 1.2 bitcast_convert_fusion
  (71 shorter events, 11.8 us)
Async XLA Ops:
  3.1 4.3 %copy-start.3 = (bf16[320,1024]{1,0:T(8,128)(2,1)S(1)}, bf16[320,1024]{1,0:T(8,128)(2,1)}, u32[]{:S(2)}) copy-start(bf16[320,1024]{1,0:T(8,128)(2,1)} %param.7) | copy-start | bytes 1966084
  3.1 21.3 %all-to-all-start = ((bf16[128,4,1280]{0,2,1:T(8,128)(2,1)}), bf16[128,4,1280]{0,2,1:T(8,128)(2,1)S(1)}, u32[]{:S(2)}, u32[]{:S(2)}) async-start(bf16[128,4,1280]{0,2,1:T(8,128)(2,1)} %bitcast.2), calls=%async_computation | async-start | bytes 2621440 | tf_op jit(solution)/shard_map/hidden_columns/all_to_all | solution.py:210
  7.4 21.0 %collective-permute-start = (bf16[320,1024]{1,0:T(8,128)(2,1)S(1)}, bf16[320,1024]{1,0:T(8,128)(2,1)}, u32[]{:S(2)}, u32[]{:S(2)}) collective-permute-start(bf16[320,1024]{1,0:T(8,128)(2,1)S(1)} %copy-done.3), channel_id=1, source_target_pairs={{0,16},{16,0},{1,17},{17,1},{2,18},{18,2},{3,19},{19,3},{4,20},{20... | collective-permute-start | bytes 1966088 | tf_op jit(solution)/shard_map/weight_rows/ppermute | solution.py:172
  8.7 16.3 %collective-permute-start.1 = (bf16[128,1024]{1,0:T(8,128)(2,1)}, bf16[128,1024]{1,0:T(8,128)(2,1)S(1)}, u32[]{:S(2)}, u32[]{:S(2)}) collective-permute-start(bf16[128,1024]{1,0:T(8,128)(2,1)} %refs_7_.1), channel_id=1, source_target_pairs={{0,2},{1,3},{2,4},{3,5},{4,6},{5,7},{8,10},{9,11},{10,12},{11,13},... | collective-permute-start | bytes 786440 | tf_op jit(solution)/shard_map/keys/ppermute | solution.py:164
  11.8 16.1 %collective-permute-start.2 = (bf16[128,1024]{1,0:T(8,128)(2,1)}, bf16[128,1024]{1,0:T(8,128)(2,1)}, u32[]{:S(2)}, u32[]{:S(2)}) collective-permute-start(bf16[128,1024]{1,0:T(8,128)(2,1)} %refs_7_.1), channel_id=1, source_target_pairs={{0,1},{1,2},{2,3},{3,4},{4,5},{5,6},{6,7},{8,9},{9,10},{10,11},{11... | collective-permute-start | bytes 786440 | tf_op jit(solution)/shard_map/keys/ppermute | solution.py:164
  25.0 7.6 %copy-start.13 = (bf16[128,1024]{1,0:T(8,128)(2,1)}, bf16[128,1024]{1,0:T(8,128)(2,1)S(1)}, u32[]{:S(2)}) copy-start(bf16[128,1024]{1,0:T(8,128)(2,1)S(1)} %collective-permute-done.1.refs_4_.refs_5_) | copy-start | bytes 786436
  30.7 6.0 %collective-permute-start.4 = (bf16[2,320,1024]{2,1,0:T(8,128)(2,1)}, bf16[2,320,1024]{2,1,0:T(8,128)(2,1)}, u32[]{:S(2)}, u32[]{:S(2)}) collective-permute-start(bf16[2,320,1024]{2,1,0:T(8,128)(2,1)} %pad_maximum_fusion.1), channel_id=1, source_target_pairs={{0,8},{8,0},{1,9},{9,1},{2,10},{10,2},{3,11},{11,3},{4,12},{12,4},... | collective-permute-start | bytes 3932168 | tf_op jit(solution)/shard_map/weight_rows/ppermute | solution.py:172
  33.6 15.6 %collective-permute-start.3 = (bf16[2,128,1024]{2,1,0:T(8,128)(2,1)S(1)}, bf16[2,128,1024]{2,1,0:T(8,128)(2,1)}, u32[]{:S(2)}, u32[]{:S(2)}) collective-permute-start(bf16[2,128,1024]{2,1,0:T(8,128)(2,1)S(1)} %pad_maximum_fusion.4), channel_id=1, source_target_pairs={{0,2},{1,3},{2,4},{3,5},{4,6},{5,7},{8,10},{9,11},{10,12},{11,13},... | collective-permute-start | bytes 1572872 | tf_op jit(solution)/shard_map/keys/ppermute | solution.py:164
  38.5 2.5 %copy-start = (bf16[2,2,320,1024]{3,2,1,0:T(8,128)(2,1)}, bf16[2,2,320,1024]{3,2,1,0:T(8,128)(2,1)S(1)}, u32[]{:S(2)}) copy-start(bf16[2,2,320,1024]{3,2,1,0:T(8,128)(2,1)S(1)} %pad_maximum_fusion) | copy-start | bytes 7864324
  41.0 4.4 %copy-start.17 = (s32[1,8]{1,0:T(1,128)S(1)}, s32[1,8]{1,0:T(1,128)}, u32[]{:S(2)}) copy-start(s32[1,8]{1,0:T(1,128)} %param.11) | copy-start | bytes 100
  41.0 25.3 %all-to-all-start.1 = ((bf16[4,128,1024]{2,1,0:T(8,128)(2,1)}), bf16[4,128,1024]{2,1,0:T(8,128)(2,1)S(1)}, u32[]{:S(2)}, u32[]{:S(2)}) async-start(bf16[4,128,1024]{2,1,0:T(8,128)(2,1)} %bitcast.14), calls=%async_computation.1 | async-start | bytes 2097152 | tf_op jit(solution)/shard_map/values/all_to_all | solution.py:221
  64.4 19.0 %collective-permute-start.5 = (bf16[2,128,1024]{2,1,0:T(8,128)(2,1)}, bf16[2,128,1024]{2,1,0:T(8,128)(2,1)S(1)}, u32[]{:S(2)}, u32[]{:S(2)}) collective-permute-start(bf16[2,128,1024]{2,1,0:T(8,128)(2,1)} %get-tuple-element.59), channel_id=1, source_target_pairs={{2,0},{3,1},{4,2},{5,3},{6,4},{7,5},{10,8},{11,9},{12,10},{13,11},... | collective-permute-start | bytes 1572872 | tf_op jit(solution)/shard_map/value_grad/ppermute | solution.py:168
  66.5 18.9 %copy-start.12 = (bf16[128,1024]{1,0:T(8,128)(2,1)}, bf16[128,1024]{1,0:T(8,128)(2,1)S(1)}, u32[]{:S(2)}) copy-start(bf16[128,1024]{1,0:T(8,128)(2,1)S(1)} %reduce_sum.24.refs_11_) | copy-start | bytes 786436
  66.5 8.9 %collective-permute-start.8 = (bf16[128,1024]{1,0:T(8,128)(2,1)S(1)}, bf16[128,1024]{1,0:T(8,128)(2,1)S(1)}, u32[]{:S(2)}, u32[]{:S(2)}) collective-permute-start(bf16[128,1024]{1,0:T(8,128)(2,1)S(1)} %reduce_sum.24.refs_11_), channel_id=1, source_target_pairs={{0,2},{1,3},{2,4},{3,5},{4,6},{5,7},{8,10},{9,11},{10,12},{11,13},... | collective-permute-start | bytes 786440 | tf_op jit(solution)/shard_map/values_forward/ppermute | solution.py:164
  69.9 10.1 %collective-permute-start.9 = (bf16[128,1024]{1,0:T(8,128)(2,1)S(1)}, bf16[128,1024]{1,0:T(8,128)(2,1)S(1)}, u32[]{:S(2)}, u32[]{:S(2)}) collective-permute-start(bf16[128,1024]{1,0:T(8,128)(2,1)S(1)} %reduce_sum.24.refs_11_), channel_id=1, source_target_pairs={{0,1},{1,2},{2,3},{3,4},{4,5},{5,6},{6,7},{8,9},{9,10},{10,11},{11... | collective-permute-start | bytes 786440 | tf_op jit(solution)/shard_map/values_forward/ppermute | solution.py:164
  75.5 10.0 %copy-start.14 = (bf16[128,1024]{1,0:T(8,128)(2,1)}, bf16[128,1024]{1,0:T(8,128)(2,1)S(1)}, u32[]{:S(2)}) copy-start(bf16[128,1024]{1,0:T(8,128)(2,1)S(1)} %collective-permute-done.8.refs_9_) | copy-start | bytes 786436
  80.0 3.4 %copy-start.15 = (bf16[128,1024]{1,0:T(8,128)(2,1)}, bf16[128,1024]{1,0:T(8,128)(2,1)S(1)}, u32[]{:S(2)}) copy-start(bf16[128,1024]{1,0:T(8,128)(2,1)S(1)} %collective-permute-done.9.refs_10_) | copy-start | bytes 786436
  80.0 22.0 %copy-start.5 = (f32[128,1024]{1,0:T(8,128)S(1)}, f32[128,1024]{1,0:T(8,128)}, u32[]{:S(2)}) copy-start(f32[128,1024]{1,0:T(8,128)} %get-tuple-element.62) | copy-start | bytes 1572868
  80.1 21.9 %collective-permute-start.10 = (bf16[2,128,1024]{2,1,0:T(8,128)(2,1)S(1)}, bf16[2,128,1024]{2,1,0:T(8,128)(2,1)}, u32[]{:S(2)}, u32[]{:S(2)}) collective-permute-start(bf16[2,128,1024]{2,1,0:T(8,128)(2,1)S(1)} %pad_maximum_fusion.5), channel_id=1, source_target_pairs={{0,2},{1,3},{2,4},{3,5},{4,6},{5,7},{8,10},{9,11},{10,12},{11,13},... | collective-permute-start | bytes 1572872 | tf_op jit(solution)/shard_map/values_forward/ppermute | solution.py:164
  85.4 8.7 %collective-permute-start.6 = (bf16[128,1024]{1,0:T(8,128)(2,1)}, bf16[128,1024]{1,0:T(8,128)(2,1)S(1)}, u32[]{:S(2)}, u32[]{:S(2)}) collective-permute-start(bf16[128,1024]{1,0:T(8,128)(2,1)} %get-tuple-element.108), channel_id=1, source_target_pairs={{2,0},{3,1},{4,2},{5,3},{6,4},{7,5},{10,8},{11,9},{12,10},{13,11},... | collective-permute-start | bytes 786440 | tf_op jit(solution)/shard_map/value_grad/ppermute | solution.py:168
  88.3 13.7 %collective-permute-start.7 = (bf16[128,1024]{1,0:T(8,128)(2,1)}, bf16[128,1024]{1,0:T(8,128)(2,1)S(1)}, u32[]{:S(2)}, u32[]{:S(2)}) collective-permute-start(bf16[128,1024]{1,0:T(8,128)(2,1)} %get-tuple-element.107), channel_id=1, source_target_pairs={{1,0},{2,1},{3,2},{4,3},{5,4},{6,5},{7,6},{9,8},{10,9},{11,10},{12... | collective-permute-start | bytes 786440 | tf_op jit(solution)/shard_map/value_grad/ppermute | solution.py:168
  102.1 6.5 %collective-permute-start.11 = (bf16[128,1024]{1,0:T(8,128)(2,1)S(1)}, bf16[128,1024]{1,0:T(8,128)(2,1)S(1)}, u32[]{:S(2)}, u32[]{:S(2)}) collective-permute-start(bf16[128,1024]{1,0:T(8,128)(2,1)S(1)} %add_convert_fusion.2), channel_id=1, source_target_pairs={{0,32},{32,64},{64,96},{96,0},{1,33},{33,65},{65,97},{97,1},{2,34}... | collective-permute-start | bytes 786440 | tf_op jit(solution)/shard_map/value_grad/ppermute | solution.py:176
  103.7 10.9 %collective-permute-start.12 = (bf16[128,1024]{1,0:T(8,128)(2,1)S(1)}, bf16[128,1024]{1,0:T(8,128)(2,1)S(1)}, u32[]{:S(2)}, u32[]{:S(2)}) collective-permute-start(bf16[128,1024]{1,0:T(8,128)(2,1)S(1)} %add_convert_fusion.2), channel_id=1, source_target_pairs={{0,64},{32,96},{64,0},{96,32},{1,65},{33,97},{65,1},{97,33},{2,66}... | collective-permute-start | bytes 786440 | tf_op jit(solution)/shard_map/value_grad/ppermute | solution.py:176
  106.1 8.5 %collective-permute-start.13 = (bf16[128,1024]{1,0:T(8,128)(2,1)S(1)}, bf16[128,1024]{1,0:T(8,128)(2,1)S(1)}, u32[]{:S(2)}, u32[]{:S(2)}) collective-permute-start(bf16[128,1024]{1,0:T(8,128)(2,1)S(1)} %add_convert_fusion.2), channel_id=1, source_target_pairs={{0,96},{32,0},{64,32},{96,64},{1,97},{33,1},{65,33},{97,65},{2,98}... | collective-permute-start | bytes 786440 | tf_op jit(solution)/shard_map/value_grad/ppermute | solution.py:176
  116.4 4.6 %copy-start.1 = (bf16[2,2,320,1024]{3,2,1,0:T(8,128)(2,1)S(1)}, bf16[2,2,320,1024]{3,2,1,0:T(8,128)(2,1)}, u32[]{:S(2)}) copy-start(bf16[2,2,320,1024]{3,2,1,0:T(8,128)(2,1)} %copy-done) | copy-start | bytes 7864324
  116.5 7.1 %collective-permute-start.14 = (bf16[640,1024]{1,0:T(8,128)(2,1)S(1)}, bf16[640,1024]{1,0:T(8,128)(2,1)S(1)}, u32[]{:S(2)}, u32[]{:S(2)}) collective-permute-start(bf16[640,1024]{1,0:T(8,128)(2,1)S(1)} %pad_maximum_fusion.2), channel_id=1, source_target_pairs={{0,8},{8,0},{1,9},{9,1},{2,10},{10,2},{3,11},{11,3},{4,12},{12,4},... | collective-permute-start | bytes 3932168 | tf_op jit(solution)/shard_map/weight_grad/ppermute | solution.py:172
  125.2 24.5 %all-to-all-start.2 = ((bf16[16,40,1024]{2,1,0:T(8,128)(2,1)}), bf16[16,40,1024]{2,1,0:T(8,128)(2,1)S(1)}, u32[]{:S(2)}, u32[]{:S(2)}) async-start(bf16[16,40,1024]{2,1,0:T(8,128)(2,1)} %bitcast.19), calls=%async_computation.2 | async-start | bytes 2621440 | tf_op jit(solution)/shard_map/weight_grad/all_to_all | solution.py:250
  133.1 17.0 %collective-permute-start.15 = (bf16[128,1280]{1,0:T(8,128)(2,1)}, bf16[128,1280]{1,0:T(8,128)(2,1)S(1)}, u32[]{:S(2)}, u32[]{:S(2)}) collective-permute-start(bf16[128,1280]{1,0:T(8,128)(2,1)} %get-tuple-element.99), channel_id=1, source_target_pairs={{0,96},{32,0},{64,32},{96,64},{1,97},{33,1},{65,33},{97,65},{2,98}... | collective-permute-start | bytes 983048 | tf_op jit(solution)/shard_map/input_grad/ppermute | solution.py:176
  134.9 15.1 %collective-permute-start.16 = (bf16[128,1280]{1,0:T(8,128)(2,1)}, bf16[128,1280]{1,0:T(8,128)(2,1)S(1)}, u32[]{:S(2)}, u32[]{:S(2)}) collective-permute-start(bf16[128,1280]{1,0:T(8,128)(2,1)} %get-tuple-element.98), channel_id=1, source_target_pairs={{0,64},{32,96},{64,0},{96,32},{1,65},{33,97},{65,1},{97,33},{2,66}... | collective-permute-start | bytes 983048 | tf_op jit(solution)/shard_map/input_grad/ppermute | solution.py:176
  135.8 17.5 %collective-permute-start.17 = (bf16[128,1280]{1,0:T(8,128)(2,1)S(1)}, bf16[128,1280]{1,0:T(8,128)(2,1)S(1)}, u32[]{:S(2)}, u32[]{:S(2)}) collective-permute-start(bf16[128,1280]{1,0:T(8,128)(2,1)S(1)} %get-tuple-element.97), channel_id=1, source_target_pairs={{0,32},{32,64},{64,96},{96,0},{1,33},{33,65},{65,97},{97,1},{2,34}... | collective-permute-start | bytes 983048 | tf_op jit(solution)/shard_map/input_grad/ppermute | solution.py:176
  150.0 16.1 %copy-start.16 = (bf16[128,1024]{1,0:T(8,128)(2,1)S(1)}, bf16[128,1024]{1,0:T(8,128)(2,1)}, u32[]{:S(2)}) copy-start(bf16[128,1024]{1,0:T(8,128)(2,1)} %get-tuple-element.84) | copy-start | bytes 786436
  150.0 16.0 %copy-start.6 = (bf16[128,1280]{1,0:T(8,128)(2,1)}, bf16[128,1280]{1,0:T(8,128)(2,1)S(1)}, u32[]{:S(2)}) copy-start(bf16[128,1280]{1,0:T(8,128)(2,1)S(1)} %collective-permute-done.15) | copy-start | bytes 983044
  150.0 16.0 %copy-start.8 = (bf16[128,1280]{1,0:T(8,128)(2,1)}, bf16[128,1280]{1,0:T(8,128)(2,1)S(1)}, u32[]{:S(2)}) copy-start(bf16[128,1280]{1,0:T(8,128)(2,1)S(1)} %collective-permute-done.16) | copy-start | bytes 983044
  153.3 12.8 %copy-start.10 = (bf16[128,1280]{1,0:T(8,128)(2,1)}, bf16[128,1280]{1,0:T(8,128)(2,1)S(1)}, u32[]{:S(2)}) copy-start(bf16[128,1280]{1,0:T(8,128)(2,1)S(1)} %collective-permute-done.17) | copy-start | bytes 983044
  154.2 40.2 %all-to-all-start.3 = ((bf16[8,40,1024]{2,1,0:T(8,128)(2,1)}), bf16[8,40,1024]{2,1,0:T(8,128)(2,1)S(1)}, u32[]{:S(2)}, u32[]{:S(2)}) async-start(bf16[8,40,1024]{2,1,0:T(8,128)(2,1)} %broadcast_in_dim.14), calls=%async_computation.3 | async-start | bytes 1310720 | tf_op jit(solution)/shard_map/weight_grad/all_to_all | solution.py:180
  160.9 14.7 %collective-permute-start.18 = (bf16[128,1024]{1,0:T(8,128)(2,1)}, bf16[128,1024]{1,0:T(8,128)(2,1)S(1)}, u32[]{:S(2)}, u32[]{:S(2)}) collective-permute-start(bf16[128,1024]{1,0:T(8,128)(2,1)} %get-tuple-element.81), channel_id=1, source_target_pairs={{4,0},{5,1},{6,2},{7,3},{12,8},{13,9},{14,10},{15,11},{20,16},{21,... | collective-permute-start | bytes 786440 | tf_op jit(solution)/shard_map/key_grad/ppermute | solution.py:168
  162.2 19.0 %collective-permute-start.19 = (bf16[128,1024]{1,0:T(8,128)(2,1)}, bf16[128,1024]{1,0:T(8,128)(2,1)S(1)}, u32[]{:S(2)}, u32[]{:S(2)}) collective-permute-start(bf16[128,1024]{1,0:T(8,128)(2,1)} %get-tuple-element.82), channel_id=1, source_target_pairs={{3,0},{4,1},{5,2},{6,3},{7,4},{11,8},{12,9},{13,10},{14,11},{15,12... | collective-permute-start | bytes 786440 | tf_op jit(solution)/shard_map/key_grad/ppermute | solution.py:168
  164.1 22.6 %collective-permute-start.20 = (bf16[128,1024]{1,0:T(8,128)(2,1)}, bf16[128,1024]{1,0:T(8,128)(2,1)S(1)}, u32[]{:S(2)}, u32[]{:S(2)}) collective-permute-start(bf16[128,1024]{1,0:T(8,128)(2,1)} %get-tuple-element.83), channel_id=1, source_target_pairs={{2,0},{3,1},{4,2},{5,3},{6,4},{7,5},{10,8},{11,9},{12,10},{13,11},... | collective-permute-start | bytes 786440 | tf_op jit(solution)/shard_map/key_grad/ppermute | solution.py:168
  166.1 27.4 %collective-permute-start.21 = (bf16[128,1024]{1,0:T(8,128)(2,1)S(1)}, bf16[128,1024]{1,0:T(8,128)(2,1)S(1)}, u32[]{:S(2)}, u32[]{:S(2)}) collective-permute-start(bf16[128,1024]{1,0:T(8,128)(2,1)S(1)} %copy-done.16), channel_id=1, source_target_pairs={{1,0},{2,1},{3,2},{4,3},{5,4},{6,5},{7,6},{9,8},{10,9},{11,10},{12... | collective-permute-start | bytes 786440 | tf_op jit(solution)/shard_map/key_grad/ppermute | solution.py:168
  168.0 1.0 copy-start.7
  168.0 1.1 copy-start.9
  168.2 1.1 copy-start.11
  168.2 25.4 %copy-start.4 = (f32[128,1024]{1,0:T(8,128)S(1)}, f32[128,1024]{1,0:T(8,128)}, u32[]{:S(2)}) copy-start(f32[128,1024]{1,0:T(8,128)} %get-tuple-element.85) | copy-start | bytes 1572868
  169.2 26.4 %copy-start.2 = (bf16[128,5120]{1,0:T(8,128)(2,1)}, bf16[128,5120]{1,0:T(8,128)(2,1)S(1)}, u32[]{:S(2)}) copy-start(bf16[128,5120]{1,0:T(8,128)(2,1)S(1)} %constant_dynamic-update-slice_fusion) | copy-start | bytes 3932164

commit v5 on v4

--- a/solution.py
+++ b/solution.py
@@ -24,7 +24,7 @@
 WP = 4
 
 
-def probs_kernel(meta, q, do, k01, k2, k3, k4, e_out, qt_out, dt_out, li_out, v01, v2, v3, v4, bias):
+def probs_kernel(meta, q, do, k01, k2, k3, k4, e_out, qt_out, dt_out, li_out, v0, v1, v2, v3, v4, bias):
     rows = q.shape[0]
     ks = (k01.at[0], k01.at[1], k2, k3, k4)
 
@@ -64,7 +64,7 @@
         dt_out[0, :, cols] = (dt.astype(f32) * li).astype(bf)
     dall = dt_out[0]
     nt = (((1,), (1,)), ((), ()))
-    for c, v in enumerate((v01.at[0], v01.at[1], v2, v3, v4)):
+    for c, v in enumerate((v0, v1, v2, v3, v4)):
         e = e_out[0, c * rows : (c + 1) * rows, :]
         v[...] = lax.dot_general(e, dall, nt, preferred_element_type=f32).astype(v.dtype)
 
@@ -149,7 +149,7 @@
 def probs_call(meta, q, do, ks):
     scratch = [pltpu.VMEM((CH * RB, RB), f32)]
     ins = ["m", "b", "b", "p", "n", "n", "n"]
-    outs = ["e", "t", "t", "s", "p", "n", "n", "o"]
+    outs = ["e", "t", "t", "s"] + ["n"] * (CH - 1) + ["o"]
     return call(probs_kernel, (meta, q, do, *ks), ins, outs, scratch, 2 * CH, CH, 1)
 
 
@@ -224,12 +224,14 @@
         e, qt, dt, li, *dv = probs_call(meta, query, cot, (k01, k2, k3, key))
     with jax.named_scope("values_forward"):
         v2, v3 = forward(values, 2), forward(values, 1)
-        v01 = forward(jnp.stack([v2, v3]), 2)
     with jax.named_scope("value_grad"):
-        dv = relay_sum(dv, backward(dv[0], 2))
-        dv, v01, v2, v3 = lax.optimization_barrier((dv, v01, v2, v3))
+        dv = [backward(dv[c], CH - 1 - c) for c in range(CH - 1)] + [dv[-1]]
+        dv, v2, v3 = lax.optimization_barrier((dv, v2, v3))
         vgrad = sum(d.astype(f32) for d in dv).astype(bf)
         vys = [vgrad] + [along_y(vgrad, k) for k in (1, 2, 3)]
+    with jax.named_scope("values_forward"):
+        v01 = forward(jnp.stack([v2, v3]), 2)
+        vys, v01 = lax.optimization_barrier((vys, v01))
         vy = jnp.concatenate(vys)
         vs = (v01, v2, v3, values)
     with jax.named_scope("weight_grad"):

time: 197 us -> 190 us (0.964)
  waiting for transfers between devices: 68.9 us -> 64.1 us
    ppermute x6, waiting for transfers between devices: 14.2 us -> 6.13 us  [forward(): return lax.ppermute(x, ('x', 'zh'), [(i, i + k) for i in range(N - k)])]
    ppermute x6, starting transfers between devices: 17 us -> 21 us  [forward(): return lax.ppermute(x, ('x', 'zh'), [(i, i + k) for i in range(N - k)])]
    ppermute x7 -> x8, starting transfers between devices: 17.5 us -> 14.2 us  [backward(): return lax.ppermute(x, ('x', 'zh'), [(i + k, i) for i in range(N - k)])]
    convert_element_type x1 -> x0, other arithmetic: 2.02 us -> none  [relay_sum(): one = (one.astype(f32) + got[1].astype(f32)).astype(bf)]
    ppermute x7 -> x8, waiting for transfers between devices: 32.2 us -> 34 us  [backward(): return lax.ppermute(x, ('x', 'zh'), [(i + k, i) for i in range(N - k)])]
    unnamed x37 -> x42, local copies, waits for them, and re-layouts: 3.42 us -> 4.17 us
  transfers between devices with their start and end apart: 26 -> 27, of which waited for: 16 -> 15; matrix products, arithmetic and copies ran while one was open for 7% -> 6% of each run, Pallas kernels for 15% -> 15%
where the time goes in v5:
time: 190 us; the launch traced here: 189 us
  starting transfers between devices  71 us (37%)
  waiting for transfers between devices  64.1 us (34%)
  Pallas kernels  28.4 us (15%)
  other arithmetic  11.3 us (6%)
  local copies, waits for them, and re-layouts  7.25 us (4%)
  matrix products  5.62 us (3%)
    ppermute x8, waiting for transfers between devices, backward(): return lax.ppermute(x, ('x', 'zh'), [(i + k, i) for i in range(N - k)])  34 us
    pallas_call x2, Pallas kernels, call(): pl.pallas_call(heads, grid=(KV // hp,), in_specs=[spec(k) for k in ins],...  28.4 us
    ppermute x6, starting transfers between devices, forward(): return lax.ppermute(x, ('x', 'zh'), [(i, i + k) for i in range(N - k)])  21 us
    ppermute x8, starting transfers between devices, backward(): return lax.ppermute(x, ('x', 'zh'), [(i + k, i) for i in range(N - k)])  14.2 us
    ppermute x6, waiting for transfers between devices, along_y(): return lax.ppermute(x, 'y', [(i, (i + k) % 4) for i in range(4)])  11.9 us
    all_to_all x1, waiting for transfers between devices, body(): lax.all_to_all(hidden.reshape(rows, 4, depth), 'y', 1, 0, tiled=True)  10.3 us
    ppermute x6, starting transfers between devices, along_y(): return lax.ppermute(x, 'y', [(i, (i + k) % 4) for i in range(4)])  8.4 us
    all_to_all x1, starting transfers between devices, over_seq(): return lax.all_to_all(x, ('x', 'zh'), 0, 0, tiled=True)  6.65 us
  transfers between devices with their start and end apart: 27, of which 15 were waited for; matrix products, arithmetic and copies ran while one was open for 6% of the time, Pallas kernels for 15%

profile of v5, /device:TPU:67, one launch (start us, length us, event | category | flops | bytes accessed | tf_op | source)
XLA Modules:
  0.0 188.9 jit_solution(14978936757802666498)
XLA Ops:
  0.6 2.4 %copy.12 = bf16[128,5120]{0,1:T(8,128)(2,1)} copy(bf16[128,5120]{1,0:T(8,128)(2,1)} %param.6) | data formatting | bytes 2621440 | tf_op args[0]
  3.1 4.3 %all-to-all-start = ((bf16[128,4,1280]{0,2,1:T(8,128)(2,1)}), bf16[128,4,1280]{0,2,1:T(8,128)(2,1)S(1)}, u32[]{:S(2)}, u32[]{:S(2)}) async-start(bf16[128,4,1280]{0,2,1:T(8,128)(2,1)} %bitcast.2), calls=%async_computation | async-start | bytes 2621440 | tf_op jit(solution)/shard_map/hidden_columns/all_to_all | solution.py:210
  7.4 1.3 collective-permute-start
  8.7 3.1 %collective-permute-start.1 = (bf16[128,1024]{1,0:T(8,128)(2,1)}, bf16[128,1024]{1,0:T(8,128)(2,1)S(1)}, u32[]{:S(2)}, u32[]{:S(2)}) collective-permute-start(bf16[128,1024]{1,0:T(8,128)(2,1)} %refs_7_.1), channel_id=1, source_target_pairs={{0,2},{1,3},{2,4},{3,5},{4,6},{5,7},{8,10},{9,11},{10,12},{11,13},... | collective-permute-start | bytes 786440 | tf_op jit(solution)/shard_map/keys/ppermute | solution.py:164
  11.8 2.2 %collective-permute-start.2 = (bf16[128,1024]{1,0:T(8,128)(2,1)}, bf16[128,1024]{1,0:T(8,128)(2,1)}, u32[]{:S(2)}, u32[]{:S(2)}) collective-permute-start(bf16[128,1024]{1,0:T(8,128)(2,1)} %refs_7_.1), channel_id=1, source_target_pairs={{0,1},{1,2},{2,3},{3,4},{4,5},{5,6},{6,7},{8,9},{9,10},{10,11},{11... | collective-permute-start | bytes 786440 | tf_op jit(solution)/shard_map/keys/ppermute | solution.py:164
  14.1 10.3 %all-to-all-done = bf16[128,4,1280]{0,2,1:T(8,128)(2,1)S(1)} async-done(((bf16[128,4,1280]{0,2,1:T(8,128)(2,1)}), bf16[128,4,1280]{0,2,1:T(8,128)(2,1)S(1)}, u32[]{:S(2)}, u32[]{:S(2)}) %all-to-all-start) | async-done | bytes 1310752 | tf_op jit(solution)/shard_map/hidden_columns/all_to_all | solution.py:210
  25.0 2.9 %collective-permute-done.2.refs_5_.refs_6_ = bf16[128,1024]{1,0:T(8,128)(2,1)} collective-permute-done((bf16[128,1024]{1,0:T(8,128)(2,1)}, bf16[128,1024]{1,0:T(8,128)(2,1)}, u32[]{:S(2)}, u32[]{:S(2)}) %collective-permute-start.2) | collective-permute-done | bytes 262176 | tf_op jit(solution)/shard_map/keys/ppermute | solution.py:164
  28.4 1.2 select_bitcast_fusion.3
  30.7 1.9 collective-permute-start.4
  33.6 3.1 %collective-permute-start.3 = (bf16[2,128,1024]{2,1,0:T(8,128)(2,1)S(1)}, bf16[2,128,1024]{2,1,0:T(8,128)(2,1)}, u32[]{:S(2)}, u32[]{:S(2)}) collective-permute-start(bf16[2,128,1024]{2,1,0:T(8,128)(2,1)S(1)} %pad_maximum_fusion.3), channel_id=1, source_target_pairs={{0,2},{1,3},{2,4},{3,5},{4,6},{5,7},{8,10},{9,11},{10,12},{11,13},... | collective-permute-start | bytes 1572872 | tf_op jit(solution)/shard_map/keys/ppermute | solution.py:164
  36.7 1.5 select_bitcast_fusion.1
  38.5 2.5 %convolution_convert_fusion.2 = bf16[512,1024]{1,0:T(8,128)(2,1)} fusion(bf16[512,1280]{1,0:T(8,128)(2,1)S(1)} %bitcast.32, bf16[1280,1024]{1,0:T(8,128)(2,1)S(1)} %bitcast.35), kind=kOutput, calls=%fused_computation.4 | convolution fusion | flops 1342701568 | bytes 4980736 | tf_op jit(solution)/shard_map/values/dot_general | solution.py:219
  41.0 4.4 %all-to-all-start.1 = ((bf16[4,128,1024]{2,1,0:T(8,128)(2,1)}), bf16[4,128,1024]{2,1,0:T(8,128)(2,1)S(1)}, u32[]{:S(2)}, u32[]{:S(2)}) async-start(bf16[4,128,1024]{2,1,0:T(8,128)(2,1)} %bitcast.14), calls=%async_computation.1 | async-start | bytes 2097152 | tf_op jit(solution)/shard_map/values/all_to_all | solution.py:221
  46.0 3.2 %collective-permute-done.3.refs_3_.refs_4_ = bf16[2,128,1024]{2,1,0:T(8,128)(2,1)} collective-permute-done((bf16[2,128,1024]{2,1,0:T(8,128)(2,1)S(1)}, bf16[2,128,1024]{2,1,0:T(8,128)(2,1)}, u32[]{:S(2)}, u32[]{:S(2)}) %collective-permute-start.3) | collective-permute-done | bytes 524320 | tf_op jit(solution)/shard_map/keys/ppermute | solution.py:164
  49.2 15.2 %probs.1 = (bf16[8,640,1024]{2,1,0:T(8,128)(2,1)}, bf16[8,128,1024]{2,1,0:T(8,128)(2,1)}, bf16[8,128,1024]{2,1,0:T(8,128)(2,1)}, f32[8,8,1024]{2,1,0:T(8,128)}, ...) custom-call(s32[9]{0:T(128)} %pad_add_fusion.refs_0_, ...), custom_call_target="tpu_custom_call" | custom-call | flops 2684354560 | bytes 16777216 | tf_op jit(solution)/shard_map/probs/pallas_call | solution.py:135
  64.3 1.4 collective-permute-start.5
  65.8 1.9 %collective-permute-start.6 = (bf16[128,1024]{1,0:T(8,128)(2,1)}, bf16[128,1024]{1,0:T(8,128)(2,1)}, u32[]{:S(2)}, u32[]{:S(2)}) collective-permute-start(bf16[128,1024]{1,0:T(8,128)(2,1)} %get-tuple-element.65), channel_id=1, source_target_pairs={{3,0},{4,1},{5,2},{6,3},{7,4},{11,8},{12,9},{13,10},{14,11},{15,12... | collective-permute-start | bytes 786440 | tf_op jit(solution)/shard_map/value_grad/ppermute | solution.py:168
  67.7 1.9 %collective-permute-start.7 = (bf16[128,1024]{1,0:T(8,128)(2,1)}, bf16[128,1024]{1,0:T(8,128)(2,1)}, u32[]{:S(2)}, u32[]{:S(2)}) collective-permute-start(bf16[128,1024]{1,0:T(8,128)(2,1)} %get-tuple-element.66), channel_id=1, source_target_pairs={{2,0},{3,1},{4,2},{5,3},{6,4},{7,5},{10,8},{11,9},{12,10},{13,11},... | collective-permute-start | bytes 786440 | tf_op jit(solution)/shard_map/value_grad/ppermute | solution.py:168
  69.6 1.9 %collective-permute-start.8 = (bf16[128,1024]{1,0:T(8,128)(2,1)}, bf16[128,1024]{1,0:T(8,128)(2,1)}, u32[]{:S(2)}, u32[]{:S(2)}) collective-permute-start(bf16[128,1024]{1,0:T(8,128)(2,1)} %get-tuple-element.67), channel_id=1, source_target_pairs={{1,0},{2,1},{3,2},{4,3},{5,4},{6,5},{7,6},{9,8},{10,9},{11,10},{12... | collective-permute-start | bytes 786440 | tf_op jit(solution)/shard_map/value_grad/ppermute | solution.py:168
  71.8 5.8 %collective-permute-start.10 = (bf16[128,1024]{1,0:T(8,128)(2,1)S(1)}, bf16[128,1024]{1,0:T(8,128)(2,1)S(1)}, u32[]{:S(2)}, u32[]{:S(2)}) collective-permute-start(bf16[128,1024]{1,0:T(8,128)(2,1)S(1)} %reduce_sum.24.refs_11_), channel_id=1, source_target_pairs={{0,1},{1,2},{2,3},{3,4},{4,5},{5,6},{6,7},{8,9},{9,10},{10,11},{11... | collective-permute-start | bytes 786440 | tf_op jit(solution)/shard_map/values_forward/ppermute | solution.py:164
  77.6 4.4 %collective-permute-start.9 = (bf16[128,1024]{1,0:T(8,128)(2,1)S(1)}, bf16[128,1024]{1,0:T(8,128)(2,1)S(1)}, u32[]{:S(2)}, u32[]{:S(2)}) collective-permute-start(bf16[128,1024]{1,0:T(8,128)(2,1)S(1)} %reduce_sum.24.refs_11_), channel_id=1, source_target_pairs={{0,2},{1,3},{2,4},{3,5},{4,6},{5,7},{8,10},{9,11},{10,12},{11,13},... | collective-permute-start | bytes 786440 | tf_op jit(solution)/shard_map/values_forward/ppermute | solution.py:164
  82.1 5.5 %collective-permute-done.7 = bf16[128,1024]{1,0:T(8,128)(2,1)} collective-permute-done((bf16[128,1024]{1,0:T(8,128)(2,1)}, bf16[128,1024]{1,0:T(8,128)(2,1)}, u32[]{:S(2)}, u32[]{:S(2)}) %collective-permute-start.7) | collective-permute-done | bytes 262176 | tf_op jit(solution)/shard_map/value_grad/ppermute | solution.py:168
  87.6 4.2 %collective-permute-done.8 = bf16[128,1024]{1,0:T(8,128)(2,1)} collective-permute-done((bf16[128,1024]{1,0:T(8,128)(2,1)}, bf16[128,1024]{1,0:T(8,128)(2,1)}, u32[]{:S(2)}, u32[]{:S(2)}) %collective-permute-start.8) | collective-permute-done | bytes 262176 | tf_op jit(solution)/shard_map/value_grad/ppermute | solution.py:168
  91.9 2.4 %collective-permute-start.14 = (bf16[2,128,1024]{2,1,0:T(8,128)(2,1)S(1)}, bf16[2,128,1024]{2,1,0:T(8,128)(2,1)S(1)}, u32[]{:S(2)}, u32[]{:S(2)}) collective-permute-start(bf16[2,128,1024]{2,1,0:T(8,128)(2,1)S(1)} %pad_maximum_fusion.4), channel_id=1, source_target_pairs={{0,2},{1,3},{2,4},{3,5},{4,6},{5,7},{8,10},{9,11},{10,12},{11,13},... | collective-permute-start | bytes 1572872 | tf_op jit(solution)/shard_map/values_forward/ppermute | solution.py:164
  94.3 1.3 add_convert_fusion.2
  95.6 1.5 collective-permute-start.11
  97.2 2.4 %collective-permute-start.12 = (bf16[128,1024]{1,0:T(8,128)(2,1)S(1)}, bf16[128,1024]{1,0:T(8,128)(2,1)S(1)}, u32[]{:S(2)}, u32[]{:S(2)}) collective-permute-start(bf16[128,1024]{1,0:T(8,128)(2,1)S(1)} %add_convert_fusion.2), channel_id=1, source_target_pairs={{0,64},{32,96},{64,0},{96,32},{1,65},{33,97},{65,1},{97,33},{2,66}... | collective-permute-start | bytes 786440 | tf_op jit(solution)/shard_map/value_grad/ppermute | solution.py:176
  99.6 1.2 collective-permute-start.13
  100.8 1.9 %collective-permute-done.11 = bf16[128,1024]{1,0:T(8,128)(2,1)S(1)} collective-permute-done((bf16[128,1024]{1,0:T(8,128)(2,1)S(1)}, bf16[128,1024]{1,0:T(8,128)(2,1)S(1)}, u32[]{:S(2)}, u32[]{:S(2)}) %collective-permute-start.11) | collective-permute-done | bytes 262176 | tf_op jit(solution)/shard_map/value_grad/ppermute | solution.py:176
  102.7 6.8 %collective-permute-done.12 = bf16[128,1024]{1,0:T(8,128)(2,1)S(1)} collective-permute-done((bf16[128,1024]{1,0:T(8,128)(2,1)S(1)}, bf16[128,1024]{1,0:T(8,128)(2,1)S(1)}, u32[]{:S(2)}, u32[]{:S(2)}) %collective-permute-start.12) | collective-permute-done | bytes 262176 | tf_op jit(solution)/shard_map/value_grad/ppermute | solution.py:176
  110.3 1.6 convolution_convert_fusion
  112.3 3.0 %collective-permute-start.15 = (bf16[640,1024]{1,0:T(8,128)(2,1)S(1)}, bf16[640,1024]{1,0:T(8,128)(2,1)S(1)}, u32[]{:S(2)}, u32[]{:S(2)}) collective-permute-start(bf16[640,1024]{1,0:T(8,128)(2,1)S(1)} %pad_maximum_fusion.2), channel_id=1, source_target_pairs={{0,8},{8,0},{1,9},{9,1},{2,10},{10,2},{3,11},{11,3},{4,12},{12,4},... | collective-permute-start | bytes 3932168 | tf_op jit(solution)/shard_map/weight_grad/ppermute | solution.py:172
  115.2 1.6 convolution_convert_fusion.1
  117.9 1.6 add_convert_fusion
  119.6 5.8 %all-to-all-start.2 = ((bf16[16,40,1024]{2,1,0:T(8,128)(2,1)}), bf16[16,40,1024]{2,1,0:T(8,128)(2,1)S(1)}, u32[]{:S(2)}, u32[]{:S(2)}) async-start(bf16[16,40,1024]{2,1,0:T(8,128)(2,1)} %bitcast.17), calls=%async_computation.2 | async-start | bytes 2621440 | tf_op jit(solution)/shard_map/weight_grad/all_to_all | solution.py:252
  126.3 1.9 collective-permute-start.16
  129.6 13.2 %grads.1 = (bf16[128,8192]{1,0:T(8,128)(2,1)}, bf16[128,8192]{1,0:T(8,128)(2,1)}, bf16[128,1024]{1,0:T(8,128)(2,1)}, bf16[128,1024]{1,0:T(8,128)(2,1)}, bf16[128...) custom-call(bf16[8,128,1024]{2,1,0:T(8,128)(2,1)} %get-tuple-element.60.refs_0_, ...), custom_call_target="tpu_custom_call" | custom-call | flops 5368709120 | bytes 16777216 | tf_op jit(solution)/shard_map/grads/pallas_call | solution.py:135
  143.3 3.2 %collective-permute-done.18 = bf16[128,1280]{1,0:T(8,128)(2,1)S(1)} collective-permute-done((bf16[128,1280]{1,0:T(8,128)(2,1)S(1)}, bf16[128,1280]{1,0:T(8,128)(2,1)S(1)}, u32[]{:S(2)}, u32[]{:S(2)}) %collective-permute-start.18) | collective-permute-done | bytes 327712 | tf_op jit(solution)/shard_map/input_grad/ppermute | solution.py:176
  147.5 6.6 %all-to-all-start.3 = ((bf16[8,40,1024]{2,1,0:T(8,128)(2,1)}), bf16[8,40,1024]{2,1,0:T(8,128)(2,1)S(1)}, u32[]{:S(2)}, u32[]{:S(2)}) async-start(bf16[8,40,1024]{2,1,0:T(8,128)(2,1)} %broadcast_in_dim.14), calls=%async_computation.3 | async-start | bytes 1310720 | tf_op jit(solution)/shard_map/weight_grad/all_to_all | solution.py:180
  154.1 1.3 collective-permute-start.19
  155.4 1.9 %collective-permute-start.20 = (bf16[128,1024]{1,0:T(8,128)(2,1)}, bf16[128,1024]{1,0:T(8,128)(2,1)S(1)}, u32[]{:S(2)}, u32[]{:S(2)}) collective-permute-start(bf16[128,1024]{1,0:T(8,128)(2,1)} %get-tuple-element.96), channel_id=1, source_target_pairs={{3,0},{4,1},{5,2},{6,3},{7,4},{11,8},{12,9},{13,10},{14,11},{15,12... | collective-permute-start | bytes 786440 | tf_op jit(solution)/shard_map/key_grad/ppermute | solution.py:168
  157.4 1.9 %collective-permute-start.21 = (bf16[128,1024]{1,0:T(8,128)(2,1)}, bf16[128,1024]{1,0:T(8,128)(2,1)S(1)}, u32[]{:S(2)}, u32[]{:S(2)}) collective-permute-start(bf16[128,1024]{1,0:T(8,128)(2,1)} %get-tuple-element.97), channel_id=1, source_target_pairs={{2,0},{3,1},{4,2},{5,3},{6,4},{7,5},{10,8},{11,9},{12,10},{13,11},... | collective-permute-start | bytes 786440 | tf_op jit(solution)/shard_map/key_grad/ppermute | solution.py:168
  159.3 1.9 %collective-permute-start.22 = (bf16[128,1024]{1,0:T(8,128)(2,1)S(1)}, bf16[128,1024]{1,0:T(8,128)(2,1)S(1)}, u32[]{:S(2)}, u32[]{:S(2)}) collective-permute-start(bf16[128,1024]{1,0:T(8,128)(2,1)S(1)} %copy-done.17), channel_id=1, source_target_pairs={{1,0},{2,1},{3,2},{4,3},{5,4},{6,5},{7,6},{9,8},{10,9},{11,10},{12... | collective-permute-start | bytes 786440 | tf_op jit(solution)/shard_map/key_grad/ppermute | solution.py:168
  162.5 6.3 %collective-permute-done.19 = bf16[128,1024]{1,0:T(8,128)(2,1)S(1)} collective-permute-done((bf16[128,1024]{1,0:T(8,128)(2,1)}, bf16[128,1024]{1,0:T(8,128)(2,1)S(1)}, u32[]{:S(2)}, u32[]{:S(2)}) %collective-permute-start.19) | collective-permute-done | bytes 262176 | tf_op jit(solution)/shard_map/key_grad/ppermute | solution.py:168
  168.8 5.6 %collective-permute-done.20 = bf16[128,1024]{1,0:T(8,128)(2,1)S(1)} collective-permute-done((bf16[128,1024]{1,0:T(8,128)(2,1)}, bf16[128,1024]{1,0:T(8,128)(2,1)S(1)}, u32[]{:S(2)}, u32[]{:S(2)}) %collective-permute-start.20) | collective-permute-done | bytes 262176 | tf_op jit(solution)/shard_map/key_grad/ppermute | solution.py:168
  174.4 5.5 %collective-permute-done.21 = bf16[128,1024]{1,0:T(8,128)(2,1)S(1)} collective-permute-done((bf16[128,1024]{1,0:T(8,128)(2,1)}, bf16[128,1024]{1,0:T(8,128)(2,1)S(1)}, u32[]{:S(2)}, u32[]{:S(2)}) %collective-permute-start.21) | collective-permute-done | bytes 262176 | tf_op jit(solution)/shard_map/key_grad/ppermute | solution.py:168
  179.9 6.9 %collective-permute-done.22 = bf16[128,1024]{1,0:T(8,128)(2,1)S(1)} collective-permute-done((bf16[128,1024]{1,0:T(8,128)(2,1)S(1)}, bf16[128,1024]{1,0:T(8,128)(2,1)S(1)}, u32[]{:S(2)}, u32[]{:S(2)}) %collective-permute-start.22) | collective-permute-done | bytes 262176 | tf_op jit(solution)/shard_map/key_grad/ppermute | solution.py:168
  187.7 1.2 bitcast_convert_fusion
  (78 shorter events, 12.5 us)
Async XLA Ops:
  3.1 4.3 %copy-start.3 = (bf16[320,1024]{1,0:T(8,128)(2,1)S(1)}, bf16[320,1024]{1,0:T(8,128)(2,1)}, u32[]{:S(2)}) copy-start(bf16[320,1024]{1,0:T(8,128)(2,1)} %param.7) | copy-start | bytes 1966084
  3.1 21.3 %all-to-all-start = ((bf16[128,4,1280]{0,2,1:T(8,128)(2,1)}), bf16[128,4,1280]{0,2,1:T(8,128)(2,1)S(1)}, u32[]{:S(2)}, u32[]{:S(2)}) async-start(bf16[128,4,1280]{0,2,1:T(8,128)(2,1)} %bitcast.2), calls=%async_computation | async-start | bytes 2621440 | tf_op jit(solution)/shard_map/hidden_columns/all_to_all | solution.py:210
  7.4 21.0 %collective-permute-start = (bf16[320,1024]{1,0:T(8,128)(2,1)S(1)}, bf16[320,1024]{1,0:T(8,128)(2,1)}, u32[]{:S(2)}, u32[]{:S(2)}) collective-permute-start(bf16[320,1024]{1,0:T(8,128)(2,1)S(1)} %copy-done.3), channel_id=1, source_target_pairs={{0,16},{16,0},{1,17},{17,1},{2,18},{18,2},{3,19},{19,3},{4,20},{20... | collective-permute-start | bytes 1966088 | tf_op jit(solution)/shard_map/weight_rows/ppermute | solution.py:172
  8.7 16.3 %collective-permute-start.1 = (bf16[128,1024]{1,0:T(8,128)(2,1)}, bf16[128,1024]{1,0:T(8,128)(2,1)S(1)}, u32[]{:S(2)}, u32[]{:S(2)}) collective-permute-start(bf16[128,1024]{1,0:T(8,128)(2,1)} %refs_7_.1), channel_id=1, source_target_pairs={{0,2},{1,3},{2,4},{3,5},{4,6},{5,7},{8,10},{9,11},{10,12},{11,13},... | collective-permute-start | bytes 786440 | tf_op jit(solution)/shard_map/keys/ppermute | solution.py:164
  11.8 16.1 %collective-permute-start.2 = (bf16[128,1024]{1,0:T(8,128)(2,1)}, bf16[128,1024]{1,0:T(8,128)(2,1)}, u32[]{:S(2)}, u32[]{:S(2)}) collective-permute-start(bf16[128,1024]{1,0:T(8,128)(2,1)} %refs_7_.1), channel_id=1, source_target_pairs={{0,1},{1,2},{2,3},{3,4},{4,5},{5,6},{6,7},{8,9},{9,10},{10,11},{11... | collective-permute-start | bytes 786440 | tf_op jit(solution)/shard_map/keys/ppermute | solution.py:164
  25.0 7.6 %copy-start.13 = (bf16[128,1024]{1,0:T(8,128)(2,1)}, bf16[128,1024]{1,0:T(8,128)(2,1)S(1)}, u32[]{:S(2)}) copy-start(bf16[128,1024]{1,0:T(8,128)(2,1)S(1)} %collective-permute-done.1.refs_4_.refs_5_) | copy-start | bytes 786436
  30.7 6.0 %collective-permute-start.4 = (bf16[2,320,1024]{2,1,0:T(8,128)(2,1)}, bf16[2,320,1024]{2,1,0:T(8,128)(2,1)}, u32[]{:S(2)}, u32[]{:S(2)}) collective-permute-start(bf16[2,320,1024]{2,1,0:T(8,128)(2,1)} %pad_maximum_fusion.1), channel_id=1, source_target_pairs={{0,8},{8,0},{1,9},{9,1},{2,10},{10,2},{3,11},{11,3},{4,12},{12,4},... | collective-permute-start | bytes 3932168 | tf_op jit(solution)/shard_map/weight_rows/ppermute | solution.py:172
  33.6 15.6 %collective-permute-start.3 = (bf16[2,128,1024]{2,1,0:T(8,128)(2,1)S(1)}, bf16[2,128,1024]{2,1,0:T(8,128)(2,1)}, u32[]{:S(2)}, u32[]{:S(2)}) collective-permute-start(bf16[2,128,1024]{2,1,0:T(8,128)(2,1)S(1)} %pad_maximum_fusion.3), channel_id=1, source_target_pairs={{0,2},{1,3},{2,4},{3,5},{4,6},{5,7},{8,10},{9,11},{10,12},{11,13},... | collective-permute-start | bytes 1572872 | tf_op jit(solution)/shard_map/keys/ppermute | solution.py:164
  38.5 2.5 %copy-start = (bf16[2,2,320,1024]{3,2,1,0:T(8,128)(2,1)}, bf16[2,2,320,1024]{3,2,1,0:T(8,128)(2,1)S(1)}, u32[]{:S(2)}) copy-start(bf16[2,2,320,1024]{3,2,1,0:T(8,128)(2,1)S(1)} %pad_maximum_fusion) | copy-start | bytes 7864324
  41.0 4.4 %copy-start.18 = (s32[1,8]{1,0:T(1,128)S(1)}, s32[1,8]{1,0:T(1,128)}, u32[]{:S(2)}) copy-start(s32[1,8]{1,0:T(1,128)} %param.11) | copy-start | bytes 100
  41.0 30.6 %all-to-all-start.1 = ((bf16[4,128,1024]{2,1,0:T(8,128)(2,1)}), bf16[4,128,1024]{2,1,0:T(8,128)(2,1)S(1)}, u32[]{:S(2)}, u32[]{:S(2)}) async-start(bf16[4,128,1024]{2,1,0:T(8,128)(2,1)} %bitcast.14), calls=%async_computation.1 | async-start | bytes 2097152 | tf_op jit(solution)/shard_map/values/all_to_all | solution.py:221
  64.3 30.0 %copy-start.4 = (f32[128,1024]{1,0:T(8,128)S(1)}, f32[128,1024]{1,0:T(8,128)}, u32[]{:S(2)}) copy-start(f32[128,1024]{1,0:T(8,128)} %get-tuple-element.74) | copy-start | bytes 1572868
  64.3 13.2 %collective-permute-start.5 = (bf16[128,1024]{1,0:T(8,128)(2,1)}, bf16[128,1024]{1,0:T(8,128)(2,1)S(1)}, u32[]{:S(2)}, u32[]{:S(2)}) collective-permute-start(bf16[128,1024]{1,0:T(8,128)(2,1)} %get-tuple-element.64), channel_id=1, source_target_pairs={{4,0},{5,1},{6,2},{7,3},{12,8},{13,9},{14,10},{15,11},{20,16},{21,... | collective-permute-start | bytes 786440 | tf_op jit(solution)/shard_map/value_grad/ppermute | solution.py:168
  65.8 16.3 %collective-permute-start.6 = (bf16[128,1024]{1,0:T(8,128)(2,1)}, bf16[128,1024]{1,0:T(8,128)(2,1)}, u32[]{:S(2)}, u32[]{:S(2)}) collective-permute-start(bf16[128,1024]{1,0:T(8,128)(2,1)} %get-tuple-element.65), channel_id=1, source_target_pairs={{3,0},{4,1},{5,2},{6,3},{7,4},{11,8},{12,9},{13,10},{14,11},{15,12... | collective-permute-start | bytes 786440 | tf_op jit(solution)/shard_map/value_grad/ppermute | solution.py:168
  67.7 19.9 %collective-permute-start.7 = (bf16[128,1024]{1,0:T(8,128)(2,1)}, bf16[128,1024]{1,0:T(8,128)(2,1)}, u32[]{:S(2)}, u32[]{:S(2)}) collective-permute-start(bf16[128,1024]{1,0:T(8,128)(2,1)} %get-tuple-element.66), channel_id=1, source_target_pairs={{2,0},{3,1},{4,2},{5,3},{6,4},{7,5},{10,8},{11,9},{12,10},{13,11},... | collective-permute-start | bytes 786440 | tf_op jit(solution)/shard_map/value_grad/ppermute | solution.py:168
  69.6 22.2 %collective-permute-start.8 = (bf16[128,1024]{1,0:T(8,128)(2,1)}, bf16[128,1024]{1,0:T(8,128)(2,1)}, u32[]{:S(2)}, u32[]{:S(2)}) collective-permute-start(bf16[128,1024]{1,0:T(8,128)(2,1)} %get-tuple-element.67), channel_id=1, source_target_pairs={{1,0},{2,1},{3,2},{4,3},{5,4},{6,5},{7,6},{9,8},{10,9},{11,10},{12... | collective-permute-start | bytes 786440 | tf_op jit(solution)/shard_map/value_grad/ppermute | solution.py:168
  71.8 23.8 %copy-start.12 = (bf16[128,1024]{1,0:T(8,128)(2,1)}, bf16[128,1024]{1,0:T(8,128)(2,1)S(1)}, u32[]{:S(2)}) copy-start(bf16[128,1024]{1,0:T(8,128)(2,1)S(1)} %reduce_sum.24.refs_11_) | copy-start | bytes 786436
  71.8 20.1 %collective-permute-start.10 = (bf16[128,1024]{1,0:T(8,128)(2,1)S(1)}, bf16[128,1024]{1,0:T(8,128)(2,1)S(1)}, u32[]{:S(2)}, u32[]{:S(2)}) collective-permute-start(bf16[128,1024]{1,0:T(8,128)(2,1)S(1)} %reduce_sum.24.refs_11_), channel_id=1, source_target_pairs={{0,1},{1,2},{2,3},{3,4},{4,5},{5,6},{6,7},{8,9},{9,10},{10,11},{11... | collective-permute-start | bytes 786440 | tf_op jit(solution)/shard_map/values_forward/ppermute | solution.py:164
  77.6 14.3 %collective-permute-start.9 = (bf16[128,1024]{1,0:T(8,128)(2,1)S(1)}, bf16[128,1024]{1,0:T(8,128)(2,1)S(1)}, u32[]{:S(2)}, u32[]{:S(2)}) collective-permute-start(bf16[128,1024]{1,0:T(8,128)(2,1)S(1)} %reduce_sum.24.refs_11_), channel_id=1, source_target_pairs={{0,2},{1,3},{2,4},{3,5},{4,6},{5,7},{8,10},{9,11},{10,12},{11,13},... | collective-permute-start | bytes 786440 | tf_op jit(solution)/shard_map/values_forward/ppermute | solution.py:164
  91.8 2.5 %copy-start.14 = (bf16[128,1024]{1,0:T(8,128)(2,1)}, bf16[128,1024]{1,0:T(8,128)(2,1)S(1)}, u32[]{:S(2)}) copy-start(bf16[128,1024]{1,0:T(8,128)(2,1)S(1)} %collective-permute-done.10.refs_10_) | copy-start | bytes 786436
  91.8 3.8 %copy-start.15 = (bf16[128,1024]{1,0:T(8,128)(2,1)}, bf16[128,1024]{1,0:T(8,128)(2,1)S(1)}, u32[]{:S(2)}) copy-start(bf16[128,1024]{1,0:T(8,128)(2,1)S(1)} %collective-permute-done.9.refs_9_) | copy-start | bytes 786436
  91.9 17.6 %collective-permute-start.14 = (bf16[2,128,1024]{2,1,0:T(8,128)(2,1)S(1)}, bf16[2,128,1024]{2,1,0:T(8,128)(2,1)S(1)}, u32[]{:S(2)}, u32[]{:S(2)}) collective-permute-start(bf16[2,128,1024]{2,1,0:T(8,128)(2,1)S(1)} %pad_maximum_fusion.4), channel_id=1, source_target_pairs={{0,2},{1,3},{2,4},{3,5},{4,6},{5,7},{8,10},{9,11},{10,12},{11,13},... | collective-permute-start | bytes 1572872 | tf_op jit(solution)/shard_map/values_forward/ppermute | solution.py:164
  95.6 7.1 %collective-permute-start.11 = (bf16[128,1024]{1,0:T(8,128)(2,1)S(1)}, bf16[128,1024]{1,0:T(8,128)(2,1)S(1)}, u32[]{:S(2)}, u32[]{:S(2)}) collective-permute-start(bf16[128,1024]{1,0:T(8,128)(2,1)S(1)} %add_convert_fusion.2), channel_id=1, source_target_pairs={{0,32},{32,64},{64,96},{96,0},{1,33},{33,65},{65,97},{97,1},{2,34}... | collective-permute-start | bytes 786440 | tf_op jit(solution)/shard_map/value_grad/ppermute | solution.py:176
  97.2 12.4 %collective-permute-start.12 = (bf16[128,1024]{1,0:T(8,128)(2,1)S(1)}, bf16[128,1024]{1,0:T(8,128)(2,1)S(1)}, u32[]{:S(2)}, u32[]{:S(2)}) collective-permute-start(bf16[128,1024]{1,0:T(8,128)(2,1)S(1)} %add_convert_fusion.2), channel_id=1, source_target_pairs={{0,64},{32,96},{64,0},{96,32},{1,65},{33,97},{65,1},{97,33},{2,66}... | collective-permute-start | bytes 786440 | tf_op jit(solution)/shard_map/value_grad/ppermute | solution.py:176
  99.6 10.0 %collective-permute-start.13 = (bf16[128,1024]{1,0:T(8,128)(2,1)S(1)}, bf16[128,1024]{1,0:T(8,128)(2,1)S(1)}, u32[]{:S(2)}, u32[]{:S(2)}) collective-permute-start(bf16[128,1024]{1,0:T(8,128)(2,1)S(1)} %add_convert_fusion.2), channel_id=1, source_target_pairs={{0,96},{32,0},{64,32},{96,64},{1,97},{33,1},{65,33},{97,65},{2,98}... | collective-permute-start | bytes 786440 | tf_op jit(solution)/shard_map/value_grad/ppermute | solution.py:176
  109.5 0.8 copy-start.16
  112.2 3.1 %copy-start.1 = (bf16[2,2,320,1024]{3,2,1,0:T(8,128)(2,1)S(1)}, bf16[2,2,320,1024]{3,2,1,0:T(8,128)(2,1)}, u32[]{:S(2)}) copy-start(bf16[2,2,320,1024]{3,2,1,0:T(8,128)(2,1)} %copy-done) | copy-start | bytes 7864324
  112.3 5.6 %collective-permute-start.15 = (bf16[640,1024]{1,0:T(8,128)(2,1)S(1)}, bf16[640,1024]{1,0:T(8,128)(2,1)S(1)}, u32[]{:S(2)}, u32[]{:S(2)}) collective-permute-start(bf16[640,1024]{1,0:T(8,128)(2,1)S(1)} %pad_maximum_fusion.2), channel_id=1, source_target_pairs={{0,8},{8,0},{1,9},{9,1},{2,10},{10,2},{3,11},{11,3},{4,12},{12,4},... | collective-permute-start | bytes 3932168 | tf_op jit(solution)/shard_map/weight_grad/ppermute | solution.py:172
  119.6 23.4 %all-to-all-start.2 = ((bf16[16,40,1024]{2,1,0:T(8,128)(2,1)}), bf16[16,40,1024]{2,1,0:T(8,128)(2,1)S(1)}, u32[]{:S(2)}, u32[]{:S(2)}) async-start(bf16[16,40,1024]{2,1,0:T(8,128)(2,1)} %bitcast.17), calls=%async_computation.2 | async-start | bytes 2621440 | tf_op jit(solution)/shard_map/weight_grad/all_to_all | solution.py:252
  126.3 17.0 %collective-permute-start.16 = (bf16[128,1280]{1,0:T(8,128)(2,1)}, bf16[128,1280]{1,0:T(8,128)(2,1)S(1)}, u32[]{:S(2)}, u32[]{:S(2)}) collective-permute-start(bf16[128,1280]{1,0:T(8,128)(2,1)} %get-tuple-element.113), channel_id=1, source_target_pairs={{0,96},{32,0},{64,32},{96,64},{1,97},{33,1},{65,33},{97,65},{2,98}... | collective-permute-start | bytes 983048 | tf_op jit(solution)/shard_map/input_grad/ppermute | solution.py:176
  128.2 15.1 %collective-permute-start.17 = (bf16[128,1280]{1,0:T(8,128)(2,1)}, bf16[128,1280]{1,0:T(8,128)(2,1)S(1)}, u32[]{:S(2)}, u32[]{:S(2)}) collective-permute-start(bf16[128,1280]{1,0:T(8,128)(2,1)} %get-tuple-element.112), channel_id=1, source_target_pairs={{0,64},{32,96},{64,0},{96,32},{1,65},{33,97},{65,1},{97,33},{2,66}... | collective-permute-start | bytes 983048 | tf_op jit(solution)/shard_map/input_grad/ppermute | solution.py:176
  129.0 17.5 %collective-permute-start.18 = (bf16[128,1280]{1,0:T(8,128)(2,1)S(1)}, bf16[128,1280]{1,0:T(8,128)(2,1)S(1)}, u32[]{:S(2)}, u32[]{:S(2)}) collective-permute-start(bf16[128,1280]{1,0:T(8,128)(2,1)S(1)} %get-tuple-element.111), channel_id=1, source_target_pairs={{0,32},{32,64},{64,96},{96,0},{1,33},{33,65},{65,97},{97,1},{2,34}... | collective-permute-start | bytes 983048 | tf_op jit(solution)/shard_map/input_grad/ppermute | solution.py:176
  143.2 16.1 %copy-start.17 = (bf16[128,1024]{1,0:T(8,128)(2,1)S(1)}, bf16[128,1024]{1,0:T(8,128)(2,1)}, u32[]{:S(2)}) copy-start(bf16[128,1024]{1,0:T(8,128)(2,1)} %get-tuple-element.98) | copy-start | bytes 786436
  143.3 16.0 %copy-start.6 = (bf16[128,1280]{1,0:T(8,128)(2,1)}, bf16[128,1280]{1,0:T(8,128)(2,1)S(1)}, u32[]{:S(2)}) copy-start(bf16[128,1280]{1,0:T(8,128)(2,1)S(1)} %collective-permute-done.16) | copy-start | bytes 983044
  143.3 16.0 %copy-start.8 = (bf16[128,1280]{1,0:T(8,128)(2,1)}, bf16[128,1280]{1,0:T(8,128)(2,1)S(1)}, u32[]{:S(2)}) copy-start(bf16[128,1280]{1,0:T(8,128)(2,1)S(1)} %collective-permute-done.17) | copy-start | bytes 983044
  146.5 14.7 %copy-start.10 = (bf16[128,1280]{1,0:T(8,128)(2,1)}, bf16[128,1280]{1,0:T(8,128)(2,1)S(1)}, u32[]{:S(2)}) copy-start(bf16[128,1280]{1,0:T(8,128)(2,1)S(1)} %collective-permute-done.18) | copy-start | bytes 983044
  147.5 40.2 %all-to-all-start.3 = ((bf16[8,40,1024]{2,1,0:T(8,128)(2,1)}), bf16[8,40,1024]{2,1,0:T(8,128)(2,1)S(1)}, u32[]{:S(2)}, u32[]{:S(2)}) async-start(bf16[8,40,1024]{2,1,0:T(8,128)(2,1)} %broadcast_in_dim.14), calls=%async_computation.3 | async-start | bytes 1310720 | tf_op jit(solution)/shard_map/weight_grad/all_to_all | solution.py:180
  154.1 14.7 %collective-permute-start.19 = (bf16[128,1024]{1,0:T(8,128)(2,1)}, bf16[128,1024]{1,0:T(8,128)(2,1)S(1)}, u32[]{:S(2)}, u32[]{:S(2)}) collective-permute-start(bf16[128,1024]{1,0:T(8,128)(2,1)} %get-tuple-element.95), channel_id=1, source_target_pairs={{4,0},{5,1},{6,2},{7,3},{12,8},{13,9},{14,10},{15,11},{20,16},{21,... | collective-permute-start | bytes 786440 | tf_op jit(solution)/shard_map/key_grad/ppermute | solution.py:168
  155.4 19.0 %collective-permute-start.20 = (bf16[128,1024]{1,0:T(8,128)(2,1)}, bf16[128,1024]{1,0:T(8,128)(2,1)S(1)}, u32[]{:S(2)}, u32[]{:S(2)}) collective-permute-start(bf16[128,1024]{1,0:T(8,128)(2,1)} %get-tuple-element.96), channel_id=1, source_target_pairs={{3,0},{4,1},{5,2},{6,3},{7,4},{11,8},{12,9},{13,10},{14,11},{15,12... | collective-permute-start | bytes 786440 | tf_op jit(solution)/shard_map/key_grad/ppermute | solution.py:168
  157.4 22.6 %collective-permute-start.21 = (bf16[128,1024]{1,0:T(8,128)(2,1)}, bf16[128,1024]{1,0:T(8,128)(2,1)S(1)}, u32[]{:S(2)}, u32[]{:S(2)}) collective-permute-start(bf16[128,1024]{1,0:T(8,128)(2,1)} %get-tuple-element.97), channel_id=1, source_target_pairs={{2,0},{3,1},{4,2},{5,3},{6,4},{7,5},{10,8},{11,9},{12,10},{13,11},... | collective-permute-start | bytes 786440 | tf_op jit(solution)/shard_map/key_grad/ppermute | solution.py:168
  159.3 27.5 %collective-permute-start.22 = (bf16[128,1024]{1,0:T(8,128)(2,1)S(1)}, bf16[128,1024]{1,0:T(8,128)(2,1)S(1)}, u32[]{:S(2)}, u32[]{:S(2)}) collective-permute-start(bf16[128,1024]{1,0:T(8,128)(2,1)S(1)} %copy-done.17), channel_id=1, source_target_pairs={{1,0},{2,1},{3,2},{4,3},{5,4},{6,5},{7,6},{9,8},{10,9},{11,10},{12... | collective-permute-start | bytes 786440 | tf_op jit(solution)/shard_map/key_grad/ppermute | solution.py:168
  161.2 1.0 copy-start.7
  161.3 1.1 copy-start.9
  161.4 1.1 copy-start.11
  161.4 25.4 %copy-start.5 = (f32[128,1024]{1,0:T(8,128)S(1)}, f32[128,1024]{1,0:T(8,128)}, u32[]{:S(2)}) copy-start(f32[128,1024]{1,0:T(8,128)} %get-tuple-element.99) | copy-start | bytes 1572868
  162.5 26.4 %copy-start.2 = (bf16[128,5120]{1,0:T(8,128)(2,1)}, bf16[128,5120]{1,0:T(8,128)(2,1)S(1)}, u32[]{:S(2)}) copy-start(bf16[128,5120]{1,0:T(8,128)(2,1)S(1)} %constant_dynamic-update-slice_fusion.4) | copy-start | bytes 3932164

commit v6 on v5

--- a/solution.py
+++ b/solution.py
@@ -230,7 +230,8 @@
         vgrad = sum(d.astype(f32) for d in dv).astype(bf)
         vys = [vgrad] + [along_y(vgrad, k) for k in (1, 2, 3)]
     with jax.named_scope("values_forward"):
-        v01 = forward(jnp.stack([v2, v3]), 2)
+        pair, _ = lax.optimization_barrier(([v2, v3], vgrad))
+        v01 = forward(jnp.stack(pair), 2)
         vys, v01 = lax.optimization_barrier((vys, v01))
         vy = jnp.concatenate(vys)
         vs = (v01, v2, v3, values)

time: 190 us -> 189 us (level)
  no operation moved by 1% of the time
where the time goes in v6:
time: 189 us; the launch traced here: 188 us
  starting transfers between devices  70.9 us (38%)
  waiting for transfers between devices  64.2 us (34%)
  Pallas kernels  28.4 us (15%)
  other arithmetic  11.5 us (6%)
  local copies, waits for them, and re-layouts  6.57 us (3%)
  matrix products  5.62 us (3%)
    ppermute x8, waiting for transfers between devices, backward(): return lax.ppermute(x, ('x', 'zh'), [(i + k, i) for i in range(N - k)])  34.1 us
    pallas_call x2, Pallas kernels, call(): pl.pallas_call(heads, grid=(KV // hp,), in_specs=[spec(k) for k in ins],...  28.4 us
    ppermute x6, starting transfers between devices, forward(): return lax.ppermute(x, ('x', 'zh'), [(i, i + k) for i in range(N - k)])  20.9 us
    ppermute x8, starting transfers between devices, backward(): return lax.ppermute(x, ('x', 'zh'), [(i + k, i) for i in range(N - k)])  14.2 us
    ppermute x6, waiting for transfers between devices, along_y(): return lax.ppermute(x, 'y', [(i, (i + k) % 4) for i in range(4)])  11.9 us
    all_to_all x1, waiting for transfers between devices, body(): lax.all_to_all(hidden.reshape(rows, 4, depth), 'y', 1, 0, tiled=True)  10.3 us
    ppermute x6, starting transfers between devices, along_y(): return lax.ppermute(x, 'y', [(i, (i + k) % 4) for i in range(4)])  8.39 us
    all_to_all x1, starting transfers between devices, over_seq(): return lax.all_to_all(x, ('x', 'zh'), 0, 0, tiled=True)  6.65 us
  transfers between devices with their start and end apart: 27, of which 15 were waited for; matrix products, arithmetic and copies ran while one was open for 6% of the time, Pallas kernels for 15%

profile of v6, /device:TPU:67, one launch (start us, length us, event | category | flops | bytes accessed | tf_op | source)
XLA Modules:
  0.0 188.4 jit_solution(1287328979217024228)
XLA Ops:
  0.6 2.4 %copy.12 = bf16[128,5120]{0,1:T(8,128)(2,1)} copy(bf16[128,5120]{1,0:T(8,128)(2,1)} %param.6) | data formatting | bytes 2621440 | tf_op args[0]
  3.1 4.3 %all-to-all-start = ((bf16[128,4,1280]{0,2,1:T(8,128)(2,1)}), bf16[128,4,1280]{0,2,1:T(8,128)(2,1)S(1)}, u32[]{:S(2)}, u32[]{:S(2)}) async-start(bf16[128,4,1280]{0,2,1:T(8,128)(2,1)} %bitcast.2), calls=%async_computation | async-start | bytes 2621440 | tf_op jit(solution)/shard_map/hidden_columns/all_to_all | solution.py:210
  7.4 1.3 collective-permute-start
  8.7 3.1 %collective-permute-start.1 = (bf16[128,1024]{1,0:T(8,128)(2,1)}, bf16[128,1024]{1,0:T(8,128)(2,1)S(1)}, u32[]{:S(2)}, u32[]{:S(2)}) collective-permute-start(bf16[128,1024]{1,0:T(8,128)(2,1)} %refs_7_.1), channel_id=1, source_target_pairs={{0,2},{1,3},{2,4},{3,5},{4,6},{5,7},{8,10},{9,11},{10,12},{11,13},... | collective-permute-start | bytes 786440 | tf_op jit(solution)/shard_map/keys/ppermute | solution.py:164
  11.8 2.2 %collective-permute-start.2 = (bf16[128,1024]{1,0:T(8,128)(2,1)}, bf16[128,1024]{1,0:T(8,128)(2,1)}, u32[]{:S(2)}, u32[]{:S(2)}) collective-permute-start(bf16[128,1024]{1,0:T(8,128)(2,1)} %refs_7_.1), channel_id=1, source_target_pairs={{0,1},{1,2},{2,3},{3,4},{4,5},{5,6},{6,7},{8,9},{9,10},{10,11},{11... | collective-permute-start | bytes 786440 | tf_op jit(solution)/shard_map/keys/ppermute | solution.py:164
  14.1 10.3 %all-to-all-done = bf16[128,4,1280]{0,2,1:T(8,128)(2,1)S(1)} async-done(((bf16[128,4,1280]{0,2,1:T(8,128)(2,1)}), bf16[128,4,1280]{0,2,1:T(8,128)(2,1)S(1)}, u32[]{:S(2)}, u32[]{:S(2)}) %all-to-all-start) | async-done | bytes 1310752 | tf_op jit(solution)/shard_map/hidden_columns/all_to_all | solution.py:210
  25.0 2.9 %collective-permute-done.2.refs_5_.refs_6_ = bf16[128,1024]{1,0:T(8,128)(2,1)} collective-permute-done((bf16[128,1024]{1,0:T(8,128)(2,1)}, bf16[128,1024]{1,0:T(8,128)(2,1)}, u32[]{:S(2)}, u32[]{:S(2)}) %collective-permute-start.2) | collective-permute-done | bytes 262176 | tf_op jit(solution)/shard_map/keys/ppermute | solution.py:164
  28.4 1.2 select_bitcast_fusion.3
  30.7 1.9 collective-permute-start.4
  33.6 3.1 %collective-permute-start.3 = (bf16[2,128,1024]{2,1,0:T(8,128)(2,1)S(1)}, bf16[2,128,1024]{2,1,0:T(8,128)(2,1)}, u32[]{:S(2)}, u32[]{:S(2)}) collective-permute-start(bf16[2,128,1024]{2,1,0:T(8,128)(2,1)S(1)} %pad_maximum_fusion.3), channel_id=1, source_target_pairs={{0,2},{1,3},{2,4},{3,5},{4,6},{5,7},{8,10},{9,11},{10,12},{11,13},... | collective-permute-start | bytes 1572872 | tf_op jit(solution)/shard_map/keys/ppermute | solution.py:164
  36.7 1.5 select_bitcast_fusion.1
  38.5 2.5 %convolution_convert_fusion.2 = bf16[512,1024]{1,0:T(8,128)(2,1)} fusion(bf16[512,1280]{1,0:T(8,128)(2,1)S(1)} %bitcast.32, bf16[1280,1024]{1,0:T(8,128)(2,1)S(1)} %bitcast.35), kind=kOutput, calls=%fused_computation.4 | convolution fusion | flops 1342701568 | bytes 4980736 | tf_op jit(solution)/shard_map/values/dot_general | solution.py:219
  41.0 4.4 %all-to-all-start.1 = ((bf16[4,128,1024]{2,1,0:T(8,128)(2,1)}), bf16[4,128,1024]{2,1,0:T(8,128)(2,1)S(1)}, u32[]{:S(2)}, u32[]{:S(2)}) async-start(bf16[4,128,1024]{2,1,0:T(8,128)(2,1)} %bitcast.14), calls=%async_computation.1 | async-start | bytes 2097152 | tf_op jit(solution)/shard_map/values/all_to_all | solution.py:221
  46.0 3.2 %collective-permute-done.3.refs_3_.refs_4_ = bf16[2,128,1024]{2,1,0:T(8,128)(2,1)} collective-permute-done((bf16[2,128,1024]{2,1,0:T(8,128)(2,1)S(1)}, bf16[2,128,1024]{2,1,0:T(8,128)(2,1)}, u32[]{:S(2)}, u32[]{:S(2)}) %collective-permute-start.3) | collective-permute-done | bytes 524320 | tf_op jit(solution)/shard_map/keys/ppermute | solution.py:164
  49.2 15.2 %probs.1 = (bf16[8,640,1024]{2,1,0:T(8,128)(2,1)}, bf16[8,128,1024]{2,1,0:T(8,128)(2,1)}, bf16[8,128,1024]{2,1,0:T(8,128)(2,1)}, f32[8,8,1024]{2,1,0:T(8,128)}, ...) custom-call(s32[9]{0:T(128)} %pad_add_fusion.refs_0_, ...), custom_call_target="tpu_custom_call" | custom-call | flops 2684354560 | bytes 16777216 | tf_op jit(solution)/shard_map/probs/pallas_call | solution.py:135
  64.3 1.4 collective-permute-start.5
  65.8 1.9 %collective-permute-start.6 = (bf16[128,1024]{1,0:T(8,128)(2,1)}, bf16[128,1024]{1,0:T(8,128)(2,1)}, u32[]{:S(2)}, u32[]{:S(2)}) collective-permute-start(bf16[128,1024]{1,0:T(8,128)(2,1)} %get-tuple-element.67), channel_id=1, source_target_pairs={{3,0},{4,1},{5,2},{6,3},{7,4},{11,8},{12,9},{13,10},{14,11},{15,12... | collective-permute-start | bytes 786440 | tf_op jit(solution)/shard_map/value_grad/ppermute | solution.py:168
  67.7 1.9 %collective-permute-start.7 = (bf16[128,1024]{1,0:T(8,128)(2,1)}, bf16[128,1024]{1,0:T(8,128)(2,1)}, u32[]{:S(2)}, u32[]{:S(2)}) collective-permute-start(bf16[128,1024]{1,0:T(8,128)(2,1)} %get-tuple-element.68), channel_id=1, source_target_pairs={{2,0},{3,1},{4,2},{5,3},{6,4},{7,5},{10,8},{11,9},{12,10},{13,11},... | collective-permute-start | bytes 786440 | tf_op jit(solution)/shard_map/value_grad/ppermute | solution.py:168
  69.6 1.9 %collective-permute-start.8 = (bf16[128,1024]{1,0:T(8,128)(2,1)}, bf16[128,1024]{1,0:T(8,128)(2,1)}, u32[]{:S(2)}, u32[]{:S(2)}) collective-permute-start(bf16[128,1024]{1,0:T(8,128)(2,1)} %get-tuple-element.69), channel_id=1, source_target_pairs={{1,0},{2,1},{3,2},{4,3},{5,4},{6,5},{7,6},{9,8},{10,9},{11,10},{12... | collective-permute-start | bytes 786440 | tf_op jit(solution)/shard_map/value_grad/ppermute | solution.py:168
  71.8 5.8 %collective-permute-start.10 = (bf16[128,1024]{1,0:T(8,128)(2,1)S(1)}, bf16[128,1024]{1,0:T(8,128)(2,1)S(1)}, u32[]{:S(2)}, u32[]{:S(2)}) collective-permute-start(bf16[128,1024]{1,0:T(8,128)(2,1)S(1)} %reduce_sum.24.refs_11_), channel_id=1, source_target_pairs={{0,1},{1,2},{2,3},{3,4},{4,5},{5,6},{6,7},{8,9},{9,10},{10,11},{11... | collective-permute-start | bytes 786440 | tf_op jit(solution)/shard_map/values_forward/ppermute | solution.py:164
  77.6 4.4 %collective-permute-start.9 = (bf16[128,1024]{1,0:T(8,128)(2,1)S(1)}, bf16[128,1024]{1,0:T(8,128)(2,1)S(1)}, u32[]{:S(2)}, u32[]{:S(2)}) collective-permute-start(bf16[128,1024]{1,0:T(8,128)(2,1)S(1)} %reduce_sum.24.refs_11_), channel_id=1, source_target_pairs={{0,2},{1,3},{2,4},{3,5},{4,6},{5,7},{8,10},{9,11},{10,12},{11,13},... | collective-permute-start | bytes 786440 | tf_op jit(solution)/shard_map/values_forward/ppermute | solution.py:164
  82.0 5.6 %collective-permute-done.7 = bf16[128,1024]{1,0:T(8,128)(2,1)} collective-permute-done((bf16[128,1024]{1,0:T(8,128)(2,1)}, bf16[128,1024]{1,0:T(8,128)(2,1)}, u32[]{:S(2)}, u32[]{:S(2)}) %collective-permute-start.7) | collective-permute-done | bytes 262176 | tf_op jit(solution)/shard_map/value_grad/ppermute | solution.py:168
  87.6 4.2 %collective-permute-done.8 = bf16[128,1024]{1,0:T(8,128)(2,1)} collective-permute-done((bf16[128,1024]{1,0:T(8,128)(2,1)}, bf16[128,1024]{1,0:T(8,128)(2,1)}, u32[]{:S(2)}, u32[]{:S(2)}) %collective-permute-start.8) | collective-permute-done | bytes 262176 | tf_op jit(solution)/shard_map/value_grad/ppermute | solution.py:168
  91.9 1.5 add_convert_fusion.2
  93.4 2.3 %collective-permute-start.14 = (bf16[2,128,1024]{2,1,0:T(8,128)(2,1)S(1)}, bf16[2,128,1024]{2,1,0:T(8,128)(2,1)S(1)}, u32[]{:S(2)}, u32[]{:S(2)}) collective-permute-start(bf16[2,128,1024]{2,1,0:T(8,128)(2,1)S(1)} %pad_maximum_fusion.4), channel_id=1, source_target_pairs={{0,2},{1,3},{2,4},{3,5},{4,6},{5,7},{8,10},{9,11},{10,12},{11,13},... | collective-permute-start | bytes 1572872 | tf_op jit(solution)/shard_map/values_forward/ppermute | solution.py:164
  95.8 1.5 collective-permute-start.11
  97.3 2.4 %collective-permute-start.12 = (bf16[128,1024]{1,0:T(8,128)(2,1)S(1)}, bf16[128,1024]{1,0:T(8,128)(2,1)S(1)}, u32[]{:S(2)}, u32[]{:S(2)}) collective-permute-start(bf16[128,1024]{1,0:T(8,128)(2,1)S(1)} %add_convert_fusion.2), channel_id=1, source_target_pairs={{0,64},{32,96},{64,0},{96,32},{1,65},{33,97},{65,1},{97,33},{2,66}... | collective-permute-start | bytes 786440 | tf_op jit(solution)/shard_map/value_grad/ppermute | solution.py:176
  99.7 1.2 collective-permute-start.13
  101.0 1.9 %collective-permute-done.11 = bf16[128,1024]{1,0:T(8,128)(2,1)S(1)} collective-permute-done((bf16[128,1024]{1,0:T(8,128)(2,1)S(1)}, bf16[128,1024]{1,0:T(8,128)(2,1)S(1)}, u32[]{:S(2)}, u32[]{:S(2)}) %collective-permute-start.11) | collective-permute-done | bytes 262176 | tf_op jit(solution)/shard_map/value_grad/ppermute | solution.py:176
  102.9 6.8 %collective-permute-done.12 = bf16[128,1024]{1,0:T(8,128)(2,1)S(1)} collective-permute-done((bf16[128,1024]{1,0:T(8,128)(2,1)S(1)}, bf16[128,1024]{1,0:T(8,128)(2,1)S(1)}, u32[]{:S(2)}, u32[]{:S(2)}) %collective-permute-start.12) | collective-permute-done | bytes 262176 | tf_op jit(solution)/shard_map/value_grad/ppermute | solution.py:176
  109.8 1.6 convolution_convert_fusion
  111.8 3.0 %collective-permute-start.15 = (bf16[640,1024]{1,0:T(8,128)(2,1)S(1)}, bf16[640,1024]{1,0:T(8,128)(2,1)S(1)}, u32[]{:S(2)}, u32[]{:S(2)}) collective-permute-start(bf16[640,1024]{1,0:T(8,128)(2,1)S(1)} %pad_maximum_fusion.2), channel_id=1, source_target_pairs={{0,8},{8,0},{1,9},{9,1},{2,10},{10,2},{3,11},{11,3},{4,12},{12,4},... | collective-permute-start | bytes 3932168 | tf_op jit(solution)/shard_map/weight_grad/ppermute | solution.py:172
  114.8 1.6 convolution_convert_fusion.1
  117.4 1.6 add_convert_fusion
  119.1 5.8 %all-to-all-start.2 = ((bf16[16,40,1024]{2,1,0:T(8,128)(2,1)}), bf16[16,40,1024]{2,1,0:T(8,128)(2,1)S(1)}, u32[]{:S(2)}, u32[]{:S(2)}) async-start(bf16[16,40,1024]{2,1,0:T(8,128)(2,1)} %bitcast.17), calls=%async_computation.2 | async-start | bytes 2621440 | tf_op jit(solution)/shard_map/weight_grad/all_to_all | solution.py:253
  125.8 1.9 collective-permute-start.16
  129.1 13.2 %grads.1 = (bf16[128,8192]{1,0:T(8,128)(2,1)}, bf16[128,8192]{1,0:T(8,128)(2,1)}, bf16[128,1024]{1,0:T(8,128)(2,1)}, bf16[128,1024]{1,0:T(8,128)(2,1)}, bf16[128...) custom-call(bf16[8,128,1024]{2,1,0:T(8,128)(2,1)} %get-tuple-element.62.refs_0_, ...), custom_call_target="tpu_custom_call" | custom-call | flops 5368709120 | bytes 16777216 | tf_op jit(solution)/shard_map/grads/pallas_call | solution.py:135
  142.8 3.2 %collective-permute-done.18 = bf16[128,1280]{1,0:T(8,128)(2,1)S(1)} collective-permute-done((bf16[128,1280]{1,0:T(8,128)(2,1)S(1)}, bf16[128,1280]{1,0:T(8,128)(2,1)S(1)}, u32[]{:S(2)}, u32[]{:S(2)}) %collective-permute-start.18) | collective-permute-done | bytes 327712 | tf_op jit(solution)/shard_map/input_grad/ppermute | solution.py:176
  147.0 6.6 %all-to-all-start.3 = ((bf16[8,40,1024]{2,1,0:T(8,128)(2,1)}), bf16[8,40,1024]{2,1,0:T(8,128)(2,1)S(1)}, u32[]{:S(2)}, u32[]{:S(2)}) async-start(bf16[8,40,1024]{2,1,0:T(8,128)(2,1)} %broadcast_in_dim.14), calls=%async_computation.3 | async-start | bytes 1310720 | tf_op jit(solution)/shard_map/weight_grad/all_to_all | solution.py:180
  153.6 1.3 collective-permute-start.19
  154.9 1.9 %collective-permute-start.20 = (bf16[128,1024]{1,0:T(8,128)(2,1)}, bf16[128,1024]{1,0:T(8,128)(2,1)S(1)}, u32[]{:S(2)}, u32[]{:S(2)}) collective-permute-start(bf16[128,1024]{1,0:T(8,128)(2,1)} %get-tuple-element.100), channel_id=1, source_target_pairs={{3,0},{4,1},{5,2},{6,3},{7,4},{11,8},{12,9},{13,10},{14,11},{15,12... | collective-permute-start | bytes 786440 | tf_op jit(solution)/shard_map/key_grad/ppermute | solution.py:168
  156.9 1.9 %collective-permute-start.21 = (bf16[128,1024]{1,0:T(8,128)(2,1)}, bf16[128,1024]{1,0:T(8,128)(2,1)S(1)}, u32[]{:S(2)}, u32[]{:S(2)}) collective-permute-start(bf16[128,1024]{1,0:T(8,128)(2,1)} %get-tuple-element.101), channel_id=1, source_target_pairs={{2,0},{3,1},{4,2},{5,3},{6,4},{7,5},{10,8},{11,9},{12,10},{13,11},... | collective-permute-start | bytes 786440 | tf_op jit(solution)/shard_map/key_grad/ppermute | solution.py:168
  158.8 1.9 %collective-permute-start.22 = (bf16[128,1024]{1,0:T(8,128)(2,1)S(1)}, bf16[128,1024]{1,0:T(8,128)(2,1)S(1)}, u32[]{:S(2)}, u32[]{:S(2)}) collective-permute-start(bf16[128,1024]{1,0:T(8,128)(2,1)S(1)} %copy-done.17), channel_id=1, source_target_pairs={{1,0},{2,1},{3,2},{4,3},{5,4},{6,5},{7,6},{9,8},{10,9},{11,10},{12... | collective-permute-start | bytes 786440 | tf_op jit(solution)/shard_map/key_grad/ppermute | solution.py:168
  162.0 6.3 %collective-permute-done.19 = bf16[128,1024]{1,0:T(8,128)(2,1)S(1)} collective-permute-done((bf16[128,1024]{1,0:T(8,128)(2,1)}, bf16[128,1024]{1,0:T(8,128)(2,1)S(1)}, u32[]{:S(2)}, u32[]{:S(2)}) %collective-permute-start.19) | collective-permute-done | bytes 262176 | tf_op jit(solution)/shard_map/key_grad/ppermute | solution.py:168
  168.3 5.6 %collective-permute-done.20 = bf16[128,1024]{1,0:T(8,128)(2,1)S(1)} collective-permute-done((bf16[128,1024]{1,0:T(8,128)(2,1)}, bf16[128,1024]{1,0:T(8,128)(2,1)S(1)}, u32[]{:S(2)}, u32[]{:S(2)}) %collective-permute-start.20) | collective-permute-done | bytes 262176 | tf_op jit(solution)/shard_map/key_grad/ppermute | solution.py:168
  173.9 5.5 %collective-permute-done.21 = bf16[128,1024]{1,0:T(8,128)(2,1)S(1)} collective-permute-done((bf16[128,1024]{1,0:T(8,128)(2,1)}, bf16[128,1024]{1,0:T(8,128)(2,1)S(1)}, u32[]{:S(2)}, u32[]{:S(2)}) %collective-permute-start.21) | collective-permute-done | bytes 262176 | tf_op jit(solution)/shard_map/key_grad/ppermute | solution.py:168
  179.4 6.9 %collective-permute-done.22 = bf16[128,1024]{1,0:T(8,128)(2,1)S(1)} collective-permute-done((bf16[128,1024]{1,0:T(8,128)(2,1)S(1)}, bf16[128,1024]{1,0:T(8,128)(2,1)S(1)}, u32[]{:S(2)}, u32[]{:S(2)}) %collective-permute-start.22) | collective-permute-done | bytes 262176 | tf_op jit(solution)/shard_map/key_grad/ppermute | solution.py:168
  187.2 1.2 bitcast_convert_fusion
  (78 shorter events, 11.8 us)
Async XLA Ops:
  3.1 4.3 %copy-start.3 = (bf16[320,1024]{1,0:T(8,128)(2,1)S(1)}, bf16[320,1024]{1,0:T(8,128)(2,1)}, u32[]{:S(2)}) copy-start(bf16[320,1024]{1,0:T(8,128)(2,1)} %param.7) | copy-start | bytes 1966084
  3.1 21.3 %all-to-all-start = ((bf16[128,4,1280]{0,2,1:T(8,128)(2,1)}), bf16[128,4,1280]{0,2,1:T(8,128)(2,1)S(1)}, u32[]{:S(2)}, u32[]{:S(2)}) async-start(bf16[128,4,1280]{0,2,1:T(8,128)(2,1)} %bitcast.2), calls=%async_computation | async-start | bytes 2621440 | tf_op jit(solution)/shard_map/hidden_columns/all_to_all | solution.py:210
  7.4 21.0 %collective-permute-start = (bf16[320,1024]{1,0:T(8,128)(2,1)S(1)}, bf16[320,1024]{1,0:T(8,128)(2,1)}, u32[]{:S(2)}, u32[]{:S(2)}) collective-permute-start(bf16[320,1024]{1,0:T(8,128)(2,1)S(1)} %copy-done.3), channel_id=1, source_target_pairs={{0,16},{16,0},{1,17},{17,1},{2,18},{18,2},{3,19},{19,3},{4,20},{20... | collective-permute-start | bytes 1966088 | tf_op jit(solution)/shard_map/weight_rows/ppermute | solution.py:172
  8.7 16.3 %collective-permute-start.1 = (bf16[128,1024]{1,0:T(8,128)(2,1)}, bf16[128,1024]{1,0:T(8,128)(2,1)S(1)}, u32[]{:S(2)}, u32[]{:S(2)}) collective-permute-start(bf16[128,1024]{1,0:T(8,128)(2,1)} %refs_7_.1), channel_id=1, source_target_pairs={{0,2},{1,3},{2,4},{3,5},{4,6},{5,7},{8,10},{9,11},{10,12},{11,13},... | collective-permute-start | bytes 786440 | tf_op jit(solution)/shard_map/keys/ppermute | solution.py:164
  11.8 16.1 %collective-permute-start.2 = (bf16[128,1024]{1,0:T(8,128)(2,1)}, bf16[128,1024]{1,0:T(8,128)(2,1)}, u32[]{:S(2)}, u32[]{:S(2)}) collective-permute-start(bf16[128,1024]{1,0:T(8,128)(2,1)} %refs_7_.1), channel_id=1, source_target_pairs={{0,1},{1,2},{2,3},{3,4},{4,5},{5,6},{6,7},{8,9},{9,10},{10,11},{11... | collective-permute-start | bytes 786440 | tf_op jit(solution)/shard_map/keys/ppermute | solution.py:164
  25.0 7.6 %copy-start.13 = (bf16[128,1024]{1,0:T(8,128)(2,1)}, bf16[128,1024]{1,0:T(8,128)(2,1)S(1)}, u32[]{:S(2)}) copy-start(bf16[128,1024]{1,0:T(8,128)(2,1)S(1)} %collective-permute-done.1.refs_4_.refs_5_) | copy-start | bytes 786436
  30.7 6.0 %collective-permute-start.4 = (bf16[2,320,1024]{2,1,0:T(8,128)(2,1)}, bf16[2,320,1024]{2,1,0:T(8,128)(2,1)}, u32[]{:S(2)}, u32[]{:S(2)}) collective-permute-start(bf16[2,320,1024]{2,1,0:T(8,128)(2,1)} %pad_maximum_fusion.1), channel_id=1, source_target_pairs={{0,8},{8,0},{1,9},{9,1},{2,10},{10,2},{3,11},{11,3},{4,12},{12,4},... | collective-permute-start | bytes 3932168 | tf_op jit(solution)/shard_map/weight_rows/ppermute | solution.py:172
  33.6 15.6 %collective-permute-start.3 = (bf16[2,128,1024]{2,1,0:T(8,128)(2,1)S(1)}, bf16[2,128,1024]{2,1,0:T(8,128)(2,1)}, u32[]{:S(2)}, u32[]{:S(2)}) collective-permute-start(bf16[2,128,1024]{2,1,0:T(8,128)(2,1)S(1)} %pad_maximum_fusion.3), channel_id=1, source_target_pairs={{0,2},{1,3},{2,4},{3,5},{4,6},{5,7},{8,10},{9,11},{10,12},{11,13},... | collective-permute-start | bytes 1572872 | tf_op jit(solution)/shard_map/keys/ppermute | solution.py:164
  38.5 2.5 %copy-start = (bf16[2,2,320,1024]{3,2,1,0:T(8,128)(2,1)}, bf16[2,2,320,1024]{3,2,1,0:T(8,128)(2,1)S(1)}, u32[]{:S(2)}) copy-start(bf16[2,2,320,1024]{3,2,1,0:T(8,128)(2,1)S(1)} %pad_maximum_fusion) | copy-start | bytes 7864324
  41.0 4.4 %copy-start.18 = (s32[1,8]{1,0:T(1,128)S(1)}, s32[1,8]{1,0:T(1,128)}, u32[]{:S(2)}) copy-start(s32[1,8]{1,0:T(1,128)} %param.11) | copy-start | bytes 100
  41.0 30.6 %all-to-all-start.1 = ((bf16[4,128,1024]{2,1,0:T(8,128)(2,1)}), bf16[4,128,1024]{2,1,0:T(8,128)(2,1)S(1)}, u32[]{:S(2)}, u32[]{:S(2)}) async-start(bf16[4,128,1024]{2,1,0:T(8,128)(2,1)} %bitcast.14), calls=%async_computation.1 | async-start | bytes 2097152 | tf_op jit(solution)/shard_map/values/all_to_all | solution.py:221
  64.3 27.5 %copy-start.5 = (f32[128,1024]{1,0:T(8,128)S(1)}, f32[128,1024]{1,0:T(8,128)}, u32[]{:S(2)}) copy-start(f32[128,1024]{1,0:T(8,128)} %get-tuple-element.76) | copy-start | bytes 1572868
  64.3 13.2 %collective-permute-start.5 = (bf16[128,1024]{1,0:T(8,128)(2,1)}, bf16[128,1024]{1,0:T(8,128)(2,1)S(1)}, u32[]{:S(2)}, u32[]{:S(2)}) collective-permute-start(bf16[128,1024]{1,0:T(8,128)(2,1)} %get-tuple-element.66), channel_id=1, source_target_pairs={{4,0},{5,1},{6,2},{7,3},{12,8},{13,9},{14,10},{15,11},{20,16},{21,... | collective-permute-start | bytes 786440 | tf_op jit(solution)/shard_map/value_grad/ppermute | solution.py:168
  65.8 16.2 %collective-permute-start.6 = (bf16[128,1024]{1,0:T(8,128)(2,1)}, bf16[128,1024]{1,0:T(8,128)(2,1)}, u32[]{:S(2)}, u32[]{:S(2)}) collective-permute-start(bf16[128,1024]{1,0:T(8,128)(2,1)} %get-tuple-element.67), channel_id=1, source_target_pairs={{3,0},{4,1},{5,2},{6,3},{7,4},{11,8},{12,9},{13,10},{14,11},{15,12... | collective-permute-start | bytes 786440 | tf_op jit(solution)/shard_map/value_grad/ppermute | solution.py:168
  67.7 19.9 %collective-permute-start.7 = (bf16[128,1024]{1,0:T(8,128)(2,1)}, bf16[128,1024]{1,0:T(8,128)(2,1)}, u32[]{:S(2)}, u32[]{:S(2)}) collective-permute-start(bf16[128,1024]{1,0:T(8,128)(2,1)} %get-tuple-element.68), channel_id=1, source_target_pairs={{2,0},{3,1},{4,2},{5,3},{6,4},{7,5},{10,8},{11,9},{12,10},{13,11},... | collective-permute-start | bytes 786440 | tf_op jit(solution)/shard_map/value_grad/ppermute | solution.py:168
  69.6 22.2 %collective-permute-start.8 = (bf16[128,1024]{1,0:T(8,128)(2,1)}, bf16[128,1024]{1,0:T(8,128)(2,1)}, u32[]{:S(2)}, u32[]{:S(2)}) collective-permute-start(bf16[128,1024]{1,0:T(8,128)(2,1)} %get-tuple-element.69), channel_id=1, source_target_pairs={{1,0},{2,1},{3,2},{4,3},{5,4},{6,5},{7,6},{9,8},{10,9},{11,10},{12... | collective-permute-start | bytes 786440 | tf_op jit(solution)/shard_map/value_grad/ppermute | solution.py:168
  71.8 21.6 %copy-start.12 = (bf16[128,1024]{1,0:T(8,128)(2,1)}, bf16[128,1024]{1,0:T(8,128)(2,1)S(1)}, u32[]{:S(2)}) copy-start(bf16[128,1024]{1,0:T(8,128)(2,1)S(1)} %reduce_sum.24.refs_11_) | copy-start | bytes 786436
  71.8 20.1 %collective-permute-start.10 = (bf16[128,1024]{1,0:T(8,128)(2,1)S(1)}, bf16[128,1024]{1,0:T(8,128)(2,1)S(1)}, u32[]{:S(2)}, u32[]{:S(2)}) collective-permute-start(bf16[128,1024]{1,0:T(8,128)(2,1)S(1)} %reduce_sum.24.refs_11_), channel_id=1, source_target_pairs={{0,1},{1,2},{2,3},{3,4},{4,5},{5,6},{6,7},{8,9},{9,10},{10,11},{11... | collective-permute-start | bytes 786440 | tf_op jit(solution)/shard_map/values_forward/ppermute | solution.py:164
  77.6 14.3 %collective-permute-start.9 = (bf16[128,1024]{1,0:T(8,128)(2,1)S(1)}, bf16[128,1024]{1,0:T(8,128)(2,1)S(1)}, u32[]{:S(2)}, u32[]{:S(2)}) collective-permute-start(bf16[128,1024]{1,0:T(8,128)(2,1)S(1)} %reduce_sum.24.refs_11_), channel_id=1, source_target_pairs={{0,2},{1,3},{2,4},{3,5},{4,6},{5,7},{8,10},{9,11},{10,12},{11,13},... | collective-permute-start | bytes 786440 | tf_op jit(solution)/shard_map/values_forward/ppermute | solution.py:164
  91.8 1.6 copy-start.14
  91.8 1.6 copy-start.15
  93.4 16.3 %collective-permute-start.14 = (bf16[2,128,1024]{2,1,0:T(8,128)(2,1)S(1)}, bf16[2,128,1024]{2,1,0:T(8,128)(2,1)S(1)}, u32[]{:S(2)}, u32[]{:S(2)}) collective-permute-start(bf16[2,128,1024]{2,1,0:T(8,128)(2,1)S(1)} %pad_maximum_fusion.4), channel_id=1, source_target_pairs={{0,2},{1,3},{2,4},{3,5},{4,6},{5,7},{8,10},{9,11},{10,12},{11,13},... | collective-permute-start | bytes 1572872 | tf_op jit(solution)/shard_map/values_forward/ppermute | solution.py:164
  95.8 7.1 %collective-permute-start.11 = (bf16[128,1024]{1,0:T(8,128)(2,1)S(1)}, bf16[128,1024]{1,0:T(8,128)(2,1)S(1)}, u32[]{:S(2)}, u32[]{:S(2)}) collective-permute-start(bf16[128,1024]{1,0:T(8,128)(2,1)S(1)} %add_convert_fusion.2), channel_id=1, source_target_pairs={{0,32},{32,64},{64,96},{96,0},{1,33},{33,65},{65,97},{97,1},{2,34}... | collective-permute-start | bytes 786440 | tf_op jit(solution)/shard_map/value_grad/ppermute | solution.py:176
  97.3 12.4 %collective-permute-start.12 = (bf16[128,1024]{1,0:T(8,128)(2,1)S(1)}, bf16[128,1024]{1,0:T(8,128)(2,1)S(1)}, u32[]{:S(2)}, u32[]{:S(2)}) collective-permute-start(bf16[128,1024]{1,0:T(8,128)(2,1)S(1)} %add_convert_fusion.2), channel_id=1, source_target_pairs={{0,64},{32,96},{64,0},{96,32},{1,65},{33,97},{65,1},{97,33},{2,66}... | collective-permute-start | bytes 786440 | tf_op jit(solution)/shard_map/value_grad/ppermute | solution.py:176
  99.7 10.0 %collective-permute-start.13 = (bf16[128,1024]{1,0:T(8,128)(2,1)S(1)}, bf16[128,1024]{1,0:T(8,128)(2,1)S(1)}, u32[]{:S(2)}, u32[]{:S(2)}) collective-permute-start(bf16[128,1024]{1,0:T(8,128)(2,1)S(1)} %add_convert_fusion.2), channel_id=1, source_target_pairs={{0,96},{32,0},{64,32},{96,64},{1,97},{33,1},{65,33},{97,65},{2,98}... | collective-permute-start | bytes 786440 | tf_op jit(solution)/shard_map/value_grad/ppermute | solution.py:176
  109.7 1.7 copy-start.16
  111.7 3.1 %copy-start.1 = (bf16[2,2,320,1024]{3,2,1,0:T(8,128)(2,1)S(1)}, bf16[2,2,320,1024]{3,2,1,0:T(8,128)(2,1)}, u32[]{:S(2)}) copy-start(bf16[2,2,320,1024]{3,2,1,0:T(8,128)(2,1)} %copy-done) | copy-start | bytes 7864324
  111.8 5.6 %collective-permute-start.15 = (bf16[640,1024]{1,0:T(8,128)(2,1)S(1)}, bf16[640,1024]{1,0:T(8,128)(2,1)S(1)}, u32[]{:S(2)}, u32[]{:S(2)}) collective-permute-start(bf16[640,1024]{1,0:T(8,128)(2,1)S(1)} %pad_maximum_fusion.2), channel_id=1, source_target_pairs={{0,8},{8,0},{1,9},{9,1},{2,10},{10,2},{3,11},{11,3},{4,12},{12,4},... | collective-permute-start | bytes 3932168 | tf_op jit(solution)/shard_map/weight_grad/ppermute | solution.py:172
  119.1 23.4 %all-to-all-start.2 = ((bf16[16,40,1024]{2,1,0:T(8,128)(2,1)}), bf16[16,40,1024]{2,1,0:T(8,128)(2,1)S(1)}, u32[]{:S(2)}, u32[]{:S(2)}) async-start(bf16[16,40,1024]{2,1,0:T(8,128)(2,1)} %bitcast.17), calls=%async_computation.2 | async-start | bytes 2621440 | tf_op jit(solution)/shard_map/weight_grad/all_to_all | solution.py:253
  125.8 17.0 %collective-permute-start.16 = (bf16[128,1280]{1,0:T(8,128)(2,1)}, bf16[128,1280]{1,0:T(8,128)(2,1)S(1)}, u32[]{:S(2)}, u32[]{:S(2)}) collective-permute-start(bf16[128,1280]{1,0:T(8,128)(2,1)} %get-tuple-element.117), channel_id=1, source_target_pairs={{0,96},{32,0},{64,32},{96,64},{1,97},{33,1},{65,33},{97,65},{2,98}... | collective-permute-start | bytes 983048 | tf_op jit(solution)/shard_map/input_grad/ppermute | solution.py:176
  127.7 15.1 %collective-permute-start.17 = (bf16[128,1280]{1,0:T(8,128)(2,1)}, bf16[128,1280]{1,0:T(8,128)(2,1)S(1)}, u32[]{:S(2)}, u32[]{:S(2)}) collective-permute-start(bf16[128,1280]{1,0:T(8,128)(2,1)} %get-tuple-element.116), channel_id=1, source_target_pairs={{0,64},{32,96},{64,0},{96,32},{1,65},{33,97},{65,1},{97,33},{2,66}... | collective-permute-start | bytes 983048 | tf_op jit(solution)/shard_map/input_grad/ppermute | solution.py:176
  128.5 17.5 %collective-permute-start.18 = (bf16[128,1280]{1,0:T(8,128)(2,1)S(1)}, bf16[128,1280]{1,0:T(8,128)(2,1)S(1)}, u32[]{:S(2)}, u32[]{:S(2)}) collective-permute-start(bf16[128,1280]{1,0:T(8,128)(2,1)S(1)} %get-tuple-element.115), channel_id=1, source_target_pairs={{0,32},{32,64},{64,96},{96,0},{1,33},{33,65},{65,97},{97,1},{2,34}... | collective-permute-start | bytes 983048 | tf_op jit(solution)/shard_map/input_grad/ppermute | solution.py:176
  142.7 16.1 %copy-start.17 = (bf16[128,1024]{1,0:T(8,128)(2,1)S(1)}, bf16[128,1024]{1,0:T(8,128)(2,1)}, u32[]{:S(2)}) copy-start(bf16[128,1024]{1,0:T(8,128)(2,1)} %get-tuple-element.102) | copy-start | bytes 786436
  142.8 16.0 %copy-start.6 = (bf16[128,1280]{1,0:T(8,128)(2,1)}, bf16[128,1280]{1,0:T(8,128)(2,1)S(1)}, u32[]{:S(2)}) copy-start(bf16[128,1280]{1,0:T(8,128)(2,1)S(1)} %collective-permute-done.16) | copy-start | bytes 983044
  142.8 16.0 %copy-start.8 = (bf16[128,1280]{1,0:T(8,128)(2,1)}, bf16[128,1280]{1,0:T(8,128)(2,1)S(1)}, u32[]{:S(2)}) copy-start(bf16[128,1280]{1,0:T(8,128)(2,1)S(1)} %collective-permute-done.17) | copy-start | bytes 983044
  146.0 14.7 %copy-start.10 = (bf16[128,1280]{1,0:T(8,128)(2,1)}, bf16[128,1280]{1,0:T(8,128)(2,1)S(1)}, u32[]{:S(2)}) copy-start(bf16[128,1280]{1,0:T(8,128)(2,1)S(1)} %collective-permute-done.18) | copy-start | bytes 983044
  147.0 40.2 %all-to-all-start.3 = ((bf16[8,40,1024]{2,1,0:T(8,128)(2,1)}), bf16[8,40,1024]{2,1,0:T(8,128)(2,1)S(1)}, u32[]{:S(2)}, u32[]{:S(2)}) async-start(bf16[8,40,1024]{2,1,0:T(8,128)(2,1)} %broadcast_in_dim.14), calls=%async_computation.3 | async-start | bytes 1310720 | tf_op jit(solution)/shard_map/weight_grad/all_to_all | solution.py:180
  153.6 14.7 %collective-permute-start.19 = (bf16[128,1024]{1,0:T(8,128)(2,1)}, bf16[128,1024]{1,0:T(8,128)(2,1)S(1)}, u32[]{:S(2)}, u32[]{:S(2)}) collective-permute-start(bf16[128,1024]{1,0:T(8,128)(2,1)} %get-tuple-element.99), channel_id=1, source_target_pairs={{4,0},{5,1},{6,2},{7,3},{12,8},{13,9},{14,10},{15,11},{20,16},{21,... | collective-permute-start | bytes 786440 | tf_op jit(solution)/shard_map/key_grad/ppermute | solution.py:168
  154.9 19.0 %collective-permute-start.20 = (bf16[128,1024]{1,0:T(8,128)(2,1)}, bf16[128,1024]{1,0:T(8,128)(2,1)S(1)}, u32[]{:S(2)}, u32[]{:S(2)}) collective-permute-start(bf16[128,1024]{1,0:T(8,128)(2,1)} %get-tuple-element.100), channel_id=1, source_target_pairs={{3,0},{4,1},{5,2},{6,3},{7,4},{11,8},{12,9},{13,10},{14,11},{15,12... | collective-permute-start | bytes 786440 | tf_op jit(solution)/shard_map/key_grad/ppermute | solution.py:168
  156.9 22.6 %collective-permute-start.21 = (bf16[128,1024]{1,0:T(8,128)(2,1)}, bf16[128,1024]{1,0:T(8,128)(2,1)S(1)}, u32[]{:S(2)}, u32[]{:S(2)}) collective-permute-start(bf16[128,1024]{1,0:T(8,128)(2,1)} %get-tuple-element.101), channel_id=1, source_target_pairs={{2,0},{3,1},{4,2},{5,3},{6,4},{7,5},{10,8},{11,9},{12,10},{13,11},... | collective-permute-start | bytes 786440 | tf_op jit(solution)/shard_map/key_grad/ppermute | solution.py:168
  158.8 27.5 %collective-permute-start.22 = (bf16[128,1024]{1,0:T(8,128)(2,1)S(1)}, bf16[128,1024]{1,0:T(8,128)(2,1)S(1)}, u32[]{:S(2)}, u32[]{:S(2)}) collective-permute-start(bf16[128,1024]{1,0:T(8,128)(2,1)S(1)} %copy-done.17), channel_id=1, source_target_pairs={{1,0},{2,1},{3,2},{4,3},{5,4},{6,5},{7,6},{9,8},{10,9},{11,10},{12... | collective-permute-start | bytes 786440 | tf_op jit(solution)/shard_map/key_grad/ppermute | solution.py:168
  160.8 1.0 copy-start.7
  160.8 1.1 copy-start.9
  160.9 1.1 copy-start.11
  160.9 25.4 %copy-start.4 = (f32[128,1024]{1,0:T(8,128)S(1)}, f32[128,1024]{1,0:T(8,128)}, u32[]{:S(2)}) copy-start(f32[128,1024]{1,0:T(8,128)} %get-tuple-element.103) | copy-start | bytes 1572868
  162.0 26.4 %copy-start.2 = (bf16[128,5120]{1,0:T(8,128)(2,1)}, bf16[128,5120]{1,0:T(8,128)(2,1)S(1)}, u32[]{:S(2)}) copy-start(bf16[128,5120]{1,0:T(8,128)(2,1)S(1)} %constant_dynamic-update-slice_fusion.4) | copy-start | bytes 3932164
